TPU v7x, 256 devices: a whole 4x4x8 slice. The times are simulated.
256 devices in a mesh: pts: 32 (over z, y_hi, core), lts: 8 (over y_lo, x).
Axes of the slice: x: 4, y: 4 (y_hi: 2, y_lo: 2; y = y_hi * 2 + y_lo), z: 8, core: 2. Of those that a mesh axis runs over, the one named last changes fastest.
Arguments:
- normals: float32 [3, 8192], P(None, 'pts'), may hold values from -1 to 1, as said below
- view_index: int32 [8192], P('pts'), may hold values from 0 to 63
- cam_dirs: float32 [3, 64], replicated, may hold values from -1 to 1, as said below
- albedo: float32 [3, 8192], P(None, 'pts'), may hold values from 0.05 to 0.95
- roughness: float32 [8192], P('pts'), may hold values from 0.3 to 0.9
- point_feat: float32 [32, 8192], P(None, 'pts'), may hold values from -6 to 6
- observed: float32 [3, 8192], P(None, 'pts'), may hold values from 0 to 1.5
- texel_feat: float32 [32, 32768], P(None, 'lts'), may hold values from -6 to 6
- env: float32 [3, 32768], P(None, 'lts'), may hold values from 0.1 to 10
Outputs:
- radiance: float32 [3, 8192], P(None, 'pts')
- grad_albedo: float32 [3, 8192], P(None, 'pts')
- grad_roughness: float32 [8192], P('pts')
- grad_point_feat: float32 [32, 8192], P(None, 'pts')
- light_step: float32 [3, 32768], P(None, 'lts')
- feat_step: float32 [32, 32768], P(None, 'lts')
Inputs may be any that keep to these rules, and one draw needn't show every extreme that they name: `normals`: each column is a unit vector. `cam_dirs`: each column is a unit vector.
All inputs are finite; a program needn't handle non-finite values.
Results may differ from a plain program's by a relative error of at most 0.0003.
Values sent between devices are 32-bit elements; how exact they have to be, the bound alone decides.
No kernel may reach another device: no remote copies, remote signals or barrier semaphores. Data moves between devices by JAX's collectives and lax.ppermute only.
A program may use at most 64 MiB of HBM per device.

v0:
```python
import math

import jax
import jax.numpy as jnp
from jax import lax
from jax.sharding import PartitionSpec as P

ROWS = 128
COLS = 256


PRECISE = lax.Precision.HIGHEST


def texel_geometry(start, count):
    texel_pos = start + jnp.arange(count, dtype=jnp.int32)
    row_pos = (texel_pos // COLS).astype(jnp.float32)
    col_pos = (texel_pos % COLS).astype(jnp.float32)
    theta = math.pi * (row_pos + 0.5) / ROWS
    azimuth = 2.0 * math.pi * (col_pos + 0.5) / COLS
    sine = jnp.sin(theta)
    directions = jnp.stack([sine * jnp.cos(azimuth), sine * jnp.sin(azimuth), jnp.cos(theta)])
    weights = sine * (0.5 * math.pi)
    return (directions, weights)


def visibility_score(point_block, texel_block):
    return jnp.einsum("fp,fl->pl", point_block, texel_block, precision=PRECISE) / math.sqrt(
        point_block.shape[0]
    )


def lobe_kernel(albedo, rough, score, lights, normals, views, directions, weights):
    cos_light = jnp.einsum("kp,kl->pl", normals, directions, precision=PRECISE)
    cos_view = jnp.einsum("kp,kl->pl", views, directions, precision=PRECISE)
    normal_view = jnp.sum(normals * views, axis=0)
    view_floor = jnp.maximum(normal_view, 0.1)
    lit = jnp.maximum(cos_light, 0.0)
    half_len = jnp.sqrt(jnp.maximum(2.0 + 2.0 * cos_view, 0.5))
    normal_half = (cos_light + normal_view[:, None]) / half_len
    view_half = (1.0 + cos_view) / half_len
    alpha = rough * rough
    alpha_sq = (alpha * alpha)[:, None]
    denom = normal_half * normal_half * (alpha_sq - 1.0) + 1.0
    distrib = alpha_sq / (math.pi * denom * denom)
    half_rough = (alpha * 0.5)[:, None]
    fresnel = 0.04 + 0.96 * (1.0 - view_half) ** 5
    shadow = (lit * (1.0 - half_rough) + half_rough) * (
        view_floor[:, None] * (1.0 - half_rough) + half_rough
    )
    specular = distrib * fresnel / (4.0 * shadow)
    base = jax.nn.sigmoid(score) * lit * weights[None, :]
    contrib = (albedo[:, :, None] / math.pi + specular[None]) * base[None] * lights[:, None, :]
    shaded = 4.0 * math.pi / (ROWS * COLS) * jnp.sum(contrib, axis=2)
    energy = jnp.sum(contrib * contrib, axis=1)
    return (shaded, energy)


def texel_update(gain, energy, grad_texel, points_all, scale):
    light_step = gain / jnp.sqrt(energy + 1e-06 * points_all)
    total_energy = jnp.sum(energy, axis=0, keepdims=True)
    feat_step = grad_texel * scale / jnp.sqrt(total_energy + 3e-06 * points_all)
    return (light_step, feat_step)


def shards(normals, view_index, cam_dirs, albedo, roughness, point_feat, observed, texel_feat, env):
    pts_local = normals.shape[1]
    tex_local = env.shape[1]
    cameras = cam_dirs.shape[1]
    feat_width = point_feat.shape[0]
    choose = (jnp.arange(cameras, dtype=jnp.int32)[:, None] == view_index[None, :]).astype(
        jnp.float32
    )
    views = jnp.dot(cam_dirs, choose, precision=PRECISE, preferred_element_type=jnp.float32)
    start = lax.axis_index("lts") * tex_local
    directions, weights = texel_geometry(start, tex_local)
    block = min(1024, tex_local)
    nblocks = tex_local // block

    def texel_blocks(array):
        return array.reshape(array.shape[0], nblocks, block).transpose(1, 0, 2)

    def texel_join(array):
        return array.transpose(1, 0, 2).reshape(array.shape[1], tex_local)

    pieces = (
        texel_blocks(directions),
        weights.reshape(nblocks, block),
        texel_blocks(texel_feat),
        texel_blocks(env),
    )

    def forward(total, parts):
        dirs_blk, wts_blk, feat_blk, env_blk = parts
        score = visibility_score(point_feat, feat_blk)
        shaded, energy = lobe_kernel(
            albedo, roughness, score, env_blk, normals, views, dirs_blk, wts_blk
        )
        return (total + shaded, None)

    partial_rad, unused = lax.scan(forward, jnp.zeros((3, pts_local), jnp.float32), pieces)
    radiance = lax.psum(partial_rad, "lts")
    resid = radiance - observed

    def backward(carry, parts):
        grad_alb, grad_rgh, grad_feat = carry
        dirs_blk, wts_blk, feat_blk, env_blk = parts
        score = visibility_score(point_feat, feat_blk)

        def local(alb_in, rgh_in, score_in, env_in):
            return lobe_kernel(alb_in, rgh_in, score_in, env_in, normals, views, dirs_blk, wts_blk)

        shaded_now, pull, energy = jax.vjp(local, albedo, roughness, score, env_blk, has_aux=True)
        dalb, drgh, dscore, dlight = pull(resid)
        dfeat = jnp.einsum("fl,pl->fp", feat_blk, dscore, precision=PRECISE) / math.sqrt(feat_width)
        dtex = jnp.einsum("fp,pl->fl", point_feat, dscore, precision=PRECISE) / math.sqrt(
            feat_width
        )
        return ((grad_alb + dalb, grad_rgh + drgh, grad_feat + dfeat), (dlight, dtex, energy))

    init = (
        jnp.zeros((3, pts_local), jnp.float32),
        jnp.zeros((pts_local,), jnp.float32),
        jnp.zeros((feat_width, pts_local), jnp.float32),
    )
    (grad_alb, grad_rgh, grad_feat), (light_parts, tex_parts, energy_parts) = lax.scan(
        backward, init, pieces
    )
    grad_albedo, grad_roughness, grad_point_feat = lax.psum((grad_alb, grad_rgh, grad_feat), "lts")
    scale = tex_local * lax.axis_size("lts") / (4.0 * math.pi)
    points_all = lax.axis_size("pts") * pts_local
    gain = env * texel_join(light_parts) * scale
    energy = texel_join(energy_parts)
    grad_texel = texel_join(tex_parts)
    gain_all, energy_all, texel_all = lax.psum((gain, energy, grad_texel), "pts")
    light_step, feat_step = texel_update(gain_all, energy_all, texel_all, points_all, scale)
    return (radiance, grad_albedo, grad_roughness, grad_point_feat, light_step, feat_step)


def solution(mesh):
    return jax.shard_map(
        shards,
        mesh=mesh,
        in_specs=(
            P(None, "pts"),
            P("pts"),
            P(),
            P(None, "pts"),
            P("pts"),
            P(None, "pts"),
            P(None, "pts"),
            P(None, "lts"),
            P(None, "lts"),
        ),
        out_specs=(
            P(None, "pts"),
            P(None, "pts"),
            P("pts"),
            P(None, "pts"),
            P(None, "lts"),
            P(None, "lts"),
        ),
        check_vma=False,
    )
```

profile of v0, /device:TPU:1, one launch (start us, length us, event | category | flops | bytes accessed | tf_op | source)
XLA Modules:
  0.0 708.0 jit_solution(1342174445527583117)
XLA Ops:
  11.4 27.1 %while.40 = (s32[]{:T(128)}, f32[3,256]{1,0:T(4,128)S(1)}, f32[3,256]{1,0:T(4,128)S(1)}, f32[256,1]{0,1:T(1,128)S(1)}, f32[4,3,1024]{2,1,0:T(4,128)S(1)}, /*inde...) while((s32[]{:T(128)}, f32[3,256]{1,0:T(4,128)S(1)}, ...), condition=%wide.region_3.4_spmd.clone, body=%wide.region_1.3_spmd.clone.sunk | while | flops 131337984 | bytes 11824807 | solution.py:101
  38.5 17.0 %psum.49 = f32[3,256]{1,0:T(4,128)S(1)} all-reduce(f32[3,256]{1,0:T(4,128)S(1)} %get-tuple-element.494), channel_id=1, replica_groups=mesh['pts'=32,'lts'=8] {'lts'}, use_global_device_ids=true, to_apply=%region_4.5 | all-reduce | flops 768 | bytes 6144 | tf_op jit(solution)/shard_map/psum | solution.py:102
  56.1 122.6 %while.41 = (s32[]{:T(128)}, f32[3,256]{1,0:T(4,128)S(1)}, f32[256]{0:T(256)S(1)}, f32[32,256]{1,0:T(8,128)S(1)}, f32[4,3,1024]{2,1,0:T(4,128)S(1)}, /*index=5*/...) while((s32[]{:T(128)}, f32[3,256]{1,0:T(4,128)S(1)}, ...), condition=%wide.wide.region_16.17_spmd.clone.clone, body=%wide.wide.region_5.16_spmd.clone.clone.sunk | while | flops 357360896 | bytes 43776288 | solution.py:126
  58.2 4.7 fusion.145
  67.1 4.5 fusion.146
  71.6 2.6 copy.72
  75.6 4.4 divide_multiply_fusion.4
  84.0 2.7 multiply_reduce_fusion.7
  88.9 4.7 fusion.145
  97.7 4.5 fusion.146
  102.3 2.6 copy.72
  106.3 4.4 divide_multiply_fusion.4
  114.6 2.7 multiply_reduce_fusion.7
  119.5 4.7 fusion.145
  128.4 4.5 fusion.146
  136.9 4.4 divide_multiply_fusion.4
  145.3 2.7 multiply_reduce_fusion.7
  150.2 4.7 fusion.145
  159.0 4.5 fusion.146
  167.6 4.4 divide_multiply_fusion.4
  175.9 2.7 multiply_reduce_fusion.7
  181.3 24.8 %all-reduce.1 = (f32[3,256]{1,0:T(4,128)}, f32[256]{0:T(256)}, f32[32,256]{1,0:T(8,128)}) all-reduce(f32[3,256]{1,0:T(4,128)S(1)} %get-tuple-element.495, f32[256]{0:T(256)S(1)} %get-tuple-element.496, f32[32,256]{1,0:T(8,128)S(1)} %get-tuple-element.497), channel_id=1, replica_groups=mesh['pts'=32,'lts'=8] {'lts'}, use_global_device_ids=true, to_apply=%region_17.18 | all-reduce | flops 9216 | bytes 73728 | tf_op jit(solution)/shard_map/psum | solution.py:129
  206.1 222.2 %all-reduce.7.cloned.1.call-done = (f32[3,4096]{1,0:T(4,128)}, f32[3,4096]{1,0:T(4,128)}) async-done(((f32[3,4096]{1,0:T(4,128)}, f32[3,4096]{1,0:T(4,128)}), (f32[3,4096]{1,0:T(4,128)}, f32[3,4096]{1,0:T(4,128)})) %all-reduce.7.cloned.1.call-update) | async-done | bytes 98320 | tf_op jit(solution)/shard_map/psum | solution.py:135
  429.9 269.4 %all-reduce.5.cloned.1.call-done = f32[32,4096]{1,0:T(8,128)} async-done(((f32[32,4096]{1,0:T(8,128)}), f32[32,4096]{1,0:T(8,128)}) %all-reduce.5.cloned.1.call-update) | async-done | bytes 524304 | tf_op jit(solution)/shard_map/psum | solution.py:135
  (176 shorter events, 88.9 us)
Async XLA Ops:
  7.2 4.1 copy-start
  7.2 421.2 %all-reduce.7.cloned.1.call-start = ((), (), s32[]{:S(2)}) async-start(), calls=%async_computation.1 | async-start | bytes 262144 | tf_op jit(solution)/shard_map/psum | solution.py:135
  8.6 2.6 copy-start.5
  8.6 2.6 copy-start.9
  8.6 2.8 copy-start.3
  8.6 2.8 copy-start.4
  8.6 2.8 copy-start.6
  11.4 44.0 %copy-start.8 = (f32[3,256]{1,0:T(4,128)S(1)}, f32[3,256]{1,0:T(4,128)}, u32[]{:S(2)}) copy-start(f32[3,256]{1,0:T(4,128)} %param.19) | copy-start | bytes 9220
  55.5 0.6 copy-start.7
  71.6 2.6 copy-start.1
  82.4 1.6 copy-start.2
  102.3 2.6 copy-start.1
  113.0 1.6 copy-start.2
  132.9 2.6 copy-start.1
  143.7 1.6 copy-start.2
  163.6 2.6 copy-start.1
  174.3 1.6 copy-start.2
  179.3 519.9 %all-reduce.5.cloned.1.call-start = ((), (), s32[]{:S(2)}) async-start(), calls=%async_computation | async-start | bytes 1048576 | tf_op jit(solution)/shard_map/psum | solution.py:135
Sparse Core Ops, SparseCore 0:
  179.5 248.8 all-reduce.6
  431.7 267.5 all-reduce.4
where the time goes:
time: 709 us; the launch traced here: 708 us
  waiting for transfers between devices  492 us (69%)
  matrix products  61.8 us (9%)
  other arithmetic  54.9 us (8%)
  local copies, waits for them, and re-layouts  42.8 us (6%)
  blocking collectives  41.8 us (6%)
  between operations  14.2 us (2%)
    psum x2, waiting for transfers between devices, shards(): lax.psum((gain, energy, grad_texel), 'pts')  492 us
    dot_general x8, matrix products, visibility_score(): jnp.einsum('fp,fl->pl', point_block, texel_block, precision=PRECISE)  27.4 us
    psum x1, blocking collectives, shards(): lax.psum((grad_alb, grad_rgh, grad_feat), 'lts')  24.8 us
    reduce_sum x4, other arithmetic, lobe_kernel(): energy = jnp.sum(contrib * contrib, axis=1)  18.2 us
    mul x4, other arithmetic, lobe_kernel(): specular = distrib * fresnel / (4.0 * shadow)  17.7 us
    psum x1, blocking collectives, shards(): radiance = lax.psum(partial_rad, 'lts')  17 us
  transfers between devices with their start and end apart: 2, of which 2 were waited for; matrix products, arithmetic and copies ran while one was open for 0% of the time, Pallas kernels for 0%

commit v1 on v0

v1 whole, which is shorter than its diff:
```python
import functools
import math

import jax
import jax.numpy as jnp
import numpy as np
from jax import lax
from jax.experimental import pallas as pl
from jax.experimental.pallas import tpu as pltpu
from jax.sharding import PartitionSpec as P

ROWS = 128
COLS = 256
F32 = jnp.float32
BF16 = jnp.bfloat16

THETA = np.pi * (np.arange(ROWS) + 0.5) / ROWS
PHI = 2.0 * np.pi * (np.arange(COLS) + 0.5) / COLS
THETA_TABLE = np.stack([np.sin(THETA), np.cos(THETA)]).astype(np.float32)
PHI_TABLE = np.stack([np.cos(PHI), np.sin(PHI)]).astype(np.float32)

PTS = 256
BLK = 256
CHUNK = 16
(NZ, VZ, NV0, AM1, KEEP, KOFF, C1, C0, YA, YD, YG) = range(11)
NCONST = 11

TN = (((0,), (0,)), ((), ()))
NT = (((1,), (1,)), ((), ()))
NN = (((1,), (0,)), ((), ()))


def dot(a, b, dims):
    return lax.dot_general(a, b, dims, preferred_element_type=F32)


def split(x):
    hi = x.astype(BF16)
    return hi, (x - hi.astype(F32)).astype(BF16)


def shade_kernel(
    theta_ref,
    phi_ref,
    normals_ref,
    view_ref,
    cams_ref,
    albedo_ref,
    rough_ref,
    pfeat_ref,
    tfeat_ref,
    env_ref,
    bh_ref,
    bl_ref,
    sh_ref,
    sl_ref,
    qbh_ref,
    qbl_ref,
    qsh_ref,
    qsl_ref,
    sums_ref,
    fb_ref,
    fs_ref,
    energy_ref,
    const,
    azim_n,
    azim_v,
    pfs,
    score,
    yh,
    yl,
    squares,
    amat,
    ebuf,
    acc_s,
    acc_fb,
    acc_fs,
):
    step = pl.program_id(0)
    row = lax.axis_index("lts") * pl.num_programs(0) + step
    sin_t = theta_ref[0, row]
    cos_t = theta_ref[1, row]

    @pl.when(step == 0)
    def prologue():
        normals = normals_ref[...]
        cams = lax.broadcasted_iota(jnp.int32, (cams_ref.shape[1], PTS), 0)
        choose = (cams == view_ref[...]).astype(F32)
        views = lax.dot_general(
            cams_ref[...], choose, NN, precision=lax.Precision.HIGHEST, preferred_element_type=F32
        )
        rough = rough_ref[...]
        alpha = rough * rough
        alpha_sq = alpha * alpha
        half = 0.5 * alpha
        nv0 = jnp.sum(normals * views, axis=0, keepdims=True)
        nv = jnp.maximum(nv0, 0.1)
        geo_v = nv * (1.0 - half) + half
        lead = alpha_sq / (4.0 * math.pi * geo_v)
        y_d = -4.0 * alpha / (1.0 - alpha_sq)
        y_g = -0.5 / (1.0 - half)
        y_a = 2.0 / alpha - y_d - y_g - (1.0 - nv) / (2.0 * geo_v)
        two_r = 2.0 * rough
        rows = [None] * NCONST
        rows[NZ] = normals[2:3]
        rows[VZ] = 0.5 * views[2:3]
        rows[NV0] = nv0
        rows[AM1] = 0.25 * (alpha_sq - 1.0)
        rows[KEEP] = 1.0 - half
        rows[KOFF] = half
        rows[C1] = 0.96 * lead
        rows[C0] = 0.04 * lead
        rows[YA] = two_r * y_a
        rows[YD] = two_r * y_d
        rows[YG] = two_r * y_g
        rows += [normals[0:1], normals[1:2], 0.5 * views[0:1], 0.5 * views[1:2]]
        for k, r in enumerate(rows):
            ebuf[k : k + 1, :] = r
        cols = ebuf[...].T
        for k in range(NCONST):
            const[k] = jnp.broadcast_to(cols[:, k : k + 1], (PTS, 128))
        cos_p = phi_ref[0:1, :]
        sin_p = phi_ref[1:2, :]
        k = NCONST
        azim_n[...] = cols[:, k : k + 1] * cos_p + cols[:, k + 1 : k + 2] * sin_p
        azim_v[...] = cols[:, k + 2 : k + 3] * cos_p + cols[:, k + 3 : k + 4] * sin_p
        hi, lo = split((pfeat_ref[...] * (0.5 / math.sqrt(pfeat_ref.shape[0]))).T)
        pfs[:, 0:32] = hi
        pfs[:, 32:64] = lo
        pfs[:, 64:96] = hi
        ebuf[...] = jnp.zeros_like(ebuf)
        alb = albedo_ref[...] * (1.0 / math.pi)
        for j, a in enumerate((alb * alb, 2.0 * alb)):
            hi = a.astype(BF16).astype(F32)
            ebuf[0:3, :] = hi
            ebuf[3:6, :] = a - hi
            amat[:, j * PTS : (j + 1) * PTS] = ebuf[0:16, :].astype(BF16)
        ebuf[0:3, :] = jnp.ones((3, PTS), F32)
        ebuf[3:6, :] = jnp.zeros((3, PTS), F32)
        amat[:, 2 * PTS : 3 * PTS] = ebuf[0:16, :].astype(BF16)
        acc_s[...] = jnp.zeros_like(acc_s)
        acc_fb[...] = jnp.zeros_like(acc_fb)
        acc_fs[...] = jnp.zeros_like(acc_fs)

    tfeat = tfeat_ref[...]
    t_hi, t_lo = split(tfeat)
    score[...] = dot(pfs[...], jnp.concatenate([t_hi, t_hi, t_lo], axis=0), NN)

    def chunk(i, carry):
        r0 = pl.multiple_of(i * CHUNK, CHUNK)
        rows = pl.ds(r0, CHUNK)
        c = [const[k, rows, :] for k in range(NCONST)]
        nz = c[NZ] * cos_t
        vz = c[VZ] * cos_t + 0.5
        for h in range(BLK // 128):
            lanes = pl.ds(h * 128, 128)
            nl = azim_n[rows, lanes] * sin_t + nz
            vv = azim_v[rows, lanes] * sin_t + vz
            tt = jnp.tanh(score[rows, lanes])
            lit = jnp.maximum(nl, 0.0)
            inv_len = lax.rsqrt(jnp.maximum(vv, 0.125))
            nh = (nl + c[NV0]) * inv_len
            dd = nh * nh * c[AM1] + 1.0
            gg = lit * c[KEEP] + c[KOFF]
            dg = dd * gg
            inv = pl.reciprocal(dd * dg, approx=True)
            x1 = 1.0 - vv * inv_len
            x2 = x1 * x1
            fres = x2 * x2 * x1 * c[C1] + c[C0]
            base = (1.0 + tt) * lit
            spec = fres * inv * base
            fact = inv * dd * (c[YD] * gg + c[YG] * dd) + c[YA]
            yy = spec * fact
            rest = 1.0 - tt
            qb = base * rest
            qs = spec * rest
            for x, hi_ref, lo_ref in (
                (base, bh_ref, bl_ref),
                (spec, sh_ref, sl_ref),
                (qb, qbh_ref, qbl_ref),
                (qs, qsh_ref, qsl_ref),
                (yy, yh, yl),
            ):
                hi, lo = split(x)
                hi_ref[rows, lanes] = hi
                lo_ref[rows, lanes] = lo
            squares[pl.ds(r0, CHUNK), lanes] = (base * base).astype(BF16)
            squares[pl.ds(PTS + r0, CHUNK), lanes] = (base * spec).astype(BF16)
            squares[pl.ds(2 * PTS + r0, CHUNK), lanes] = (spec * spec).astype(BF16)
        return carry

    lax.fori_loop(0, PTS // CHUNK, chunk, 0)

    light = env_ref[...] * (sin_t * (0.25 * math.pi))
    l_hi = light.astype(BF16).astype(F32)
    ebuf[0:3, :] = l_hi
    ebuf[3:6, :] = light - l_hi
    lmat = ebuf[0:16, :].astype(BF16)
    for k, (hi_ref, lo_ref) in enumerate(((bh_ref, bl_ref), (sh_ref, sl_ref), (yh, yl))):
        acc_s[k] += dot(lmat, hi_ref[...], NT) + dot(lmat, lo_ref[...], NT)
    parts = [split(tfeat * light[k : k + 1]) for k in range(3)]
    f_hi = jnp.concatenate([p[0] for p in parts], axis=0)
    f_all = jnp.concatenate([p[0] for p in parts] + [p[1] for p in parts], axis=0)
    for acc, hi_ref, lo_ref in ((acc_fb, qbh_ref, qbl_ref), (acc_fs, qsh_ref, qsl_ref)):
        acc[...] += dot(f_all, hi_ref[...], NT)
        acc[0:96, :] += dot(f_hi, lo_ref[...], NT)
    eng = dot(amat[...], squares[...], NN)
    energy_ref[...] = light * light * (eng[0:3] + eng[3:6])

    @pl.when(step == pl.num_programs(0) - 1)
    def epilogue():
        for k in range(3):
            sums_ref[3 * k : 3 * k + 3, :] = acc_s[k, 0:3, :] + acc_s[k, 3:6, :]
        fb_ref[...] = acc_fb[0:96, :] + acc_fb[96:192, :]
        fs_ref[...] = acc_fs[0:96, :] + acc_fs[96:192, :]


def grad_kernel(
    scale,
    sums_ref,
    albedo_ref,
    observed_ref,
    pfeat_ref,
    fb_ref,
    fs_ref,
    energy_ref,
    theta_ref,
    env_ref,
    bh_ref,
    bl_ref,
    sh_ref,
    sl_ref,
    qbh_ref,
    qbl_ref,
    qsh_ref,
    qsl_ref,
    point_ref,
    gpf_ref,
    out_ref,
    rbuf,
    rb,
    rs,
    wb,
    ws,
):
    step = pl.program_id(0)
    row = lax.axis_index("lts") * pl.num_programs(0) + step
    sin_t = theta_ref[0, row]
    half_root = 0.5 / math.sqrt(pfeat_ref.shape[0])

    @pl.when(step == 0)
    def prologue():
        sums = sums_ref[...]
        alb = albedo_ref[...] * (1.0 / math.pi)
        radiance = scale * (alb * sums[0:3] + sums[3:6])
        resid = radiance - observed_ref[...]
        resid_a = resid * alb
        point_ref[0:3, :] = radiance
        point_ref[3:6, :] = (scale / math.pi) * resid * sums[0:3]
        point_ref[6:7, :] = scale * jnp.sum(resid * sums[6:9], axis=0, keepdims=True)
        pf = pfeat_ref[...] * half_root
        total = jnp.zeros_like(gpf_ref)
        for k in range(3):
            a = resid_a[k : k + 1]
            r = resid[k : k + 1]
            f = pl.ds(32 * k, 32)
            total += a * fb_ref[f, :] + r * fs_ref[f, :]
            for w_ref, x in ((wb, a), (ws, r)):
                hi, lo = split(pf * x)
                w_ref[pl.ds(32 * k, 32), :] = hi
                w_ref[pl.ds(96 + 32 * k, 32), :] = lo
        gpf_ref[...] = (scale * half_root) * total
        rbuf[...] = jnp.zeros_like(rbuf)
        for w_ref, x in ((rb, resid_a), (rs, resid)):
            hi = x.astype(BF16).astype(F32)
            rbuf[0:3, :] = hi
            rbuf[3:6, :] = x - hi
            w_ref[...] = rbuf[...].astype(BF16)

    light = env_ref[...] * (sin_t * (0.25 * math.pi))
    g = (
        dot(rb[...], bh_ref[...], NN)
        + dot(rb[...], bl_ref[...], NN)
        + dot(rs[...], sh_ref[...], NN)
        + dot(rs[...], sl_ref[...], NN)
    )
    x = dot(wb[...], qbh_ref[...], NN) + dot(ws[...], qsh_ref[...], NN)
    x = x[0:96] + x[96:192]
    x += dot(wb[0:96, :], qbl_ref[...], NN) + dot(ws[0:96, :], qsl_ref[...], NN)
    total = light[0:1] * x[0:32]
    for k in (1, 2):
        total += light[k : k + 1] * x[32 * k : 32 * k + 32]
    out_ref[0:32, :] = total
    out_ref[32:35, :] = light * (g[0:3] + g[3:6])
    out_ref[35:38, :] = energy_ref[...]
    out_ref[38:40, :] = jnp.zeros((2, BLK), F32)


def shards(normals, view_index, cam_dirs, albedo, roughness, point_feat, observed, texel_feat, env):
    pts = normals.shape[1]
    tex = env.shape[1]
    steps = tex // BLK
    points_all = lax.axis_size("pts") * pts
    tex_all = tex * lax.axis_size("lts")
    scale = 4.0 * math.pi / tex_all
    theta = jnp.asarray(THETA_TABLE)
    phi = jnp.asarray(PHI_TABLE)

    def whole(shape):
        return pl.BlockSpec(shape, lambda i: (0,) * len(shape))

    def tile(rows):
        return pl.BlockSpec((rows, BLK), lambda i: (0, i))

    smem = pl.BlockSpec(memory_space=pltpu.SMEM)
    big = jax.ShapeDtypeStruct((pts, tex), BF16)
    outs = pl.pallas_call(
        shade_kernel,
        grid=(steps,),
        in_specs=[
            smem,
            whole((2, COLS)),
            whole((3, pts)),
            whole((1, pts)),
            whole(cam_dirs.shape),
            whole((3, pts)),
            whole((1, pts)),
            whole((32, pts)),
            tile(32),
            tile(3),
        ],
        out_specs=[tile(pts)] * 8 + [whole((9, pts)), whole((96, pts)), whole((96, pts)), tile(3)],
        out_shape=[big] * 8
        + [
            jax.ShapeDtypeStruct((9, pts), F32),
            jax.ShapeDtypeStruct((96, pts), F32),
            jax.ShapeDtypeStruct((96, pts), F32),
            jax.ShapeDtypeStruct((3, tex), F32),
        ],
        scratch_shapes=[
            pltpu.VMEM((NCONST, PTS, 128), F32),
            pltpu.VMEM((PTS, COLS), F32),
            pltpu.VMEM((PTS, COLS), F32),
            pltpu.VMEM((PTS, 96), BF16),
            pltpu.VMEM((PTS, BLK), F32),
            pltpu.VMEM((PTS, BLK), BF16),
            pltpu.VMEM((PTS, BLK), BF16),
            pltpu.VMEM((3 * PTS, BLK), BF16),
            pltpu.VMEM((16, 3 * PTS), BF16),
            pltpu.VMEM((16, BLK), F32),
            pltpu.VMEM((3, 16, PTS), F32),
            pltpu.VMEM((192, PTS), F32),
            pltpu.VMEM((192, PTS), F32),
        ],
        compiler_params=pltpu.CompilerParams(vmem_limit_bytes=24 * 1024 * 1024),
        name="shade",
    )(
        theta,
        phi,
        normals,
        view_index.reshape(1, pts),
        cam_dirs,
        albedo,
        roughness.reshape(1, pts),
        point_feat,
        texel_feat,
        env,
    )
    mats, (sums, fb, fs, energy) = outs[:8], outs[8:]

    def swap(x, axis, bits):
        n = lax.axis_size(axis)
        return lax.ppermute(x, axis, [(i, i ^ bits) for i in range(n)])

    sums = sums + swap(sums, "lts", 4)
    sums = sums + swap(sums, "lts", 1) + swap(sums, "lts", 2) + swap(sums, "lts", 3)

    point_out, gpf, out = pl.pallas_call(
        functools.partial(grad_kernel, scale),
        grid=(steps,),
        in_specs=[
            whole((9, pts)),
            whole((3, pts)),
            whole((3, pts)),
            whole((32, pts)),
            whole((96, pts)),
            whole((96, pts)),
            tile(3),
            smem,
            tile(3),
        ]
        + [tile(pts)] * 8,
        out_specs=[whole((8, pts)), whole((32, pts)), tile(40)],
        out_shape=[
            jax.ShapeDtypeStruct((8, pts), F32),
            jax.ShapeDtypeStruct((32, pts), F32),
            jax.ShapeDtypeStruct((40, tex), F32),
        ],
        scratch_shapes=[
            pltpu.VMEM((16, PTS), F32),
            pltpu.VMEM((16, PTS), BF16),
            pltpu.VMEM((16, PTS), BF16),
            pltpu.VMEM((192, PTS), BF16),
            pltpu.VMEM((192, PTS), BF16),
        ],
        compiler_params=pltpu.CompilerParams(vmem_limit_bytes=24 * 1024 * 1024),
        name="grads",
    )(sums, albedo, observed, point_feat, fb, fs, energy, theta, env, *mats)

    gpf = gpf + swap(gpf, "lts", 4)
    gpf = gpf + swap(gpf, "lts", 1) + swap(gpf, "lts", 2) + swap(gpf, "lts", 3)

    place = lax.axis_index("pts")

    def halve(x, bit):
        n = x.shape[1] // 2
        lo, hi = x[:, :n], x[:, n:]
        low = (place & bit) == 0
        return jnp.where(low, lo, hi) + swap(jnp.where(low, hi, lo), "pts", bit)

    def double(x, bit):
        other = swap(x, "pts", bit)
        low = (place & bit) == 0
        return jnp.concatenate([jnp.where(low, x, other), jnp.where(low, other, x)], axis=1)

    x = out
    for bit in (1, 4, 8):
        x = halve(x, bit)
    for bit in (16, 2):
        x = x + swap(x, "pts", bit)
    light_step = x[32:35] * lax.rsqrt(x[35:38] + 1e-06 * points_all)
    total = jnp.sum(x[35:38], axis=0, keepdims=True)
    feat_step = x[0:32] * lax.rsqrt(total + 3e-06 * points_all)
    x = jnp.concatenate([feat_step, light_step], axis=0)
    for bit in (8, 4, 1):
        x = double(x, bit)
    return (point_out[0:3], point_out[3:6], point_out[6], gpf, x[32:35], x[0:32])


def solution(mesh):
    return jax.shard_map(
        shards,
        mesh=mesh,
        in_specs=(
            P(None, "pts"),
            P("pts"),
            P(),
            P(None, "pts"),
            P("pts"),
            P(None, "pts"),
            P(None, "pts"),
            P(None, "lts"),
            P(None, "lts"),
        ),
        out_specs=(
            P(None, "pts"),
            P(None, "pts"),
            P("pts"),
            P(None, "pts"),
            P(None, "lts"),
            P(None, "lts"),
        ),
        check_vma=False,
    )
```

time: 709 us -> 136 us (0.19)
  waiting for transfers between devices: 492 us -> 21 us
  matrix products: 61.8 us -> 0 us
  other arithmetic: 54.9 us -> 2.47 us
  blocking collectives: 41.8 us -> 0 us
  starting transfers between devices: 0.08 us -> 39.6 us
  Pallas kernels: 0 us -> 38.3 us
  between operations: 14.2 us -> 0.82 us
  local copies, waits for them, and re-layouts: 42.8 us -> 32.8 us
    psum x2 -> x0, waiting for transfers between devices: 492 us -> none  [shards(): lax.psum((gain, energy, grad_texel), 'pts')]
    dot_general x33 -> x0, matrix products: 61.8 us -> none  [the longest x8 27.4 us: visibility_score(): jnp.einsum('fp,fl->pl', point_block, texel_block, precision=PRECISE)]
    psum x2 -> x0, blocking collectives: 41.8 us -> none  [the longest x1 24.8 us: shards(): lax.psum((grad_alb, grad_rgh, grad_feat), 'lts')]
    ppermute x0 -> x16, starting transfers between devices: none -> 39.6 us  [swap(): return lax.ppermute(x, axis, [(i, i ^ bits) for i in range(n)])]
    pallas_call x0 -> x2, Pallas kernels: none -> 38.3 us  [the longest x1 29.5 us: shards(): pl.pallas_call(shade_kernel, grid=(steps,), in_specs=[smem, whole((2, COL...]
    reduce_sum x13 -> x1, other arithmetic: 33 us -> 0.02 us  [shards(): total = jnp.sum(x[35:38], axis=0, keepdims=True)]
    unnamed x18 -> x58, local copies, waits for them, and re-layouts: 1.75 us -> 31.6 us
    ppermute x0 -> x16, waiting for transfers between devices: none -> 21 us  [swap(): return lax.ppermute(x, axis, [(i, i ^ bits) for i in range(n)])]
  transfers between devices with their start and end apart: 2 -> 16, of which waited for: 2 -> 10; matrix products, arithmetic and copies ran while one was open for 0% -> 1% of each run, Pallas kernels for 0% -> 0%
where the time goes in v1:
time: 136 us; the launch traced here: 135 us
  starting transfers between devices  39.6 us (29%)
  Pallas kernels  38.3 us (28%)
  local copies, waits for them, and re-layouts  32.8 us (24%)
  waiting for transfers between devices  21 us (15%)
  other arithmetic  2.47 us (2%)
    ppermute x16, starting transfers between devices, swap(): return lax.ppermute(x, axis, [(i, i ^ bits) for i in range(n)])  39.6 us
    unnamed x58, local copies, waits for them, and re-layouts  31.6 us
    pallas_call x1, Pallas kernels, shards(): pl.pallas_call(shade_kernel, grid=(steps,), in_specs=[smem, whole((2, COL...  29.5 us
    ppermute x16, waiting for transfers between devices, swap(): return lax.ppermute(x, axis, [(i, i ^ bits) for i in range(n)])  21 us
    pallas_call x1, Pallas kernels, shards(): pl.pallas_call(functools.partial(grad_kernel, scale), grid=(steps,), in_s...  8.78 us
  transfers between devices with their start and end apart: 16, of which 10 were waited for; matrix products, arithmetic and copies ran while one was open for 1% of the time, Pallas kernels for 0%

profile of v1, /device:TPU:1, one launch (start us, length us, event | category | flops | bytes accessed | tf_op | source)
XLA Modules:
  0.0 135.0 jit_solution(12265315975133624201)
XLA Ops:
  8.1 29.5 %shade.1 = (bf16[256,4096]{1,0:T(8,128)(2,1)S(1)}, bf16[256,4096]{1,0:T(8,128)(2,1)S(1)}, bf16[256,4096]{1,0:T(8,128)(2,1)S(1)}, bf16[256,4096]{1,0:T(8,128)(2,1...) custom-call(f32[2,128]{1,0:T(2,128)S(1)} %copy-done.23, ...), custom_call_target="tpu_custom_call" | custom-call | tf_op jit(solution)/shard_map/shade/pallas_call | solution.py:317
  47.0 2.1 %collective-permute-start = (f32[9,256]{1,0:T(8,128)S(1)}, f32[9,256]{1,0:T(8,128)S(1)}, u32[]{:S(2)}, u32[]{:S(2)}) collective-permute-start(f32[9,256]{1,0:T(8,128)S(1)} %get-tuple-element.21), channel_id=1, source_target_pairs={{0,4},{1,5},{2,6},{3,7},{4,0},{5,1},{6,2},{7,3},{8,12},{9,13},{10,... | collective-permute-start | bytes 27656 | tf_op jit(solution)/shard_map/ppermute | solution.py:373
  51.7 2.5 %collective-permute-start.2 = (f32[9,256]{1,0:T(8,128)S(1)}, f32[9,256]{1,0:T(8,128)S(1)}, u32[]{:S(2)}, u32[]{:S(2)}) collective-permute-start(f32[9,256]{1,0:T(8,128)S(1)} %add.56), channel_id=1, source_target_pairs={{0,2},{1,3},{2,0},{3,1},{4,6},{5,7},{6,4},{7,5},{8,10},{9,11},{10,... | collective-permute-start | bytes 27656 | tf_op jit(solution)/shard_map/ppermute | solution.py:373
  54.2 1.6 %collective-permute-done.2 = f32[9,256]{1,0:T(8,128)S(1)} collective-permute-done((f32[9,256]{1,0:T(8,128)S(1)}, f32[9,256]{1,0:T(8,128)S(1)}, u32[]{:S(2)}, u32[]{:S(2)}) %collective-permute-start.2) | collective-permute-done | bytes 9248 | tf_op jit(solution)/shard_map/ppermute | solution.py:373
  55.8 2.2 %collective-permute-done.3 = f32[9,256]{1,0:T(8,128)S(1)} collective-permute-done((f32[9,256]{1,0:T(8,128)S(1)}, f32[9,256]{1,0:T(8,128)S(1)}, u32[]{:S(2)}, u32[]{:S(2)}) %collective-permute-start.3) | collective-permute-done | bytes 9248 | tf_op jit(solution)/shard_map/ppermute | solution.py:373
  59.5 1.6 %copy-done.3 = bf16[256,4096]{1,0:T(8,128)(2,1)S(1)} copy-done((bf16[256,4096]{1,0:T(8,128)(2,1)S(1)}, bf16[256,4096]{1,0:T(8,128)(2,1)}, u32[]{:S(2)}) %copy-start.3) | copy-done | bytes 2097176
  61.1 1.6 %copy-done.5 = bf16[256,4096]{1,0:T(8,128)(2,1)S(1)} copy-done((bf16[256,4096]{1,0:T(8,128)(2,1)S(1)}, bf16[256,4096]{1,0:T(8,128)(2,1)}, u32[]{:S(2)}) %copy-start.5) | copy-done | bytes 2097176
  62.7 1.6 %copy-done.7 = bf16[256,4096]{1,0:T(8,128)(2,1)S(1)} copy-done((bf16[256,4096]{1,0:T(8,128)(2,1)S(1)}, bf16[256,4096]{1,0:T(8,128)(2,1)}, u32[]{:S(2)}) %copy-start.7) | copy-done | bytes 2097176
  64.3 1.6 %copy-done.9 = bf16[256,4096]{1,0:T(8,128)(2,1)S(1)} copy-done((bf16[256,4096]{1,0:T(8,128)(2,1)S(1)}, bf16[256,4096]{1,0:T(8,128)(2,1)}, u32[]{:S(2)}) %copy-start.9) | copy-done | bytes 2097176
  65.9 1.6 %copy-done.11 = bf16[256,4096]{1,0:T(8,128)(2,1)S(1)} copy-done((bf16[256,4096]{1,0:T(8,128)(2,1)S(1)}, bf16[256,4096]{1,0:T(8,128)(2,1)}, u32[]{:S(2)}) %copy-start.11) | copy-done | bytes 2097176
  72.7 8.8 %grads.1 = (f32[8,256]{1,0:T(8,128)S(1)}, f32[32,256]{1,0:T(8,128)S(1)}, f32[40,4096]{1,0:T(8,128)S(1)}) custom-call(f32[9,256]{1,0:T(8,128)S(1)} %add_add_fusion.1.sums_ref, f32[3,256]{1,0:T(4,128)S(1)} %copy-done.20, f32[3,256]{1,0:T(4,128)S(1)} %copy-done.22, f32[32,256]{1,0:T(8,128)S(1)} %copy-done.18, f32[96,256]{1,0:T(8,128)S(1)} %get-tuple-element.22.fb_ref, ...), custom_call_target="tpu_custom_call" | custom-call | tf_op jit(solution)/shard_map/grads/pallas_call | solution.py:378
  81.6 3.6 %collective-permute-start.8 = (f32[40,2048]{1,0:T(8,128)S(1)}, f32[40,2048]{1,0:T(8,128)S(1)}, u32[]{:S(2)}, u32[]{:S(2)}) collective-permute-start(f32[40,2048]{1,0:T(8,128)S(1)} %slice_select_fusion), channel_id=1, source_target_pairs={{0,8},{8,0},{16,24},{24,16},{32,40},{40,32},{48,56},{56,48},{64,72... | collective-permute-start | bytes 983048 | tf_op jit(solution)/shard_map/ppermute | solution.py:373
  86.5 1.7 %collective-permute-start.9 = (f32[40,1024]{1,0:T(8,128)S(1)}, f32[40,1024]{1,0:T(8,128)S(1)}, u32[]{:S(2)}, u32[]{:S(2)}) collective-permute-start(f32[40,1024]{1,0:T(8,128)S(1)} %slice_select_fusion.1), channel_id=1, source_target_pairs={{0,32},{8,40},{16,48},{24,56},{32,0},{40,8},{48,16},{56,24},{64,96... | collective-permute-start | bytes 491528 | tf_op jit(solution)/shard_map/ppermute | solution.py:373
  88.2 4.1 %collective-permute-done.9 = f32[40,1024]{1,0:T(8,128)S(1)} collective-permute-done((f32[40,1024]{1,0:T(8,128)S(1)}, f32[40,1024]{1,0:T(8,128)S(1)}, u32[]{:S(2)}, u32[]{:S(2)}) %collective-permute-start.9) | collective-permute-done | bytes 163872 | tf_op jit(solution)/shard_map/ppermute | solution.py:373
  92.4 3.1 %collective-permute-start.10 = (f32[40,512]{1,0:T(8,128)S(1)}, f32[40,512]{1,0:T(8,128)S(1)}, u32[]{:S(2)}, u32[]{:S(2)}) collective-permute-start(f32[40,512]{1,0:T(8,128)S(1)} %slice_select_fusion.2), channel_id=1, source_target_pairs={{0,64},{8,72},{16,80},{24,88},{32,96},{40,104},{48,112},{56,120},{... | collective-permute-start | bytes 245768 | tf_op jit(solution)/shard_map/ppermute | solution.py:373
  95.5 1.8 %collective-permute-done.10 = f32[40,512]{1,0:T(8,128)S(1)} collective-permute-done((f32[40,512]{1,0:T(8,128)S(1)}, f32[40,512]{1,0:T(8,128)S(1)}, u32[]{:S(2)}, u32[]{:S(2)}) %collective-permute-start.10) | collective-permute-done | bytes 81952 | tf_op jit(solution)/shard_map/ppermute | solution.py:373
  97.4 7.2 %collective-permute-start.11 = (f32[40,512]{1,0:T(8,128)S(1)}, f32[40,512]{1,0:T(8,128)S(1)}, u32[]{:S(2)}, u32[]{:S(2)}) collective-permute-start(f32[40,512]{1,0:T(8,128)S(1)} %select_add_fusion.2), channel_id=1, source_target_pairs={{0,128},{8,136},{16,144},{24,152},{32,160},{40,168},{48,176},{56,1... | collective-permute-start | bytes 245768 | tf_op jit(solution)/shard_map/ppermute | solution.py:373
  104.6 1.8 %collective-permute-done.11 = f32[40,512]{1,0:T(8,128)S(1)} collective-permute-done((f32[40,512]{1,0:T(8,128)S(1)}, f32[40,512]{1,0:T(8,128)S(1)}, u32[]{:S(2)}, u32[]{:S(2)}) %collective-permute-start.11) | collective-permute-done | bytes 81952 | tf_op jit(solution)/shard_map/ppermute | solution.py:373
  106.4 3.0 %collective-permute-start.12 = (f32[40,512]{1,0:T(8,128)S(1)}, f32[40,512]{1,0:T(8,128)S(1)}, u32[]{:S(2)}, u32[]{:S(2)}) collective-permute-start(f32[40,512]{1,0:T(8,128)S(1)} %add.67), channel_id=1, source_target_pairs={{0,16},{8,24},{16,0},{24,8},{32,48},{40,56},{48,32},{56,40},{64,80... | collective-permute-start | bytes 245768 | tf_op jit(solution)/shard_map/ppermute | solution.py:373
  109.4 1.9 %collective-permute-done.12 = f32[40,512]{1,0:T(8,128)S(1)} collective-permute-done((f32[40,512]{1,0:T(8,128)S(1)}, f32[40,512]{1,0:T(8,128)S(1)}, u32[]{:S(2)}, u32[]{:S(2)}) %collective-permute-start.12) | collective-permute-done | bytes 81952 | tf_op jit(solution)/shard_map/ppermute | solution.py:373
  112.3 3.7 %collective-permute-done.13 = f32[35,512]{1,0:T(8,128)S(1)} collective-permute-done((f32[35,512]{1,0:T(8,128)S(1)}, f32[35,512]{1,0:T(8,128)S(1)}, u32[]{:S(2)}, u32[]{:S(2)}) %collective-permute-start.13) | collective-permute-done | bytes 71712 | tf_op jit(solution)/shard_map/ppermute | solution.py:373
  120.2 1.9 %collective-permute-start.6 = (f32[32,256]{1,0:T(8,128)S(1)}, f32[32,256]{1,0:T(8,128)S(1)}, u32[]{:S(2)}, u32[]{:S(2)}) collective-permute-start(f32[32,256]{1,0:T(8,128)S(1)} %add.60), channel_id=1, source_target_pairs={{0,2},{1,3},{2,0},{3,1},{4,6},{5,7},{6,4},{7,5},{8,10},{9,11},{10,... | collective-permute-start | bytes 98312 | tf_op jit(solution)/shard_map/ppermute | solution.py:373
  122.1 1.9 %collective-permute-start.7 = (f32[32,256]{1,0:T(8,128)S(1)}, f32[32,256]{1,0:T(8,128)S(1)}, u32[]{:S(2)}, u32[]{:S(2)}) collective-permute-start(f32[32,256]{1,0:T(8,128)S(1)} %add.60), channel_id=1, source_target_pairs={{0,3},{1,2},{2,1},{3,0},{4,7},{5,6},{6,5},{7,4},{8,11},{9,10},{10,... | collective-permute-start | bytes 98312 | tf_op jit(solution)/shard_map/ppermute | solution.py:373
  124.1 7.6 %collective-permute-start.15 = (f32[35,2048]{1,0:T(8,128)S(1)}, f32[35,2048]{1,0:T(8,128)S(1)}, u32[]{:S(2)}, u32[]{:S(2)}) collective-permute-start(f32[35,2048]{1,0:T(8,128)S(1)} %pad_maximum_fusion.1), channel_id=1, source_target_pairs={{0,8},{8,0},{16,24},{24,16},{32,40},{40,32},{48,56},{56,48},{64,72... | collective-permute-start | bytes 860168 | tf_op jit(solution)/shard_map/ppermute | solution.py:373
  (93 shorter events, 36.2 us)
Async XLA Ops:
  44.3 1.4 %copy-start.10 = (bf16[256,4096]{1,0:T(8,128)(2,1)}, bf16[256,4096]{1,0:T(8,128)(2,1)S(1)}, u32[]{:S(2)}) copy-start(bf16[256,4096]{1,0:T(8,128)(2,1)S(1)} %get-tuple-element.31.qsh_ref) | copy-start | bytes 6291460
  47.0 3.3 %collective-permute-start = (f32[9,256]{1,0:T(8,128)S(1)}, f32[9,256]{1,0:T(8,128)S(1)}, u32[]{:S(2)}, u32[]{:S(2)}) collective-permute-start(f32[9,256]{1,0:T(8,128)S(1)} %get-tuple-element.21), channel_id=1, source_target_pairs={{0,4},{1,5},{2,6},{3,7},{4,0},{5,1},{6,2},{7,3},{8,12},{9,13},{10,... | collective-permute-start | bytes 27656 | tf_op jit(solution)/shard_map/ppermute | solution.py:373
  50.3 3.9 %collective-permute-start.1 = (f32[9,256]{1,0:T(8,128)S(1)}, f32[9,256]{1,0:T(8,128)S(1)}, u32[]{:S(2)}, u32[]{:S(2)}) collective-permute-start(f32[9,256]{1,0:T(8,128)S(1)} %add.56), channel_id=1, source_target_pairs={{0,1},{1,0},{2,3},{3,2},{4,5},{5,4},{6,7},{7,6},{8,9},{9,8},{10,11... | collective-permute-start | bytes 27656 | tf_op jit(solution)/shard_map/ppermute | solution.py:373
  51.7 4.1 %collective-permute-start.2 = (f32[9,256]{1,0:T(8,128)S(1)}, f32[9,256]{1,0:T(8,128)S(1)}, u32[]{:S(2)}, u32[]{:S(2)}) collective-permute-start(f32[9,256]{1,0:T(8,128)S(1)} %add.56), channel_id=1, source_target_pairs={{0,2},{1,3},{2,0},{3,1},{4,6},{5,7},{6,4},{7,5},{8,10},{9,11},{10,... | collective-permute-start | bytes 27656 | tf_op jit(solution)/shard_map/ppermute | solution.py:373
  54.1 3.8 %collective-permute-start.3 = (f32[9,256]{1,0:T(8,128)S(1)}, f32[9,256]{1,0:T(8,128)S(1)}, u32[]{:S(2)}, u32[]{:S(2)}) collective-permute-start(f32[9,256]{1,0:T(8,128)S(1)} %add.56), channel_id=1, source_target_pairs={{0,3},{1,2},{2,1},{3,0},{4,7},{5,6},{6,5},{7,4},{8,11},{9,10},{10,... | collective-permute-start | bytes 27656 | tf_op jit(solution)/shard_map/ppermute | solution.py:373
  57.9 1.6 %copy-start.1 = (bf16[256,4096]{1,0:T(8,128)(2,1)S(1)}, bf16[256,4096]{1,0:T(8,128)(2,1)}, u32[]{:S(2)}) copy-start(bf16[256,4096]{1,0:T(8,128)(2,1)} %copy-done) | copy-start | bytes 6291460
  59.5 1.6 %copy-start.3 = (bf16[256,4096]{1,0:T(8,128)(2,1)S(1)}, bf16[256,4096]{1,0:T(8,128)(2,1)}, u32[]{:S(2)}) copy-start(bf16[256,4096]{1,0:T(8,128)(2,1)} %copy-done.2) | copy-start | bytes 6291460
  61.1 1.6 %copy-start.5 = (bf16[256,4096]{1,0:T(8,128)(2,1)S(1)}, bf16[256,4096]{1,0:T(8,128)(2,1)}, u32[]{:S(2)}) copy-start(bf16[256,4096]{1,0:T(8,128)(2,1)} %copy-done.4) | copy-start | bytes 6291460
  62.7 1.6 %copy-start.7 = (bf16[256,4096]{1,0:T(8,128)(2,1)S(1)}, bf16[256,4096]{1,0:T(8,128)(2,1)}, u32[]{:S(2)}) copy-start(bf16[256,4096]{1,0:T(8,128)(2,1)} %copy-done.6) | copy-start | bytes 6291460
  64.3 1.6 %copy-start.9 = (bf16[256,4096]{1,0:T(8,128)(2,1)S(1)}, bf16[256,4096]{1,0:T(8,128)(2,1)}, u32[]{:S(2)}) copy-start(bf16[256,4096]{1,0:T(8,128)(2,1)} %copy-done.8) | copy-start | bytes 6291460
  65.9 1.6 %copy-start.11 = (bf16[256,4096]{1,0:T(8,128)(2,1)S(1)}, bf16[256,4096]{1,0:T(8,128)(2,1)}, u32[]{:S(2)}) copy-start(bf16[256,4096]{1,0:T(8,128)(2,1)} %copy-done.10) | copy-start | bytes 6291460
  67.5 1.6 %copy-start.13 = (bf16[256,4096]{1,0:T(8,128)(2,1)S(1)}, bf16[256,4096]{1,0:T(8,128)(2,1)}, u32[]{:S(2)}) copy-start(bf16[256,4096]{1,0:T(8,128)(2,1)} %copy-done.12) | copy-start | bytes 6291460
  81.6 4.9 %collective-permute-start.8 = (f32[40,2048]{1,0:T(8,128)S(1)}, f32[40,2048]{1,0:T(8,128)S(1)}, u32[]{:S(2)}, u32[]{:S(2)}) collective-permute-start(f32[40,2048]{1,0:T(8,128)S(1)} %slice_select_fusion), channel_id=1, source_target_pairs={{0,8},{8,0},{16,24},{24,16},{32,40},{40,32},{48,56},{56,48},{64,72... | collective-permute-start | bytes 983048 | tf_op jit(solution)/shard_map/ppermute | solution.py:373
  86.5 5.9 %collective-permute-start.9 = (f32[40,1024]{1,0:T(8,128)S(1)}, f32[40,1024]{1,0:T(8,128)S(1)}, u32[]{:S(2)}, u32[]{:S(2)}) collective-permute-start(f32[40,1024]{1,0:T(8,128)S(1)} %slice_select_fusion.1), channel_id=1, source_target_pairs={{0,32},{8,40},{16,48},{24,56},{32,0},{40,8},{48,16},{56,24},{64,96... | collective-permute-start | bytes 491528 | tf_op jit(solution)/shard_map/ppermute | solution.py:373
  92.4 4.9 %collective-permute-start.10 = (f32[40,512]{1,0:T(8,128)S(1)}, f32[40,512]{1,0:T(8,128)S(1)}, u32[]{:S(2)}, u32[]{:S(2)}) collective-permute-start(f32[40,512]{1,0:T(8,128)S(1)} %slice_select_fusion.2), channel_id=1, source_target_pairs={{0,64},{8,72},{16,80},{24,88},{32,96},{40,104},{48,112},{56,120},{... | collective-permute-start | bytes 245768 | tf_op jit(solution)/shard_map/ppermute | solution.py:373
  97.4 9.0 %collective-permute-start.11 = (f32[40,512]{1,0:T(8,128)S(1)}, f32[40,512]{1,0:T(8,128)S(1)}, u32[]{:S(2)}, u32[]{:S(2)}) collective-permute-start(f32[40,512]{1,0:T(8,128)S(1)} %select_add_fusion.2), channel_id=1, source_target_pairs={{0,128},{8,136},{16,144},{24,152},{32,160},{40,168},{48,176},{56,1... | collective-permute-start | bytes 245768 | tf_op jit(solution)/shard_map/ppermute | solution.py:373
  106.4 4.9 %collective-permute-start.12 = (f32[40,512]{1,0:T(8,128)S(1)}, f32[40,512]{1,0:T(8,128)S(1)}, u32[]{:S(2)}, u32[]{:S(2)}) collective-permute-start(f32[40,512]{1,0:T(8,128)S(1)} %add.67), channel_id=1, source_target_pairs={{0,16},{8,24},{16,0},{24,8},{32,48},{40,56},{48,32},{56,40},{64,80... | collective-permute-start | bytes 245768 | tf_op jit(solution)/shard_map/ppermute | solution.py:373
  111.4 4.6 %collective-permute-start.13 = (f32[35,512]{1,0:T(8,128)S(1)}, f32[35,512]{1,0:T(8,128)S(1)}, u32[]{:S(2)}, u32[]{:S(2)}) collective-permute-start(f32[35,512]{1,0:T(8,128)S(1)} %pad_maximum_fusion.3), channel_id=1, source_target_pairs={{0,64},{8,72},{16,80},{24,88},{32,96},{40,104},{48,112},{56,120},{... | collective-permute-start | bytes 215048 | tf_op jit(solution)/shard_map/ppermute | solution.py:373
  116.0 8.0 %collective-permute-start.14 = (f32[35,1024]{1,0:T(8,128)S(1)}, f32[35,1024]{1,0:T(8,128)S(1)}, u32[]{:S(2)}, u32[]{:S(2)}) collective-permute-start(f32[35,1024]{1,0:T(8,128)S(1)} %pad_maximum_fusion.2), channel_id=1, source_target_pairs={{0,32},{8,40},{16,48},{24,56},{32,0},{40,8},{48,16},{56,24},{64,96... | collective-permute-start | bytes 430088 | tf_op jit(solution)/shard_map/ppermute | solution.py:373
  117.4 2.8 %collective-permute-start.4 = (f32[32,256]{1,0:T(8,128)S(1)}, f32[32,256]{1,0:T(8,128)S(1)}, u32[]{:S(2)}, u32[]{:S(2)}) collective-permute-start(f32[32,256]{1,0:T(8,128)S(1)} %get-tuple-element.34), channel_id=1, source_target_pairs={{0,4},{1,5},{2,6},{3,7},{4,0},{5,1},{6,2},{7,3},{8,12},{9,13},{10,... | collective-permute-start | bytes 98312 | tf_op jit(solution)/shard_map/ppermute | solution.py:373
  120.2 12.7 %collective-permute-start.5 = (f32[32,256]{1,0:T(8,128)S(1)}, f32[32,256]{1,0:T(8,128)S(1)}, u32[]{:S(2)}, u32[]{:S(2)}) collective-permute-start(f32[32,256]{1,0:T(8,128)S(1)} %add.60), channel_id=1, source_target_pairs={{0,1},{1,0},{2,3},{3,2},{4,5},{5,4},{6,7},{7,6},{8,9},{9,8},{10,11... | collective-permute-start | bytes 98312 | tf_op jit(solution)/shard_map/ppermute | solution.py:373
  120.2 12.7 %collective-permute-start.6 = (f32[32,256]{1,0:T(8,128)S(1)}, f32[32,256]{1,0:T(8,128)S(1)}, u32[]{:S(2)}, u32[]{:S(2)}) collective-permute-start(f32[32,256]{1,0:T(8,128)S(1)} %add.60), channel_id=1, source_target_pairs={{0,2},{1,3},{2,0},{3,1},{4,6},{5,7},{6,4},{7,5},{8,10},{9,11},{10,... | collective-permute-start | bytes 98312 | tf_op jit(solution)/shard_map/ppermute | solution.py:373
  122.1 10.7 %collective-permute-start.7 = (f32[32,256]{1,0:T(8,128)S(1)}, f32[32,256]{1,0:T(8,128)S(1)}, u32[]{:S(2)}, u32[]{:S(2)}) collective-permute-start(f32[32,256]{1,0:T(8,128)S(1)} %add.60), channel_id=1, source_target_pairs={{0,3},{1,2},{2,1},{3,0},{4,7},{5,6},{6,5},{7,4},{8,11},{9,10},{10,... | collective-permute-start | bytes 98312 | tf_op jit(solution)/shard_map/ppermute | solution.py:373
  124.1 9.4 %collective-permute-start.15 = (f32[35,2048]{1,0:T(8,128)S(1)}, f32[35,2048]{1,0:T(8,128)S(1)}, u32[]{:S(2)}, u32[]{:S(2)}) collective-permute-start(f32[35,2048]{1,0:T(8,128)S(1)} %pad_maximum_fusion.1), channel_id=1, source_target_pairs={{0,8},{8,0},{16,24},{24,16},{32,40},{40,32},{48,56},{56,48},{64,72... | collective-permute-start | bytes 860168 | tf_op jit(solution)/shard_map/ppermute | solution.py:373
  (21 other events, 19.1 us)

commit v2 on v0

v2 whole, which is shorter than its diff:
```python
import functools
import math

import jax
import jax.numpy as jnp
import numpy as np
from jax import lax
from jax.experimental import pallas as pl
from jax.experimental.pallas import tpu as pltpu
from jax.sharding import PartitionSpec as P

ROWS = 128
COLS = 256
F32 = jnp.float32
BF16 = jnp.bfloat16

THETA = np.pi * (np.arange(ROWS) + 0.5) / ROWS
PHI = 2.0 * np.pi * (np.arange(COLS) + 0.5) / COLS
THETA_TABLE = np.stack([np.sin(THETA), np.cos(THETA)]).astype(np.float32)
PHI_TABLE = np.stack([np.cos(PHI), np.sin(PHI)]).astype(np.float32)

PTS = 256
BLK = 256
CHUNK = 16
UNROLL = 16
(NZ, VZ, NV0, AM1, KEEP, KOFF, C1, C0, YA, YD, YG, ALB) = range(12)
NCONST = 14

NT = (((1,), (1,)), ((), ()))
NN = (((1,), (0,)), ((), ()))


def dot(a, b, dims):
    return lax.dot_general(a, b, dims, preferred_element_type=F32)


def split(x):
    hi = x.astype(BF16)
    return hi, (x - hi.astype(F32)).astype(BF16)


def score_tile(pfs_ref, tfeat):
    t_hi, t_lo = split(tfeat)
    return dot(pfs_ref[...], jnp.concatenate([t_hi, t_hi, t_lo], axis=0), NN)


def fold(x):
    return x[0:8] + x[8:16]


def shade_kernel(
    theta_ref,
    phi_ref,
    normals_ref,
    view_ref,
    cams_ref,
    albedo_ref,
    rough_ref,
    pfeat_ref,
    tfeat_ref,
    env_ref,
    spec_ref,
    sums_ref,
    energy_ref,
    azim_n,
    pfs,
    nz_ref,
    const,
    azim_v,
    score_a,
    score_b,
    mats_a,
    mats_b,
    ebuf,
    acc,
    spec_buf,
    sems,
):
    steps = tfeat_ref.shape[1] // BLK
    first = lax.axis_index("lts") * steps

    def prologue():
        normals = normals_ref[...]
        cams = lax.broadcasted_iota(jnp.int32, (cams_ref.shape[1], PTS), 0)
        choose = (cams == view_ref[...]).astype(F32)
        views = lax.dot_general(
            cams_ref[...], choose, NN, precision=lax.Precision.HIGHEST, preferred_element_type=F32
        )
        rough = rough_ref[...]
        alpha = rough * rough
        alpha_sq = alpha * alpha
        half = 0.5 * alpha
        nv0 = jnp.sum(normals * views, axis=0, keepdims=True)
        nv = jnp.maximum(nv0, 0.1)
        geo_v = nv * (1.0 - half) + half
        lead = alpha_sq / (4.0 * math.pi * geo_v)
        y_d = -4.0 * alpha / (1.0 - alpha_sq)
        y_g = -0.5 / (1.0 - half)
        y_a = 2.0 / alpha - y_d - y_g - (1.0 - nv) / (2.0 * geo_v)
        two_r = 2.0 * rough
        rows = [None] * NCONST
        rows[NZ] = normals[2:3]
        rows[VZ] = 0.5 * views[2:3]
        rows[NV0] = nv0
        rows[AM1] = 0.25 * (alpha_sq - 1.0)
        rows[KEEP] = 1.0 - half
        rows[KOFF] = half
        rows[C1] = 0.96 * lead
        rows[C0] = 0.04 * lead
        rows[YA] = two_r * y_a
        rows[YD] = two_r * y_d
        rows[YG] = two_r * y_g
        for k in range(3):
            rows[ALB + k] = albedo_ref[k : k + 1, :] * (1.0 / math.pi)
        rows += [normals[0:1], normals[1:2], 0.5 * views[0:1], 0.5 * views[1:2]]
        ebuf[...] = jnp.zeros_like(ebuf)
        for k, r in enumerate(rows):
            ebuf[k : k + 1, :] = r
        cols = ebuf[...].T
        for k in range(NCONST):
            const[k] = jnp.broadcast_to(cols[:, k : k + 1], (PTS, 128))
        nz_ref[...] = const[NZ]
        cos_p = phi_ref[0:1, :]
        sin_p = phi_ref[1:2, :]
        k = NCONST
        azim_n[...] = cols[:, k : k + 1] * cos_p + cols[:, k + 1 : k + 2] * sin_p
        azim_v[...] = cols[:, k + 2 : k + 3] * cos_p + cols[:, k + 3 : k + 4] * sin_p
        hi, lo = split((pfeat_ref[...] * (0.5 / math.sqrt(pfeat_ref.shape[0]))).T)
        pfs[:, 0:32] = hi
        pfs[:, 32:64] = lo
        pfs[:, 64:96] = hi
        ebuf[...] = jnp.zeros_like(ebuf)
        acc[...] = jnp.zeros_like(acc)

    prologue()
    mats_b[...] = jnp.zeros_like(mats_b)

    def place(step):
        return pl.ds(pl.multiple_of(step * BLK, BLK), BLK)

    def light_of(step):
        return env_ref[:, place(step)] * (theta_ref[0, first + step] * (0.25 * math.pi))

    def spec_copy(step):
        return pltpu.make_async_copy(spec_buf.at[step], spec_ref.at[step], sems.at[step])

    def shade(step, score, mats):
        sin_t = theta_ref[0, first + step]
        cos_t = theta_ref[1, first + step]
        light = light_of(step)

        def chunk(i, eng):
            r0 = pl.multiple_of(i * CHUNK, CHUNK)
            rows = pl.ds(r0, CHUNK)
            c = [const[k, rows, :] for k in range(NCONST)]
            nz = c[NZ] * cos_t
            vz = c[VZ] * cos_t + 0.5
            eng = list(eng)
            for h in range(BLK // 128):
                lanes = pl.ds(h * 128, 128)
                nl = azim_n[rows, lanes] * sin_t + nz
                vv = azim_v[rows, lanes] * sin_t + vz
                tt = jnp.tanh(score[rows, lanes])
                lit = jnp.maximum(nl, 0.0)
                inv_len = lax.rsqrt(jnp.maximum(vv, 0.125))
                nh = (nl + c[NV0]) * inv_len
                dd = nh * nh * c[AM1] + 1.0
                gg = lit * c[KEEP] + c[KOFF]
                inv = pl.reciprocal(dd * dd * gg, approx=True)
                x1 = 1.0 - vv * inv_len
                x2 = x1 * x1
                fres = x2 * x2 * x1 * c[C1] + c[C0]
                base = (1.0 + tt) * lit
                spec = fres * inv * base
                fact = inv * dd * (c[YD] * gg + c[YG] * dd) + c[YA]
                spec_buf[step, rows, lanes] = spec
                for k, x in enumerate((base, spec, spec * fact)):
                    hi, lo = split(x)
                    mats[pl.ds(2 * k * PTS + r0, CHUNK), lanes] = hi
                    mats[pl.ds((2 * k + 1) * PTS + r0, CHUNK), lanes] = lo
                for k in range(3):
                    v = c[ALB + k] * base + spec
                    eng[3 * h + k] += fold(v * v)
            return tuple(eng)

        zero = jnp.zeros((8, 128), F32)
        eng = lax.fori_loop(0, PTS // CHUNK, chunk, (zero,) * 6, unroll=UNROLL)
        for h in range(BLK // 128):
            for k in range(3):
                lk = light[k : k + 1, 128 * h : 128 * h + 128]
                energy_ref[k : k + 1, pl.ds(pl.multiple_of(step * BLK + 128 * h, 128), 128)] = lk * lk * jnp.sum(eng[3 * h + k], axis=0, keepdims=True)

        spec_copy(step).start()

    def contract(step, mats):
        light = light_of(step)
        l_hi = light.astype(BF16).astype(F32)
        ebuf[0:3, :] = l_hi
        ebuf[3:6, :] = light - l_hi
        acc[...] += dot(ebuf[0:16, :].astype(BF16), mats[...], NT)

    score_a[...] = score_tile(pfs, tfeat_ref[:, place(0)])

    @pl.loop(0, steps // 2)
    def pair(j):
        a = 2 * j
        score_b[...] = score_tile(pfs, tfeat_ref[:, place(a + 1)])
        shade(a, score_a, mats_a)
        contract(jnp.maximum(a - 1, 0), mats_b)
        score_a[...] = score_tile(pfs, tfeat_ref[:, place(jnp.minimum(a + 2, steps - 1))])
        shade(a + 1, score_b, mats_b)
        contract(a, mats_a)

    contract(steps - 1, mats_b)
    both = acc[0:3, :] + acc[3:6, :]
    for k in range(3):
        at = 2 * k * PTS
        sums_ref[3 * k : 3 * k + 3, :] = both[:, at : at + PTS] + both[:, at + PTS : at + 2 * PTS]

    @pl.loop(0, steps)
    def drain(step):
        spec_copy(step).wait()


def grad_kernel(
    scale,
    half,
    theta_ref,
    p0_ref,
    p1_ref,
    p2_ref,
    p3_ref,
    albedo_ref,
    observed_ref,
    pfeat_ref,
    azim_n,
    pfs,
    nz_ref,
    tfeat_ref,
    env_ref,
    spec_ref,
    energy_ref,
    before_ref,
    point_ref,
    gpf_ref,
    out_ref,
    const,
    rbuf,
    wmat,
    score_a,
    score_b,
    d_a,
    d_b,
    acc,
    spec_buf,
    sems,
):
    tiles = tfeat_ref.shape[1] // BLK
    steps = tiles // 2
    core = lax.axis_index("pts") % 2
    base_tile = (core if half else 1 - core) * steps
    first = lax.axis_index("lts") * tiles + base_tile
    half_root = 0.5 / math.sqrt(pfeat_ref.shape[0])

    def prologue():
        sums = (p0_ref[...] + p1_ref[...]) + (p2_ref[...] + p3_ref[...])
        alb = albedo_ref[...] * (1.0 / math.pi)
        radiance = scale * (alb * sums[0:3] + sums[3:6])
        resid = radiance - observed_ref[...]
        point_ref[0:3, :] = radiance
        point_ref[3:6, :] = (scale / math.pi) * resid * sums[0:3]
        point_ref[6:7, :] = scale * jnp.sum(resid * sums[6:9], axis=0, keepdims=True)
        rbuf[...] = jnp.zeros_like(rbuf)
        rbuf[0:3, :] = resid * alb
        rbuf[3:6, :] = resid
        cols = rbuf[...].T
        for k in range(6):
            const[k] = jnp.broadcast_to(cols[:, k : k + 1], (PTS, 128))
        hi, lo = split(pfeat_ref[...] * half_root)
        wmat[0:32, :] = hi
        wmat[32:64, :] = lo
        acc[...] = jnp.zeros_like(acc)

    def spec_copy(step):
        return pltpu.make_async_copy(
            spec_ref.at[base_tile + step], spec_buf.at[step], sems.at[step]
        )

    @pl.loop(0, steps)
    def fetch(step):
        spec_copy(step).start()

    prologue()
    mine = pl.ds(pl.multiple_of(base_tile * BLK, BLK), steps * BLK)
    out_ref[35:38, :] = energy_ref[:, mine]
    out_ref[38:40, :] = jnp.zeros((2, steps * BLK), F32)
    d_b[...] = jnp.zeros_like(d_b)

    def place(step):
        return pl.ds(pl.multiple_of(step * BLK, BLK), BLK)

    def tfeat_of(step):
        return tfeat_ref[:, place(base_tile + step)]

    def combine(step, score, d):
        sin_t = theta_ref[0, first + step]
        cos_t = theta_ref[1, first + step]
        light = env_ref[:, place(base_tile + step)] * (sin_t * (0.25 * math.pi))
        spec_copy(step).wait()

        def chunk(i, gain):
            r0 = pl.multiple_of(i * CHUNK, CHUNK)
            rows = pl.ds(r0, CHUNK)
            c = [const[k, rows, :] for k in range(6)]
            nz = nz_ref[rows, :] * cos_t
            gain = list(gain)
            for h in range(BLK // 128):
                lanes = pl.ds(h * 128, 128)
                tt = jnp.tanh(score[rows, lanes])
                lit = jnp.maximum(azim_n[rows, lanes] * sin_t + nz, 0.0)
                base = (1.0 + tt) * lit
                spec = spec_buf[step, rows, lanes]
                total = None
                for k in range(3):
                    v = c[k] * base + c[3 + k] * spec
                    gain[3 * h + k] += fold(v)
                    lv = light[k : k + 1, 128 * h : 128 * h + 128] * v
                    total = lv if total is None else total + lv
                hi, lo = split(total * (1.0 - tt))
                d[0, rows, lanes] = hi
                d[1, rows, lanes] = lo
            return tuple(gain)

        zero = jnp.zeros((8, 128), F32)
        gain = lax.fori_loop(0, PTS // CHUNK, chunk, (zero,) * 6, unroll=UNROLL)
        for h in range(BLK // 128):
            for k in range(3):
                lk = light[k : k + 1, 128 * h : 128 * h + 128]
                out_ref[32 + k : 33 + k, pl.ds(pl.multiple_of(step * BLK + 128 * h, 128), 128)] = lk * jnp.sum(gain[3 * h + k], axis=0, keepdims=True)

    def contract(step, d):
        dh = d[0]
        dl = d[1]
        x = dot(wmat[...], dh, NN)
        out_ref[0:32, place(step)] = x[0:32] + x[32:64] + dot(wmat[0:32, :], dl, NN)
        t_hi, t_lo = split(tfeat_of(step))
        acc[...] += dot(jnp.concatenate([t_hi, t_lo], axis=0), dh, NT)
        acc[0:32, :] += dot(t_hi, dl, NT)

    score_a[...] = score_tile(pfs, tfeat_of(0))

    @pl.loop(0, steps // 2)
    def pair(j):
        a = 2 * j
        score_b[...] = score_tile(pfs, tfeat_of(a + 1))
        combine(a, score_a, d_a)
        contract(jnp.maximum(a - 1, 0), d_b)
        score_a[...] = score_tile(pfs, tfeat_of(jnp.minimum(a + 2, steps - 1)))
        combine(a + 1, score_b, d_b)
        contract(a, d_a)

    contract(steps - 1, d_b)
    gpf_ref[...] = before_ref[...] + (scale * half_root) * (acc[0:32, :] + acc[32:64, :])


def add(*arrays):
    def body(*refs):
        total = refs[0][...]
        for ref in refs[1:-1]:
            total += ref[...]
        refs[-1][...] = total

    shape = jax.ShapeDtypeStruct(arrays[0].shape, F32)
    return pl.pallas_call(body, out_shape=shape, name="add")(*arrays)


def shards(normals, view_index, cam_dirs, albedo, roughness, point_feat, observed, texel_feat, env):
    pts = normals.shape[1]
    tex = env.shape[1]
    steps = tex // BLK
    points_all = lax.axis_size("pts") * pts
    tex_all = tex * lax.axis_size("lts")
    scale = 4.0 * math.pi / tex_all
    theta = jnp.asarray(THETA_TABLE)
    phi = jnp.asarray(PHI_TABLE)

    vmem = pl.BlockSpec(memory_space=pltpu.VMEM)
    smem = pl.BlockSpec(memory_space=pltpu.SMEM)
    params = pltpu.CompilerParams(vmem_limit_bytes=60 * 1024 * 1024)

    def shape(*dims, dtype=F32):
        return jax.ShapeDtypeStruct(dims, dtype)

    spec, sums, energy, azim_n, pfs, nz = pl.pallas_call(
        shade_kernel,
        in_specs=[smem] + [vmem] * 9,
        out_specs=[pl.BlockSpec(memory_space=pl.ANY)] + [vmem] * 5,
        out_shape=[
            shape(steps, pts, BLK),
            shape(9, pts),
            shape(3, tex),
            shape(pts, COLS),
            shape(pts, 96, dtype=BF16),
            shape(pts, 128),
        ],
        scratch_shapes=[
            pltpu.VMEM((NCONST, PTS, 128), F32),
            pltpu.VMEM((PTS, COLS), F32),
            pltpu.VMEM((PTS, BLK), F32),
            pltpu.VMEM((PTS, BLK), F32),
            pltpu.VMEM((6 * PTS, BLK), BF16),
            pltpu.VMEM((6 * PTS, BLK), BF16),
            pltpu.VMEM((24, BLK), F32),
            pltpu.VMEM((16, 6 * PTS), F32),
            pltpu.VMEM((steps, PTS, BLK), F32),
            pltpu.SemaphoreType.DMA((steps,)),
        ],
        compiler_params=params,
        name="shade",
    )(
        theta,
        phi,
        normals,
        view_index.reshape(1, pts),
        cam_dirs,
        albedo,
        roughness.reshape(1, pts),
        point_feat,
        texel_feat,
        env,
    )

    def swap(x, axis, bits):
        n = lax.axis_size(axis)
        return lax.ppermute(x, axis, [(i, i ^ bits) for i in range(n)])

    sums = sums + swap(sums, "lts", 4)
    parts = [sums] + [swap(sums, "lts", k) for k in (1, 2, 3)]

    def grads(half, before):
        anywhere = pl.BlockSpec(memory_space=pl.ANY)
        return pl.pallas_call(
            functools.partial(grad_kernel, scale, half),
            in_specs=[smem] + [vmem] * 12 + [anywhere] + [vmem] * 2,
            out_specs=[vmem] * 3,
            out_shape=[shape(8, pts), shape(32, pts), shape(40, tex // 2)],
            scratch_shapes=[
                pltpu.VMEM((6, PTS, 128), F32),
                pltpu.VMEM((8, PTS), F32),
                pltpu.VMEM((64, PTS), BF16),
                pltpu.VMEM((PTS, BLK), F32),
                pltpu.VMEM((PTS, BLK), F32),
                pltpu.VMEM((2, PTS, BLK), BF16),
                pltpu.VMEM((2, PTS, BLK), BF16),
                pltpu.VMEM((64, PTS), F32),
                pltpu.VMEM((steps // 2, PTS, BLK), F32),
                pltpu.SemaphoreType.DMA((steps // 2,)),
            ],
            compiler_params=params,
            name="grads" + str(half),
        )(
            theta,
            *parts,
            albedo,
            observed,
            point_feat,
            azim_n,
            pfs,
            nz,
            texel_feat,
            env,
            spec,
            energy,
            before,
        )

    place = lax.axis_index("pts")
    barrier = lax.optimization_barrier
    _, gpf, other = grads(0, jnp.zeros((32, pts), F32))
    other = swap(other, "pts", 1)
    point_out, gpf, own = grads(1, gpf)

    quad = tex // 8
    group = (place >> 1) & 3
    mask = (8, 16, 24)
    x = own + other
    gpf_other = swap(gpf, "lts", 4)
    cut = [lax.dynamic_slice(x, (0, quad * (group ^ m)), (40, quad)) for m in range(4)]
    gpf, *cut = barrier((gpf + gpf_other, *cut))
    got = [swap(cut[m], "pts", 2 * m) for m in (1, 2, 3)]
    gpf_got = [swap(gpf, "lts", m) for m in (1, 2, 3)]
    x = (cut[0] + got[0]) + (got[1] + got[2])
    gpf = (gpf + gpf_got[0]) + (gpf_got[1] + gpf_got[2])
    x, gpf = barrier((x, gpf))
    got = [swap(x, "pts", m) for m in mask]
    x = (x + got[0]) + (got[1] + got[2])
    light_step = x[32:35] * lax.rsqrt(x[35:38] + 1e-06 * points_all)
    total = jnp.sum(x[35:38], axis=0, keepdims=True)
    feat_step = x[0:32] * lax.rsqrt(total + 3e-06 * points_all)
    x = jnp.concatenate([feat_step, light_step], axis=0)
    got = [x] + [swap(x, "pts", 2 * m) for m in (1, 2, 3)]
    pieces = []
    for j in range(4):
        k = group ^ j
        low = jnp.where(k == 0, got[0], got[1])
        pieces.append(jnp.where(k < 2, low, jnp.where(k == 2, got[2], got[3])))
    x = jnp.concatenate(pieces, axis=1)
    other = swap(x, "pts", 1)
    low = (place & 1) == 0
    x = jnp.concatenate([jnp.where(low, x, other), jnp.where(low, other, x)], axis=1)
    return (point_out[0:3], point_out[3:6], point_out[6], gpf, x[32:35], x[0:32])


def solution(mesh):
    return jax.shard_map(
        shards,
        mesh=mesh,
        in_specs=(
            P(None, "pts"),
            P("pts"),
            P(),
            P(None, "pts"),
            P("pts"),
            P(None, "pts"),
            P(None, "pts"),
            P(None, "lts"),
            P(None, "lts"),
        ),
        out_specs=(
            P(None, "pts"),
            P(None, "pts"),
            P("pts"),
            P(None, "pts"),
            P(None, "lts"),
            P(None, "lts"),
        ),
        check_vma=False,
    )
```

time: 709 us -> 94.6 us (0.13)
  waiting for transfers between devices: 492 us -> 20.8 us
  matrix products: 61.8 us -> 0 us
  other arithmetic: 54.9 us -> 4.81 us
  blocking collectives: 41.8 us -> 0 us
  local copies, waits for them, and re-layouts: 42.8 us -> 1.84 us
  starting transfers between devices: 0.08 us -> 37.7 us
  Pallas kernels: 0 us -> 28.4 us
  between operations: 14.2 us -> 0.76 us
    psum x2 -> x0, waiting for transfers between devices: 492 us -> none  [shards(): lax.psum((gain, energy, grad_texel), 'pts')]
    dot_general x33 -> x0, matrix products: 61.8 us -> none  [the longest x8 27.4 us: visibility_score(): jnp.einsum('fp,fl->pl', point_block, texel_block, precision=PRECISE)]
    psum x2 -> x0, blocking collectives: 41.8 us -> none  [the longest x1 24.8 us: shards(): lax.psum((grad_alb, grad_rgh, grad_feat), 'lts')]
    ppermute x0 -> x19, starting transfers between devices: none -> 37.7 us  [swap(): return lax.ppermute(x, axis, [(i, i ^ bits) for i in range(n)])]
    reduce_sum x13 -> x1, other arithmetic: 33 us -> 0.02 us  [shards(): total = jnp.sum(x[35:38], axis=0, keepdims=True)]
    pallas_call x0 -> x3, Pallas kernels: none -> 28.4 us  [the longest x1 14.5 us: shards(): pl.pallas_call(shade_kernel, in_specs=[smem] + [vmem] * 9, out_specs=[pl....]
    ppermute x0 -> x19, waiting for transfers between devices: none -> 20.8 us  [swap(): return lax.ppermute(x, axis, [(i, i ^ bits) for i in range(n)])]
    mul x24 -> x1, other arithmetic: 19.6 us -> 0.01 us  [shards(): feat_step = x[0:32] * lax.rsqrt(total + 3e-06 * points_all)]
  transfers between devices with their start and end apart: 2 -> 19, of which waited for: 2 -> 10; matrix products, arithmetic and copies ran while one was open for 0% -> 3% of each run, Pallas kernels for 0% -> 7%
where the time goes in v2:
time: 94.6 us; the launch traced here: 94.2 us
  starting transfers between devices  37.7 us (40%)
  Pallas kernels  28.4 us (30%)
  waiting for transfers between devices  20.8 us (22%)
  other arithmetic  4.81 us (5%)
  local copies, waits for them, and re-layouts  1.84 us (2%)
    ppermute x19, starting transfers between devices, swap(): return lax.ppermute(x, axis, [(i, i ^ bits) for i in range(n)])  37.7 us
    ppermute x19, waiting for transfers between devices, swap(): return lax.ppermute(x, axis, [(i, i ^ bits) for i in range(n)])  20.8 us
    pallas_call x1, Pallas kernels, shards(): pl.pallas_call(shade_kernel, in_specs=[smem] + [vmem] * 9, out_specs=[pl....  14.5 us
    pallas_call x2, Pallas kernels, grads(): pl.pallas_call(functools.partial(grad_kernel, scale, half), in_specs=[sme...  13.9 us
  transfers between devices with their start and end apart: 19, of which 10 were waited for; matrix products, arithmetic and copies ran while one was open for 3% of the time, Pallas kernels for 7%

profile of v2, /device:TPU:1, one launch (start us, length us, event | category | flops | bytes accessed | tf_op | source)
XLA Modules:
  0.0 94.2 jit_solution(11191815508003370680)
XLA Ops:
  0.6 14.5 %shade.1 = (f32[16,256,256]{2,1,0:T(8,128)}, f32[9,256]{1,0:T(8,128)}, f32[3,4096]{1,0:T(4,128)}, f32[256,256]{1,0:T(8,128)}, bf16[256,96]{1,0:T(8,128)(2,1)}, /*index=5*/f32[256,128]{1,0:T(8,128)}) custom-call(f32[2,128]{1,0:T(2,128)} %constant.29.clone.theta_ref, f32[2,256]{1,0:T(2,128)} %constant.30.clone.phi_ref, f32[3,256]{1,0:T(4,128)} %normals_ref.1, ...), custom_call_target="tpu_custom_call" | custom-call | tf_op jit(solution)/shard_map/shade/pallas_call | solution.py:394
  15.1 2.2 %collective-permute-start = (f32[9,256]{1,0:T(8,128)}, f32[9,256]{1,0:T(8,128)S(1)}, u32[]{:S(2)}, u32[]{:S(2)}) collective-permute-start(f32[9,256]{1,0:T(8,128)} %get-tuple-element.24), channel_id=1, source_target_pairs={{0,4},{1,5},{2,6},{3,7},{4,0},{5,1},{6,2},{7,3},{8,12},{9,13},{10,... | collective-permute-start | bytes 27656 | tf_op jit(solution)/shard_map/ppermute | solution.py:435
  19.4 1.4 %collective-permute-start.1 = (f32[9,256]{1,0:T(8,128)S(1)}, f32[9,256]{1,0:T(8,128)S(1)}, u32[]{:S(2)}, u32[]{:S(2)}) collective-permute-start(f32[9,256]{1,0:T(8,128)S(1)} %add.65.p0_ref), channel_id=1, source_target_pairs={{0,1},{1,0},{2,3},{3,2},{4,5},{5,4},{6,7},{7,6},{8,9},{9,8},{10,11... | collective-permute-start | bytes 27656 | tf_op jit(solution)/shard_map/ppermute | solution.py:435
  20.8 2.4 %collective-permute-start.2 = (f32[9,256]{1,0:T(8,128)S(1)}, f32[9,256]{1,0:T(8,128)S(1)}, u32[]{:S(2)}, u32[]{:S(2)}) collective-permute-start(f32[9,256]{1,0:T(8,128)S(1)} %add.65.p0_ref), channel_id=1, source_target_pairs={{0,2},{1,3},{2,0},{3,1},{4,6},{5,7},{6,4},{7,5},{8,10},{9,11},{10,... | collective-permute-start | bytes 27656 | tf_op jit(solution)/shard_map/ppermute | solution.py:435
  23.3 1.6 %collective-permute-done.2.p2_ref = f32[9,256]{1,0:T(8,128)S(1)} collective-permute-done((f32[9,256]{1,0:T(8,128)S(1)}, f32[9,256]{1,0:T(8,128)S(1)}, u32[]{:S(2)}, u32[]{:S(2)}) %collective-permute-start.2) | collective-permute-done | bytes 9248 | tf_op jit(solution)/shard_map/ppermute | solution.py:435
  24.9 2.2 %collective-permute-done.3.p3_ref = f32[9,256]{1,0:T(8,128)S(1)} collective-permute-done((f32[9,256]{1,0:T(8,128)S(1)}, f32[9,256]{1,0:T(8,128)S(1)}, u32[]{:S(2)}, u32[]{:S(2)}) %collective-permute-start.3) | collective-permute-done | bytes 9248 | tf_op jit(solution)/shard_map/ppermute | solution.py:435
  27.7 7.0 %grads0.1 = (f32[8,256]{1,0:T(8,128)}, f32[32,256]{1,0:T(8,128)}, f32[40,2048]{1,0:T(8,128)}) custom-call(f32[2,128]{1,0:T(2,128)} %constant.29.clone.theta_ref, f32[9,256]{1,0:T(8,128)} %copy-done, f32[9,256]{1,0:T(8,128)} %copy-done.1, f32[9,256]{1,0:T(8,128)} %copy-done.2, f32[9,256]{1,0:T(8,128)} %copy-done.3, f32[3,256]{1,0:T(4,128)} %albedo_ref.5, ...), custom_call_target="tpu_custom_call" | custom-call | tf_op jit(solution)/shard_map/grads0/pallas_call | solution.py:442
  34.6 3.6 %collective-permute-start.5 = (f32[40,2048]{1,0:T(8,128)}, f32[40,2048]{1,0:T(8,128)S(1)}, u32[]{:S(2)}, u32[]{:S(2)}) collective-permute-start(f32[40,2048]{1,0:T(8,128)} %get-tuple-element.34), channel_id=1, source_target_pairs={{0,8},{8,0},{16,24},{24,16},{32,40},{40,32},{48,56},{56,48},{64,72... | collective-permute-start | bytes 983048 | tf_op jit(solution)/shard_map/ppermute | solution.py:435
  38.3 6.9 %grads1.1 = (f32[8,256]{1,0:T(8,128)}, f32[32,256]{1,0:T(8,128)}, f32[40,2048]{1,0:T(8,128)}) custom-call(f32[2,128]{1,0:T(2,128)} %constant.29.clone.theta_ref, f32[9,256]{1,0:T(8,128)} %copy-done, f32[9,256]{1,0:T(8,128)} %copy-done.1, f32[9,256]{1,0:T(8,128)} %copy-done.2, f32[9,256]{1,0:T(8,128)} %copy-done.3, f32[3,256]{1,0:T(4,128)} %albedo_ref.5, ...), custom_call_target="tpu_custom_call" | custom-call | tf_op jit(solution)/shard_map/grads1/pallas_call | solution.py:442
  45.2 1.4 %collective-permute-start.4 = (f32[32,256]{1,0:T(8,128)}, f32[32,256]{1,0:T(8,128)S(1)}, u32[]{:S(2)}, u32[]{:S(2)}) collective-permute-start(f32[32,256]{1,0:T(8,128)} %get-tuple-element.32), channel_id=1, source_target_pairs={{0,4},{1,5},{2,6},{3,7},{4,0},{5,1},{6,2},{7,3},{8,12},{9,13},{10,... | collective-permute-start | bytes 98312 | tf_op jit(solution)/shard_map/ppermute | solution.py:435
  46.6 1.7 %collective-permute-done.4 = f32[32,256]{1,0:T(8,128)S(1)} collective-permute-done((f32[32,256]{1,0:T(8,128)}, f32[32,256]{1,0:T(8,128)S(1)}, u32[]{:S(2)}, u32[]{:S(2)}) %collective-permute-start.4) | collective-permute-done | bytes 32800 | tf_op jit(solution)/shard_map/ppermute | solution.py:435
  50.2 2.0 %collective-permute-start.11 = (f32[32,256]{1,0:T(8,128)S(1)}, f32[32,256]{1,0:T(8,128)S(1)}, u32[]{:S(2)}, u32[]{:S(2)}) collective-permute-start(f32[32,256]{1,0:T(8,128)S(1)} %add.66), channel_id=1, source_target_pairs={{0,3},{1,2},{2,1},{3,0},{4,7},{5,6},{6,5},{7,4},{8,11},{9,10},{10,... | collective-permute-start | bytes 98312 | tf_op jit(solution)/shard_map/ppermute | solution.py:435
  52.8 2.9 %collective-permute-start.6 = (f32[40,512]{1,0:T(8,128)S(1)}, f32[40,512]{1,0:T(8,128)S(1)}, u32[]{:S(2)}, u32[]{:S(2)}) collective-permute-start(f32[40,512]{1,0:T(8,128)S(1)} %get-tuple-element.36), channel_id=1, source_target_pairs={{0,16},{8,24},{16,0},{24,8},{32,48},{40,56},{48,32},{56,40},{64,80... | collective-permute-start | bytes 245768 | tf_op jit(solution)/shard_map/ppermute | solution.py:435
  55.7 1.6 %collective-permute-start.7 = (f32[40,512]{1,0:T(8,128)S(1)}, f32[40,512]{1,0:T(8,128)S(1)}, u32[]{:S(2)}, u32[]{:S(2)}) collective-permute-start(f32[40,512]{1,0:T(8,128)S(1)} %get-tuple-element.37), channel_id=1, source_target_pairs={{0,32},{8,40},{16,48},{24,56},{32,0},{40,8},{48,16},{56,24},{64,96... | collective-permute-start | bytes 245768 | tf_op jit(solution)/shard_map/ppermute | solution.py:435
  57.4 1.4 %collective-permute-start.8 = (f32[40,512]{1,0:T(8,128)S(1)}, f32[40,512]{1,0:T(8,128)S(1)}, u32[]{:S(2)}, u32[]{:S(2)}) collective-permute-start(f32[40,512]{1,0:T(8,128)S(1)} %get-tuple-element.38), channel_id=1, source_target_pairs={{0,48},{8,56},{16,32},{24,40},{32,16},{40,24},{48,0},{56,8},{64,11... | collective-permute-start | bytes 245768 | tf_op jit(solution)/shard_map/ppermute | solution.py:435
  59.5 3.6 %collective-permute-done.8 = f32[40,512]{1,0:T(8,128)S(1)} collective-permute-done((f32[40,512]{1,0:T(8,128)S(1)}, f32[40,512]{1,0:T(8,128)S(1)}, u32[]{:S(2)}, u32[]{:S(2)}) %collective-permute-start.8) | collective-permute-done | bytes 81952 | tf_op jit(solution)/shard_map/ppermute | solution.py:435
  63.1 3.3 %collective-permute-start.12 = (f32[40,512]{1,0:T(8,128)S(1)}, f32[40,512]{1,0:T(8,128)S(1)}, u32[]{:S(2)}, u32[]{:S(2)}) collective-permute-start(f32[40,512]{1,0:T(8,128)S(1)} %add_add_fusion.1), channel_id=1, source_target_pairs={{0,64},{8,72},{16,80},{24,88},{32,96},{40,104},{48,112},{56,120},{... | collective-permute-start | bytes 245768 | tf_op jit(solution)/shard_map/ppermute | solution.py:435
  66.4 4.5 %collective-permute-start.13 = (f32[40,512]{1,0:T(8,128)S(1)}, f32[40,512]{1,0:T(8,128)S(1)}, u32[]{:S(2)}, u32[]{:S(2)}) collective-permute-start(f32[40,512]{1,0:T(8,128)S(1)} %add_add_fusion.1), channel_id=1, source_target_pairs={{0,128},{8,136},{16,144},{24,152},{32,160},{40,168},{48,176},{56,1... | collective-permute-start | bytes 245768 | tf_op jit(solution)/shard_map/ppermute | solution.py:435
  70.8 2.8 %collective-permute-done.13 = f32[40,512]{1,0:T(8,128)S(1)} collective-permute-done((f32[40,512]{1,0:T(8,128)S(1)}, f32[40,512]{1,0:T(8,128)S(1)}, u32[]{:S(2)}, u32[]{:S(2)}) %collective-permute-start.13) | collective-permute-done | bytes 81952 | tf_op jit(solution)/shard_map/ppermute | solution.py:435
  73.6 4.2 %collective-permute-done.14 = f32[40,512]{1,0:T(8,128)S(1)} collective-permute-done((f32[40,512]{1,0:T(8,128)S(1)}, f32[40,512]{1,0:T(8,128)S(1)}, u32[]{:S(2)}, u32[]{:S(2)}) %collective-permute-start.14) | collective-permute-done | bytes 81952 | tf_op jit(solution)/shard_map/ppermute | solution.py:435
  78.1 1.6 %collective-permute-start.16 = (f32[35,512]{1,0:T(8,128)S(1)}, f32[35,512]{1,0:T(8,128)S(1)}, u32[]{:S(2)}, u32[]{:S(2)}) collective-permute-start(f32[35,512]{1,0:T(8,128)S(1)} %pad_maximum_fusion.2), channel_id=1, source_target_pairs={{0,32},{8,40},{16,48},{24,56},{32,0},{40,8},{48,16},{56,24},{64,96... | collective-permute-start | bytes 215048 | tf_op jit(solution)/shard_map/ppermute | solution.py:435
  79.8 2.4 %collective-permute-start.17 = (f32[35,512]{1,0:T(8,128)S(1)}, f32[35,512]{1,0:T(8,128)S(1)}, u32[]{:S(2)}, u32[]{:S(2)}) collective-permute-start(f32[35,512]{1,0:T(8,128)S(1)} %pad_maximum_fusion.2), channel_id=1, source_target_pairs={{0,48},{8,56},{16,32},{24,40},{32,16},{40,24},{48,0},{56,8},{64,11... | collective-permute-start | bytes 215048 | tf_op jit(solution)/shard_map/ppermute | solution.py:435
  82.8 2.7 %collective-permute-done.17 = f32[35,512]{1,0:T(8,128)S(1)} collective-permute-done((f32[35,512]{1,0:T(8,128)S(1)}, f32[35,512]{1,0:T(8,128)S(1)}, u32[]{:S(2)}, u32[]{:S(2)}) %collective-permute-start.17) | collective-permute-done | bytes 71712 | tf_op jit(solution)/shard_map/ppermute | solution.py:435
  85.6 5.9 %collective-permute-start.18 = (f32[35,2048]{1,0:T(8,128)S(1)}, f32[35,2048]{1,0:T(8,128)S(1)}, u32[]{:S(2)}, u32[]{:S(2)}) collective-permute-start(f32[35,2048]{1,0:T(8,128)S(1)} %pad_maximum_fusion.1), channel_id=1, source_target_pairs={{0,8},{8,0},{16,24},{24,16},{32,40},{40,32},{48,56},{56,48},{64,72... | collective-permute-start | bytes 860168 | tf_op jit(solution)/shard_map/ppermute | solution.py:435
  (47 shorter events, 9.7 us)
Async XLA Ops:
  15.1 3.6 %collective-permute-start = (f32[9,256]{1,0:T(8,128)}, f32[9,256]{1,0:T(8,128)S(1)}, u32[]{:S(2)}, u32[]{:S(2)}) collective-permute-start(f32[9,256]{1,0:T(8,128)} %get-tuple-element.24), channel_id=1, source_target_pairs={{0,4},{1,5},{2,6},{3,7},{4,0},{5,1},{6,2},{7,3},{8,12},{9,13},{10,... | collective-permute-start | bytes 27656 | tf_op jit(solution)/shard_map/ppermute | solution.py:435
  19.4 8.3 %copy-start = (f32[9,256]{1,0:T(8,128)}, f32[9,256]{1,0:T(8,128)S(1)}, u32[]{:S(2)}) copy-start(f32[9,256]{1,0:T(8,128)S(1)} %add.65.p0_ref) | copy-start | bytes 27652
  19.4 3.9 %collective-permute-start.1 = (f32[9,256]{1,0:T(8,128)S(1)}, f32[9,256]{1,0:T(8,128)S(1)}, u32[]{:S(2)}, u32[]{:S(2)}) collective-permute-start(f32[9,256]{1,0:T(8,128)S(1)} %add.65.p0_ref), channel_id=1, source_target_pairs={{0,1},{1,0},{2,3},{3,2},{4,5},{5,4},{6,7},{7,6},{8,9},{9,8},{10,11... | collective-permute-start | bytes 27656 | tf_op jit(solution)/shard_map/ppermute | solution.py:435
  20.8 4.1 %collective-permute-start.2 = (f32[9,256]{1,0:T(8,128)S(1)}, f32[9,256]{1,0:T(8,128)S(1)}, u32[]{:S(2)}, u32[]{:S(2)}) collective-permute-start(f32[9,256]{1,0:T(8,128)S(1)} %add.65.p0_ref), channel_id=1, source_target_pairs={{0,2},{1,3},{2,0},{3,1},{4,6},{5,7},{6,4},{7,5},{8,10},{9,11},{10,... | collective-permute-start | bytes 27656 | tf_op jit(solution)/shard_map/ppermute | solution.py:435
  23.2 3.8 %collective-permute-start.3 = (f32[9,256]{1,0:T(8,128)S(1)}, f32[9,256]{1,0:T(8,128)S(1)}, u32[]{:S(2)}, u32[]{:S(2)}) collective-permute-start(f32[9,256]{1,0:T(8,128)S(1)} %add.65.p0_ref), channel_id=1, source_target_pairs={{0,3},{1,2},{2,1},{3,0},{4,7},{5,6},{6,5},{7,4},{8,11},{9,10},{10,... | collective-permute-start | bytes 27656 | tf_op jit(solution)/shard_map/ppermute | solution.py:435
  23.3 4.4 %copy-start.1 = (f32[9,256]{1,0:T(8,128)}, f32[9,256]{1,0:T(8,128)S(1)}, u32[]{:S(2)}) copy-start(f32[9,256]{1,0:T(8,128)S(1)} %collective-permute-done.1.p1_ref) | copy-start | bytes 27652
  24.9 2.8 %copy-start.2 = (f32[9,256]{1,0:T(8,128)}, f32[9,256]{1,0:T(8,128)S(1)}, u32[]{:S(2)}) copy-start(f32[9,256]{1,0:T(8,128)S(1)} %collective-permute-done.2.p2_ref) | copy-start | bytes 27652
  27.0 0.6 copy-start.3
  34.6 14.4 %collective-permute-start.5 = (f32[40,2048]{1,0:T(8,128)}, f32[40,2048]{1,0:T(8,128)S(1)}, u32[]{:S(2)}, u32[]{:S(2)}) collective-permute-start(f32[40,2048]{1,0:T(8,128)} %get-tuple-element.34), channel_id=1, source_target_pairs={{0,8},{8,0},{16,24},{24,16},{32,40},{40,32},{48,56},{56,48},{64,72... | collective-permute-start | bytes 983048 | tf_op jit(solution)/shard_map/ppermute | solution.py:435
  45.2 46.3 %copy-start.4 = (f32[8,256]{1,0:T(8,128)S(1)}, f32[8,256]{1,0:T(8,128)}, u32[]{:S(2)}) copy-start(f32[8,256]{1,0:T(8,128)} %get-tuple-element.31) | copy-start | bytes 24580
  45.2 3.1 %collective-permute-start.4 = (f32[32,256]{1,0:T(8,128)}, f32[32,256]{1,0:T(8,128)S(1)}, u32[]{:S(2)}, u32[]{:S(2)}) collective-permute-start(f32[32,256]{1,0:T(8,128)} %get-tuple-element.32), channel_id=1, source_target_pairs={{0,4},{1,5},{2,6},{3,7},{4,0},{5,1},{6,2},{7,3},{8,12},{9,13},{10,... | collective-permute-start | bytes 98312 | tf_op jit(solution)/shard_map/ppermute | solution.py:435
  50.1 7.3 %collective-permute-start.10 = (f32[32,256]{1,0:T(8,128)S(1)}, f32[32,256]{1,0:T(8,128)S(1)}, u32[]{:S(2)}, u32[]{:S(2)}) collective-permute-start(f32[32,256]{1,0:T(8,128)S(1)} %add.66), channel_id=1, source_target_pairs={{0,2},{1,3},{2,0},{3,1},{4,6},{5,7},{6,4},{7,5},{8,10},{9,11},{10,... | collective-permute-start | bytes 98312 | tf_op jit(solution)/shard_map/ppermute | solution.py:435
  50.2 8.6 %collective-permute-start.11 = (f32[32,256]{1,0:T(8,128)S(1)}, f32[32,256]{1,0:T(8,128)S(1)}, u32[]{:S(2)}, u32[]{:S(2)}) collective-permute-start(f32[32,256]{1,0:T(8,128)S(1)} %add.66), channel_id=1, source_target_pairs={{0,3},{1,2},{2,1},{3,0},{4,7},{5,6},{6,5},{7,4},{8,11},{9,10},{10,... | collective-permute-start | bytes 98312 | tf_op jit(solution)/shard_map/ppermute | solution.py:435
  52.2 6.6 %collective-permute-start.9 = (f32[32,256]{1,0:T(8,128)S(1)}, f32[32,256]{1,0:T(8,128)S(1)}, u32[]{:S(2)}, u32[]{:S(2)}) collective-permute-start(f32[32,256]{1,0:T(8,128)S(1)} %add.66), channel_id=1, source_target_pairs={{0,1},{1,0},{2,3},{3,2},{4,5},{5,4},{6,7},{7,6},{8,9},{9,8},{10,11... | collective-permute-start | bytes 98312 | tf_op jit(solution)/shard_map/ppermute | solution.py:435
  52.8 6.6 %collective-permute-start.6 = (f32[40,512]{1,0:T(8,128)S(1)}, f32[40,512]{1,0:T(8,128)S(1)}, u32[]{:S(2)}, u32[]{:S(2)}) collective-permute-start(f32[40,512]{1,0:T(8,128)S(1)} %get-tuple-element.36), channel_id=1, source_target_pairs={{0,16},{8,24},{16,0},{24,8},{32,48},{40,56},{48,32},{56,40},{64,80... | collective-permute-start | bytes 245768 | tf_op jit(solution)/shard_map/ppermute | solution.py:435
  55.7 3.8 %collective-permute-start.7 = (f32[40,512]{1,0:T(8,128)S(1)}, f32[40,512]{1,0:T(8,128)S(1)}, u32[]{:S(2)}, u32[]{:S(2)}) collective-permute-start(f32[40,512]{1,0:T(8,128)S(1)} %get-tuple-element.37), channel_id=1, source_target_pairs={{0,32},{8,40},{16,48},{24,56},{32,0},{40,8},{48,16},{56,24},{64,96... | collective-permute-start | bytes 245768 | tf_op jit(solution)/shard_map/ppermute | solution.py:435
  57.4 5.7 %collective-permute-start.8 = (f32[40,512]{1,0:T(8,128)S(1)}, f32[40,512]{1,0:T(8,128)S(1)}, u32[]{:S(2)}, u32[]{:S(2)}) collective-permute-start(f32[40,512]{1,0:T(8,128)S(1)} %get-tuple-element.38), channel_id=1, source_target_pairs={{0,48},{8,56},{16,32},{24,40},{32,16},{40,24},{48,0},{56,8},{64,11... | collective-permute-start | bytes 245768 | tf_op jit(solution)/shard_map/ppermute | solution.py:435
  63.1 7.7 %collective-permute-start.12 = (f32[40,512]{1,0:T(8,128)S(1)}, f32[40,512]{1,0:T(8,128)S(1)}, u32[]{:S(2)}, u32[]{:S(2)}) collective-permute-start(f32[40,512]{1,0:T(8,128)S(1)} %add_add_fusion.1), channel_id=1, source_target_pairs={{0,64},{8,72},{16,80},{24,88},{32,96},{40,104},{48,112},{56,120},{... | collective-permute-start | bytes 245768 | tf_op jit(solution)/shard_map/ppermute | solution.py:435
  66.4 7.3 %collective-permute-start.13 = (f32[40,512]{1,0:T(8,128)S(1)}, f32[40,512]{1,0:T(8,128)S(1)}, u32[]{:S(2)}, u32[]{:S(2)}) collective-permute-start(f32[40,512]{1,0:T(8,128)S(1)} %add_add_fusion.1), channel_id=1, source_target_pairs={{0,128},{8,136},{16,144},{24,152},{32,160},{40,168},{48,176},{56,1... | collective-permute-start | bytes 245768 | tf_op jit(solution)/shard_map/ppermute | solution.py:435
  70.8 7.0 %collective-permute-start.14 = (f32[40,512]{1,0:T(8,128)S(1)}, f32[40,512]{1,0:T(8,128)S(1)}, u32[]{:S(2)}, u32[]{:S(2)}) collective-permute-start(f32[40,512]{1,0:T(8,128)S(1)} %add_add_fusion.1), channel_id=1, source_target_pairs={{0,192},{8,200},{16,208},{24,216},{32,224},{40,232},{48,240},{56,2... | collective-permute-start | bytes 245768 | tf_op jit(solution)/shard_map/ppermute | solution.py:435
  77.9 4.9 %collective-permute-start.15 = (f32[35,512]{1,0:T(8,128)S(1)}, f32[35,512]{1,0:T(8,128)S(1)}, u32[]{:S(2)}, u32[]{:S(2)}) collective-permute-start(f32[35,512]{1,0:T(8,128)S(1)} %pad_maximum_fusion.2), channel_id=1, source_target_pairs={{0,16},{8,24},{16,0},{24,8},{32,48},{40,56},{48,32},{56,40},{64,80... | collective-permute-start | bytes 215048 | tf_op jit(solution)/shard_map/ppermute | solution.py:435
  78.1 4.7 %collective-permute-start.16 = (f32[35,512]{1,0:T(8,128)S(1)}, f32[35,512]{1,0:T(8,128)S(1)}, u32[]{:S(2)}, u32[]{:S(2)}) collective-permute-start(f32[35,512]{1,0:T(8,128)S(1)} %pad_maximum_fusion.2), channel_id=1, source_target_pairs={{0,32},{8,40},{16,48},{24,56},{32,0},{40,8},{48,16},{56,24},{64,96... | collective-permute-start | bytes 215048 | tf_op jit(solution)/shard_map/ppermute | solution.py:435
  79.8 5.7 %collective-permute-start.17 = (f32[35,512]{1,0:T(8,128)S(1)}, f32[35,512]{1,0:T(8,128)S(1)}, u32[]{:S(2)}, u32[]{:S(2)}) collective-permute-start(f32[35,512]{1,0:T(8,128)S(1)} %pad_maximum_fusion.2), channel_id=1, source_target_pairs={{0,48},{8,56},{16,32},{24,40},{32,16},{40,24},{48,0},{56,8},{64,11... | collective-permute-start | bytes 215048 | tf_op jit(solution)/shard_map/ppermute | solution.py:435
  85.6 7.2 %collective-permute-start.18 = (f32[35,2048]{1,0:T(8,128)S(1)}, f32[35,2048]{1,0:T(8,128)S(1)}, u32[]{:S(2)}, u32[]{:S(2)}) collective-permute-start(f32[35,2048]{1,0:T(8,128)S(1)} %pad_maximum_fusion.1), channel_id=1, source_target_pairs={{0,8},{8,0},{16,24},{24,16},{32,40},{40,32},{48,56},{56,48},{64,72... | collective-permute-start | bytes 860168 | tf_op jit(solution)/shard_map/ppermute | solution.py:435

commit v3 on v2

--- a/solution.py
+++ b/solution.py
@@ -73,6 +73,7 @@
     mats_b,
     ebuf,
     acc,
+    acc_rad,
     spec_buf,
     sems,
 ):
@@ -131,6 +132,7 @@
         pfs[:, 64:96] = hi
         ebuf[...] = jnp.zeros_like(ebuf)
         acc[...] = jnp.zeros_like(acc)
+        acc_rad[...] = jnp.zeros_like(acc_rad)
 
     prologue()
     mats_b[...] = jnp.zeros_like(mats_b)
@@ -156,6 +158,7 @@
             nz = c[NZ] * cos_t
             vz = c[VZ] * cos_t + 0.5
             eng = list(eng)
+            rad = [None] * 3
             for h in range(BLK // 128):
                 lanes = pl.ds(h * 128, 128)
                 nl = azim_n[rows, lanes] * sin_t + nz
@@ -174,13 +177,17 @@
                 spec = fres * inv * base
                 fact = inv * dd * (c[YD] * gg + c[YG] * dd) + c[YA]
                 spec_buf[step, rows, lanes] = spec
-                for k, x in enumerate((base, spec, spec * fact)):
-                    hi, lo = split(x)
-                    mats[pl.ds(2 * k * PTS + r0, CHUNK), lanes] = hi
-                    mats[pl.ds((2 * k + 1) * PTS + r0, CHUNK), lanes] = lo
+                hi, lo = split(spec * fact)
+                mats[pl.ds(r0, CHUNK), lanes] = base.astype(BF16)
+                mats[pl.ds(PTS + r0, CHUNK), lanes] = hi
+                mats[pl.ds(2 * PTS + r0, CHUNK), lanes] = lo
                 for k in range(3):
                     v = c[ALB + k] * base + spec
                     eng[3 * h + k] += fold(v * v)
+                    lv = light[k : k + 1, 128 * h : 128 * h + 128] * v
+                    rad[k] = lv if h == 0 else rad[k] + lv
+            for k in range(3):
+                acc_rad[k, rows, :] += rad[k]
             return tuple(eng)
 
         zero = jnp.zeros((8, 128), F32)
@@ -213,9 +220,13 @@
 
     contract(steps - 1, mats_b)
     both = acc[0:3, :] + acc[3:6, :]
+    rows = [both[:, 0:PTS], both[:, PTS : 2 * PTS] + both[:, 2 * PTS : 3 * PTS]]
     for k in range(3):
-        at = 2 * k * PTS
-        sums_ref[3 * k : 3 * k + 3, :] = both[:, at : at + PTS] + both[:, at + PTS : at + 2 * PTS]
+        const[0, :, k : k + 1] = jnp.sum(acc_rad[k], axis=1, keepdims=True)
+    rows.append(const[0].T[0:3, :])
+    for j in range(sums_ref.shape[0]):
+        for k in range(3):
+            sums_ref[j, 3 * k : 3 * k + 3, :] = rows[k]
 
     @pl.loop(0, steps)
     def drain(step):
@@ -226,10 +237,7 @@
     scale,
     half,
     theta_ref,
-    p0_ref,
-    p1_ref,
-    p2_ref,
-    p3_ref,
+    sums_ref,
     albedo_ref,
     observed_ref,
     pfeat_ref,
@@ -241,7 +249,9 @@
     spec_ref,
     energy_ref,
     before_ref,
-    point_ref,
+    rad_ref,
+    galb_ref,
+    grough_ref,
     gpf_ref,
     out_ref,
     const,
@@ -263,13 +273,15 @@
     half_root = 0.5 / math.sqrt(pfeat_ref.shape[0])
 
     def prologue():
-        sums = (p0_ref[...] + p1_ref[...]) + (p2_ref[...] + p3_ref[...])
+        sums = sums_ref[0]
+        for k in range(1, sums_ref.shape[0]):
+            sums += sums_ref[k]
         alb = albedo_ref[...] * (1.0 / math.pi)
-        radiance = scale * (alb * sums[0:3] + sums[3:6])
+        radiance = scale * sums[6:9]
         resid = radiance - observed_ref[...]
-        point_ref[0:3, :] = radiance
-        point_ref[3:6, :] = (scale / math.pi) * resid * sums[0:3]
-        point_ref[6:7, :] = scale * jnp.sum(resid * sums[6:9], axis=0, keepdims=True)
+        rad_ref[...] = radiance
+        galb_ref[...] = (scale / math.pi) * resid * sums[0:3]
+        grough_ref[...] = scale * jnp.sum(resid * sums[3:6], axis=0, keepdims=True)
         rbuf[...] = jnp.zeros_like(rbuf)
         rbuf[0:3, :] = resid * alb
         rbuf[3:6, :] = resid
@@ -360,18 +372,26 @@
         contract(a, d_a)
 
     contract(steps - 1, d_b)
-    gpf_ref[...] = before_ref[...] + (scale * half_root) * (acc[0:32, :] + acc[32:64, :])
-
-
-def add(*arrays):
-    def body(*refs):
-        total = refs[0][...]
-        for ref in refs[1:-1]:
-            total += ref[...]
-        refs[-1][...] = total
-
-    shape = jax.ShapeDtypeStruct(arrays[0].shape, F32)
-    return pl.pallas_call(body, out_shape=shape, name="add")(*arrays)
+    gpf = (scale * half_root) * (acc[0:32, :] + acc[32:64, :])
+    gpf_ref[...] = gpf + before_ref[...] if half else gpf
+
+
+def join_kernel(own_ref, other_ref, feat_ref, light_ref):
+    core = lax.axis_index("pts") % 2
+    count = own_ref.shape[1]
+    for x_ref, at in ((own_ref, core), (other_ref, 1 - core)):
+        lanes = pl.ds(pl.multiple_of(at * count, count), count)
+        feat_ref[:, lanes] = x_ref[0:32, :]
+        light_ref[:, lanes] = x_ref[32:35, :]
+
+
+def join(own, other, tex):
+    return pl.pallas_call(
+        join_kernel,
+        out_shape=[jax.ShapeDtypeStruct((32, tex), F32), jax.ShapeDtypeStruct((3, tex), F32)],
+        compiler_params=pltpu.CompilerParams(vmem_limit_bytes=4 * 1024 * 1024),
+        name="join",
+    )(own, other)
 
 
 def shards(normals, view_index, cam_dirs, albedo, roughness, point_feat, observed, texel_feat, env):
@@ -386,7 +406,15 @@
 
     vmem = pl.BlockSpec(memory_space=pltpu.VMEM)
     smem = pl.BlockSpec(memory_space=pltpu.SMEM)
-    params = pltpu.CompilerParams(vmem_limit_bytes=60 * 1024 * 1024)
+    params = pltpu.CompilerParams(vmem_limit_bytes=20 * 1024 * 1024)
+
+    def hbm(x):
+        return pltpu.with_memory_space_constraint(x, pltpu.HBM)
+
+    normals, cam_dirs, albedo, point_feat, observed, texel_feat, env, theta, phi = map(
+        hbm, (normals, cam_dirs, albedo, point_feat, observed, texel_feat, env, theta, phi)
+    )
+    view_index, roughness = (hbm(x.reshape(1, pts)) for x in (view_index, roughness))
 
     def shape(*dims, dtype=F32):
         return jax.ShapeDtypeStruct(dims, dtype)
@@ -396,8 +424,8 @@
         in_specs=[smem] + [vmem] * 9,
         out_specs=[pl.BlockSpec(memory_space=pl.ANY)] + [vmem] * 5,
         out_shape=[
-            shape(steps, pts, BLK),
-            shape(9, pts),
+            pltpu.HBM((steps, pts, BLK), F32),
+            shape(lax.axis_size("lts"), 9, pts),
             shape(3, tex),
             shape(pts, COLS),
             shape(pts, 96, dtype=BF16),
@@ -408,10 +436,11 @@
             pltpu.VMEM((PTS, COLS), F32),
             pltpu.VMEM((PTS, BLK), F32),
             pltpu.VMEM((PTS, BLK), F32),
-            pltpu.VMEM((6 * PTS, BLK), BF16),
-            pltpu.VMEM((6 * PTS, BLK), BF16),
+            pltpu.VMEM((3 * PTS, BLK), BF16),
+            pltpu.VMEM((3 * PTS, BLK), BF16),
             pltpu.VMEM((24, BLK), F32),
-            pltpu.VMEM((16, 6 * PTS), F32),
+            pltpu.VMEM((16, 3 * PTS), F32),
+            pltpu.VMEM((3, PTS, 128), F32),
             pltpu.VMEM((steps, PTS, BLK), F32),
             pltpu.SemaphoreType.DMA((steps,)),
         ],
@@ -421,10 +450,10 @@
         theta,
         phi,
         normals,
-        view_index.reshape(1, pts),
+        view_index,
         cam_dirs,
         albedo,
-        roughness.reshape(1, pts),
+        roughness,
         point_feat,
         texel_feat,
         env,
@@ -434,16 +463,20 @@
         n = lax.axis_size(axis)
         return lax.ppermute(x, axis, [(i, i ^ bits) for i in range(n)])
 
-    sums = sums + swap(sums, "lts", 4)
-    parts = [sums] + [swap(sums, "lts", k) for k in (1, 2, 3)]
-
-    def grads(half, before):
+    spec = hbm(spec)
+    sums = lax.all_to_all(sums, "lts", 0, 0)
+
+    def grads(half, *before):
+        def kernel(*refs):
+            refs = refs if half else refs[:12] + (None,) + refs[12:]
+            grad_kernel(scale, half, *refs)
+
         anywhere = pl.BlockSpec(memory_space=pl.ANY)
         return pl.pallas_call(
-            functools.partial(grad_kernel, scale, half),
-            in_specs=[smem] + [vmem] * 12 + [anywhere] + [vmem] * 2,
-            out_specs=[vmem] * 3,
-            out_shape=[shape(8, pts), shape(32, pts), shape(40, tex // 2)],
+            kernel,
+            in_specs=[smem] + [vmem] * 9 + [anywhere, vmem] + [vmem] * half,
+            out_specs=[vmem] * 5,
+            out_shape=[shape(3, pts), shape(3, pts), shape(1, pts), shape(32, pts), shape(40, tex // 2)],
             scratch_shapes=[
                 pltpu.VMEM((6, PTS, 128), F32),
                 pltpu.VMEM((8, PTS), F32),
@@ -460,7 +493,7 @@
             name="grads" + str(half),
         )(
             theta,
-            *parts,
+            sums,
             albedo,
             observed,
             point_feat,
@@ -471,33 +504,34 @@
             env,
             spec,
             energy,
-            before,
+            *before,
         )
 
     place = lax.axis_index("pts")
     barrier = lax.optimization_barrier
-    _, gpf, other = grads(0, jnp.zeros((32, pts), F32))
+    *_, gpf, other = grads(0)
     other = swap(other, "pts", 1)
-    point_out, gpf, own = grads(1, gpf)
+    radiance, grad_albedo, grad_rough, gpf, own = grads(1, gpf)
 
     quad = tex // 8
     group = (place >> 1) & 3
-    mask = (8, 16, 24)
+    gpf_other = swap(gpf, "lts", 4)
     x = own + other
-    gpf_other = swap(gpf, "lts", 4)
     cut = [lax.dynamic_slice(x, (0, quad * (group ^ m)), (40, quad)) for m in range(4)]
-    gpf, *cut = barrier((gpf + gpf_other, *cut))
     got = [swap(cut[m], "pts", 2 * m) for m in (1, 2, 3)]
-    gpf_got = [swap(gpf, "lts", m) for m in (1, 2, 3)]
     x = (cut[0] + got[0]) + (got[1] + got[2])
-    gpf = (gpf + gpf_got[0]) + (gpf_got[1] + gpf_got[2])
-    x, gpf = barrier((x, gpf))
-    got = [swap(x, "pts", m) for m in mask]
-    x = (x + got[0]) + (got[1] + got[2])
+    for m, n in ((8, 1), (24, 2)):
+        x, gpf_other = barrier((x, gpf_other))
+        x_other = swap(x, "pts", m)
+        gpf = gpf + gpf_other
+        gpf_other = swap(gpf, "lts", n)
+        x = x + x_other
     light_step = x[32:35] * lax.rsqrt(x[35:38] + 1e-06 * points_all)
     total = jnp.sum(x[35:38], axis=0, keepdims=True)
     feat_step = x[0:32] * lax.rsqrt(total + 3e-06 * points_all)
     x = jnp.concatenate([feat_step, light_step], axis=0)
+    x, gpf_other = barrier((x, gpf_other))
+    gpf = gpf + gpf_other
     got = [x] + [swap(x, "pts", 2 * m) for m in (1, 2, 3)]
     pieces = []
     for j in range(4):
@@ -506,9 +540,8 @@
         pieces.append(jnp.where(k < 2, low, jnp.where(k == 2, got[2], got[3])))
     x = jnp.concatenate(pieces, axis=1)
     other = swap(x, "pts", 1)
-    low = (place & 1) == 0
-    x = jnp.concatenate([jnp.where(low, x, other), jnp.where(low, other, x)], axis=1)
-    return (point_out[0:3], point_out[3:6], point_out[6], gpf, x[32:35], x[0:32])
+    feat_step, light_step = join(x, other, tex)
+    return (radiance, grad_albedo, grad_rough.reshape(pts), gpf, light_step, feat_step)
 
 
 def solution(mesh):

time: 94.6 us -> 81.2 us (0.86)
  starting transfers between devices: 37.7 us -> 25.2 us
  blocking collectives: 0 us -> 11.1 us
  waiting for transfers between devices: 20.8 us -> 15.4 us
  other arithmetic: 4.81 us -> 0.83 us
  local copies, waits for them, and re-layouts: 1.84 us -> 0.03 us
    ppermute x19 -> x13, starting transfers between devices: 37.7 us -> 25.2 us  [swap(): return lax.ppermute(x, axis, [(i, i ^ bits) for i in range(n)])]
    all_to_all x0 -> x1, blocking collectives: none -> 11.1 us  [shards(): sums = lax.all_to_all(sums, 'lts', 0, 0)]
    ppermute x19 -> x13, waiting for transfers between devices: 20.8 us -> 15.4 us  [swap(): return lax.ppermute(x, axis, [(i, i ^ bits) for i in range(n)])]
    add x4 -> x5, other arithmetic: 2.13 us -> 0.65 us  [the longest x3 0.63 us: shards(): gpf = gpf + gpf_other]
    slice x2 -> x0, local copies, waits for them, and re-layouts: 1.16 us -> none  [the longest x1 0.6 us: shards(): point_out[3:6]]
    add x1, other arithmetic: 1.01 us -> 0.04 us  [shards(): x = own + other]
    pallas_call x2 -> x3, Pallas kernels: 13.9 us -> 13.6 us  [the longest x2 12.7 us: grads(): pl.pallas_call(kernel, in_specs=[smem] + [vmem] * 9 + [anywhere, vmem] +...]
  transfers between devices with their start and end apart: 19 -> 13, of which waited for: 10 -> 10; matrix products, arithmetic and copies ran while one was open for 3% -> 1% of each run, Pallas kernels for 7% -> 8%
where the time goes in v3:
time: 81.2 us; the launch traced here: 81 us
  Pallas kernels  27.6 us (34%)
  starting transfers between devices  25.2 us (31%)
  waiting for transfers between devices  15.4 us (19%)
  blocking collectives  11.1 us (14%)
  other arithmetic  0.83 us (1%)
    ppermute x13, starting transfers between devices, swap(): return lax.ppermute(x, axis, [(i, i ^ bits) for i in range(n)])  25.2 us
    ppermute x13, waiting for transfers between devices, swap(): return lax.ppermute(x, axis, [(i, i ^ bits) for i in range(n)])  15.4 us
    pallas_call x1, Pallas kernels, shards(): pl.pallas_call(shade_kernel, in_specs=[smem] + [vmem] * 9, out_specs=[pl....  14 us
    pallas_call x2, Pallas kernels, grads(): pl.pallas_call(kernel, in_specs=[smem] + [vmem] * 9 + [anywhere, vmem] +...  12.7 us
    all_to_all x1, blocking collectives, shards(): sums = lax.all_to_all(sums, 'lts', 0, 0)  11.1 us
  transfers between devices with their start and end apart: 13, of which 10 were waited for; matrix products, arithmetic and copies ran while one was open for 1% of the time, Pallas kernels for 8%

profile of v3, /device:TPU:1, one launch (start us, length us, event | category | flops | bytes accessed | tf_op | source)
XLA Modules:
  0.0 81.0 jit_solution(16672176221170317189)
XLA Ops:
  0.6 14.0 %shade.1 = (f32[16,256,256]{2,1,0:T(8,128)}, f32[8,9,256]{2,1,0:T(8,128)S(1)}, f32[3,4096]{1,0:T(4,128)S(1)}, f32[256,256]{1,0:T(8,128)S(1)}, bf16[256,96]{1,0:T(8,128)(2,1)S(1)}, /*index=5*/f32[256,128]{1,0:T(8,128)S(1)}) custom-call(f32[2,128]{1,0:T(2,128)} %constant.28.clone.theta_ref.refs_0_, f32[2,256]{1,0:T(2,128)} %constant.29.clone.phi_ref, ...), custom_call_target="tpu_custom_call" | custom-call | tf_op jit(solution)/shard_map/shade/pallas_call | solution.py:422
  14.7 11.1 %all_to_all.5.refs_1_ = f32[8,9,256]{2,1,0:T(8,128)S(1)} all-to-all(f32[8,9,256]{2,1,0:T(8,128)S(1)} %get-tuple-element.27), channel_id=1, replica_groups=mesh['pts'=32,'lts'=8] {'lts'}, dimensions={0} | all-to-all | bytes 147456 | tf_op jit(solution)/shard_map/all_to_all | solution.py:467
  25.8 6.4 %grads0.1 = (f32[3,256]{1,0:T(4,128)}, f32[3,256]{1,0:T(4,128)}, f32[1,256]{1,0:T(1,128)}, f32[32,256]{1,0:T(8,128)S(1)}, f32[40,2048]{1,0:T(8,128)S(1)}) custom-call(f32[2,128]{1,0:T(2,128)} %constant.28.clone.theta_ref.refs_0_, f32[8,9,256]{2,1,0:T(8,128)S(1)} %all_to_all.5.refs_1_, f32[3,256]{1,0:T(4,128)} %refs_2_.3, f32[3,256]{1,0:T(4,128)} %refs_3_.3, ...), custom_call_target="tpu_custom_call" | custom-call | tf_op jit(solution)/shard_map/grads0/pallas_call | solution.py:475
  32.2 2.2 %collective-permute-start = (f32[40,2048]{1,0:T(8,128)S(1)}, f32[40,2048]{1,0:T(8,128)S(1)}, u32[]{:S(2)}, u32[]{:S(2)}) collective-permute-start(f32[40,2048]{1,0:T(8,128)S(1)} %get-tuple-element.39), channel_id=1, source_target_pairs={{0,8},{8,0},{16,24},{24,16},{32,40},{40,32},{48,56},{56,48},{64,72... | collective-permute-start | bytes 983048 | tf_op jit(solution)/shard_map/ppermute | solution.py:464
  34.4 6.3 %grads1.1 = (f32[3,256]{1,0:T(4,128)}, f32[3,256]{1,0:T(4,128)}, f32[1,256]{1,0:T(1,128)}, f32[32,256]{1,0:T(8,128)S(1)}, f32[40,2048]{1,0:T(8,128)S(1)}) custom-call(f32[2,128]{1,0:T(2,128)} %constant.28.clone.theta_ref.refs_0_, f32[8,9,256]{2,1,0:T(8,128)S(1)} %all_to_all.5.refs_1_, f32[3,256]{1,0:T(4,128)} %refs_2_.3, f32[3,256]{1,0:T(4,128)} %refs_3_.3, ...), custom_call_target="tpu_custom_call" | custom-call | tf_op jit(solution)/shard_map/grads1/pallas_call | solution.py:475
  40.8 2.7 %collective-permute-start.1 = (f32[40,512]{1,0:T(8,128)S(1)}, f32[40,512]{1,0:T(8,128)S(1)}, u32[]{:S(2)}, u32[]{:S(2)}) collective-permute-start(f32[40,512]{1,0:T(8,128)S(1)} %get-tuple-element.52), channel_id=1, source_target_pairs={{0,16},{8,24},{16,0},{24,8},{32,48},{40,56},{48,32},{56,40},{64,80... | collective-permute-start | bytes 245768 | tf_op jit(solution)/shard_map/ppermute | solution.py:464
  43.5 1.6 %collective-permute-start.2 = (f32[40,512]{1,0:T(8,128)S(1)}, f32[40,512]{1,0:T(8,128)S(1)}, u32[]{:S(2)}, u32[]{:S(2)}) collective-permute-start(f32[40,512]{1,0:T(8,128)S(1)} %get-tuple-element.54), channel_id=1, source_target_pairs={{0,32},{8,40},{16,48},{24,56},{32,0},{40,8},{48,16},{56,24},{64,96... | collective-permute-start | bytes 245768 | tf_op jit(solution)/shard_map/ppermute | solution.py:464
  45.5 0.9 %collective-permute-done.1 = f32[40,512]{1,0:T(8,128)S(1)} collective-permute-done((f32[40,512]{1,0:T(8,128)S(1)}, f32[40,512]{1,0:T(8,128)S(1)}, u32[]{:S(2)}, u32[]{:S(2)}) %collective-permute-start.1) | collective-permute-done | bytes 81952 | tf_op jit(solution)/shard_map/ppermute | solution.py:464
  46.4 1.2 %collective-permute-done.2 = f32[40,512]{1,0:T(8,128)S(1)} collective-permute-done((f32[40,512]{1,0:T(8,128)S(1)}, f32[40,512]{1,0:T(8,128)S(1)}, u32[]{:S(2)}, u32[]{:S(2)}) %collective-permute-start.2) | collective-permute-done | bytes 81952 | tf_op jit(solution)/shard_map/ppermute | solution.py:464
  47.5 3.3 %collective-permute-done.3 = f32[40,512]{1,0:T(8,128)S(1)} collective-permute-done((f32[40,512]{1,0:T(8,128)S(1)}, f32[40,512]{1,0:T(8,128)S(1)}, u32[]{:S(2)}, u32[]{:S(2)}) %collective-permute-start.3) | collective-permute-done | bytes 81952 | tf_op jit(solution)/shard_map/ppermute | solution.py:464
  50.9 3.1 %collective-permute-start.5 = (f32[40,512]{1,0:T(8,128)S(1)}, f32[40,512]{1,0:T(8,128)S(1)}, u32[]{:S(2)}, u32[]{:S(2)}) collective-permute-start(f32[40,512]{1,0:T(8,128)S(1)} %add_add_fusion), channel_id=1, source_target_pairs={{0,64},{8,72},{16,80},{24,88},{32,96},{40,104},{48,112},{56,120},{... | collective-permute-start | bytes 245768 | tf_op jit(solution)/shard_map/ppermute | solution.py:464
  54.6 1.8 %collective-permute-done.5 = f32[40,512]{1,0:T(8,128)S(1)} collective-permute-done((f32[40,512]{1,0:T(8,128)S(1)}, f32[40,512]{1,0:T(8,128)S(1)}, u32[]{:S(2)}, u32[]{:S(2)}) %collective-permute-start.5) | collective-permute-done | bytes 81952 | tf_op jit(solution)/shard_map/ppermute | solution.py:464
  56.8 3.8 %collective-permute-start.7 = (f32[40,512]{1,0:T(8,128)S(1)}, f32[40,512]{1,0:T(8,128)S(1)}, u32[]{:S(2)}, u32[]{:S(2)}) collective-permute-start(f32[40,512]{1,0:T(8,128)S(1)} %add.65), channel_id=1, source_target_pairs={{0,192},{8,200},{16,208},{24,216},{32,224},{40,232},{48,240},{56,2... | collective-permute-start | bytes 245768 | tf_op jit(solution)/shard_map/ppermute | solution.py:464
  60.6 0.8 %collective-permute-start.8 = (f32[32,256]{1,0:T(8,128)S(1)}, f32[32,256]{1,0:T(8,128)S(1)}, u32[]{:S(2)}, u32[]{:S(2)}) collective-permute-start(f32[32,256]{1,0:T(8,128)S(1)} %add.66), channel_id=1, source_target_pairs={{0,2},{1,3},{2,0},{3,1},{4,6},{5,7},{6,4},{7,5},{8,10},{9,11},{10,... | collective-permute-start | bytes 98312 | tf_op jit(solution)/shard_map/ppermute | solution.py:464
  61.4 1.0 %collective-permute-done.7 = f32[40,512]{1,0:T(8,128)S(1)} collective-permute-done((f32[40,512]{1,0:T(8,128)S(1)}, f32[40,512]{1,0:T(8,128)S(1)}, u32[]{:S(2)}, u32[]{:S(2)}) %collective-permute-start.7) | collective-permute-done | bytes 81952 | tf_op jit(solution)/shard_map/ppermute | solution.py:464
  62.5 2.3 %collective-permute-done.8 = f32[32,256]{1,0:T(8,128)S(1)} collective-permute-done((f32[32,256]{1,0:T(8,128)S(1)}, f32[32,256]{1,0:T(8,128)S(1)}, u32[]{:S(2)}, u32[]{:S(2)}) %collective-permute-start.8) | collective-permute-done | bytes 32800 | tf_op jit(solution)/shard_map/ppermute | solution.py:464
  64.8 1.8 %collective-permute-start.10 = (f32[35,512]{1,0:T(8,128)S(1)}, f32[35,512]{1,0:T(8,128)S(1)}, u32[]{:S(2)}, u32[]{:S(2)}) collective-permute-start(f32[35,512]{1,0:T(8,128)S(1)} %pad_maximum_fusion.1), channel_id=1, source_target_pairs={{0,32},{8,40},{16,48},{24,56},{32,0},{40,8},{48,16},{56,24},{64,96... | collective-permute-start | bytes 215048 | tf_op jit(solution)/shard_map/ppermute | solution.py:464
  66.6 1.3 %collective-permute-start.11 = (f32[35,512]{1,0:T(8,128)S(1)}, f32[35,512]{1,0:T(8,128)S(1)}, u32[]{:S(2)}, u32[]{:S(2)}) collective-permute-start(f32[35,512]{1,0:T(8,128)S(1)} %pad_maximum_fusion.1), channel_id=1, source_target_pairs={{0,48},{8,56},{16,32},{24,40},{32,16},{40,24},{48,0},{56,8},{64,11... | collective-permute-start | bytes 215048 | tf_op jit(solution)/shard_map/ppermute | solution.py:464
  68.0 1.4 %collective-permute-start.9 = (f32[35,512]{1,0:T(8,128)S(1)}, f32[35,512]{1,0:T(8,128)S(1)}, u32[]{:S(2)}, u32[]{:S(2)}) collective-permute-start(f32[35,512]{1,0:T(8,128)S(1)} %pad_maximum_fusion.1), channel_id=1, source_target_pairs={{0,16},{8,24},{16,0},{24,8},{32,48},{40,56},{48,32},{56,40},{64,80... | collective-permute-start | bytes 215048 | tf_op jit(solution)/shard_map/ppermute | solution.py:464
  69.3 3.0 %collective-permute-done.11 = f32[35,512]{1,0:T(8,128)S(1)} collective-permute-done((f32[35,512]{1,0:T(8,128)S(1)}, f32[35,512]{1,0:T(8,128)S(1)}, u32[]{:S(2)}, u32[]{:S(2)}) %collective-permute-start.11) | collective-permute-done | bytes 71712 | tf_op jit(solution)/shard_map/ppermute | solution.py:464
  72.4 0.8 %collective-permute-done.9 = f32[35,512]{1,0:T(8,128)S(1)} collective-permute-done((f32[35,512]{1,0:T(8,128)S(1)}, f32[35,512]{1,0:T(8,128)S(1)}, u32[]{:S(2)}, u32[]{:S(2)}) %collective-permute-start.9) | collective-permute-done | bytes 71712 | tf_op jit(solution)/shard_map/ppermute | solution.py:464
  73.3 5.6 %collective-permute-start.12 = (f32[35,2048]{1,0:T(8,128)S(1)}, f32[35,2048]{1,0:T(8,128)S(1)}, u32[]{:S(2)}, u32[]{:S(2)}) collective-permute-start(f32[35,2048]{1,0:T(8,128)S(1)} %pad_maximum_fusion.own_ref), channel_id=1, source_target_pairs={{0,8},{8,0},{16,24},{24,16},{32,40},{40,32},{48,56},{56,48},{64,72... | collective-permute-start | bytes 860168 | tf_op jit(solution)/shard_map/ppermute | solution.py:464
  79.5 0.6 collective-permute-done.12.other_ref
  80.1 0.9 %join.1 = (f32[32,4096]{1,0:T(8,128)}, f32[3,4096]{1,0:T(4,128)}) custom-call(f32[35,2048]{1,0:T(8,128)S(1)} %pad_maximum_fusion.own_ref, f32[35,2048]{1,0:T(8,128)S(1)} %collective-permute-done.12.other_ref), custom_call_target="tpu_custom_call" | custom-call | tf_op jit(solution)/shard_map/join/pallas_call | solution.py:389
  (21 shorter events, 2.2 us)
Async XLA Ops:
  32.2 8.4 %collective-permute-start = (f32[40,2048]{1,0:T(8,128)S(1)}, f32[40,2048]{1,0:T(8,128)S(1)}, u32[]{:S(2)}, u32[]{:S(2)}) collective-permute-start(f32[40,2048]{1,0:T(8,128)S(1)} %get-tuple-element.39), channel_id=1, source_target_pairs={{0,8},{8,0},{16,24},{24,16},{32,40},{40,32},{48,56},{56,48},{64,72... | collective-permute-start | bytes 983048 | tf_op jit(solution)/shard_map/ppermute | solution.py:464
  40.8 5.6 %collective-permute-start.1 = (f32[40,512]{1,0:T(8,128)S(1)}, f32[40,512]{1,0:T(8,128)S(1)}, u32[]{:S(2)}, u32[]{:S(2)}) collective-permute-start(f32[40,512]{1,0:T(8,128)S(1)} %get-tuple-element.52), channel_id=1, source_target_pairs={{0,16},{8,24},{16,0},{24,8},{32,48},{40,56},{48,32},{56,40},{64,80... | collective-permute-start | bytes 245768 | tf_op jit(solution)/shard_map/ppermute | solution.py:464
  43.5 4.1 %collective-permute-start.2 = (f32[40,512]{1,0:T(8,128)S(1)}, f32[40,512]{1,0:T(8,128)S(1)}, u32[]{:S(2)}, u32[]{:S(2)}) collective-permute-start(f32[40,512]{1,0:T(8,128)S(1)} %get-tuple-element.54), channel_id=1, source_target_pairs={{0,32},{8,40},{16,48},{24,56},{32,0},{40,8},{48,16},{56,24},{64,96... | collective-permute-start | bytes 245768 | tf_op jit(solution)/shard_map/ppermute | solution.py:464
  45.1 5.8 %collective-permute-start.3 = (f32[40,512]{1,0:T(8,128)S(1)}, f32[40,512]{1,0:T(8,128)S(1)}, u32[]{:S(2)}, u32[]{:S(2)}) collective-permute-start(f32[40,512]{1,0:T(8,128)S(1)} %get-tuple-element.53), channel_id=1, source_target_pairs={{0,48},{8,56},{16,32},{24,40},{32,16},{40,24},{48,0},{56,8},{64,11... | collective-permute-start | bytes 245768 | tf_op jit(solution)/shard_map/ppermute | solution.py:464
  45.2 5.7 %collective-permute-start.4 = (f32[32,256]{1,0:T(8,128)S(1)}, f32[32,256]{1,0:T(8,128)S(1)}, u32[]{:S(2)}, u32[]{:S(2)}) collective-permute-start(f32[32,256]{1,0:T(8,128)S(1)} %get-tuple-element.37), channel_id=1, source_target_pairs={{0,4},{1,5},{2,6},{3,7},{4,0},{5,1},{6,2},{7,3},{8,12},{9,13},{10,... | collective-permute-start | bytes 98312 | tf_op jit(solution)/shard_map/ppermute | solution.py:464
  50.9 5.5 %collective-permute-start.5 = (f32[40,512]{1,0:T(8,128)S(1)}, f32[40,512]{1,0:T(8,128)S(1)}, u32[]{:S(2)}, u32[]{:S(2)}) collective-permute-start(f32[40,512]{1,0:T(8,128)S(1)} %add_add_fusion), channel_id=1, source_target_pairs={{0,64},{8,72},{16,80},{24,88},{32,96},{40,104},{48,112},{56,120},{... | collective-permute-start | bytes 245768 | tf_op jit(solution)/shard_map/ppermute | solution.py:464
  54.0 2.8 %collective-permute-start.6 = (f32[32,256]{1,0:T(8,128)S(1)}, f32[32,256]{1,0:T(8,128)S(1)}, u32[]{:S(2)}, u32[]{:S(2)}) collective-permute-start(f32[32,256]{1,0:T(8,128)S(1)} %add.64), channel_id=1, source_target_pairs={{0,1},{1,0},{2,3},{3,2},{4,5},{5,4},{6,7},{7,6},{8,9},{9,8},{10,11... | collective-permute-start | bytes 98312 | tf_op jit(solution)/shard_map/ppermute | solution.py:464
  56.8 5.7 %collective-permute-start.7 = (f32[40,512]{1,0:T(8,128)S(1)}, f32[40,512]{1,0:T(8,128)S(1)}, u32[]{:S(2)}, u32[]{:S(2)}) collective-permute-start(f32[40,512]{1,0:T(8,128)S(1)} %add.65), channel_id=1, source_target_pairs={{0,192},{8,200},{16,208},{24,216},{32,224},{40,232},{48,240},{56,2... | collective-permute-start | bytes 245768 | tf_op jit(solution)/shard_map/ppermute | solution.py:464
  60.6 4.3 %collective-permute-start.8 = (f32[32,256]{1,0:T(8,128)S(1)}, f32[32,256]{1,0:T(8,128)S(1)}, u32[]{:S(2)}, u32[]{:S(2)}) collective-permute-start(f32[32,256]{1,0:T(8,128)S(1)} %add.66), channel_id=1, source_target_pairs={{0,2},{1,3},{2,0},{3,1},{4,6},{5,7},{6,4},{7,5},{8,10},{9,11},{10,... | collective-permute-start | bytes 98312 | tf_op jit(solution)/shard_map/ppermute | solution.py:464
  64.8 4.5 %collective-permute-start.10 = (f32[35,512]{1,0:T(8,128)S(1)}, f32[35,512]{1,0:T(8,128)S(1)}, u32[]{:S(2)}, u32[]{:S(2)}) collective-permute-start(f32[35,512]{1,0:T(8,128)S(1)} %pad_maximum_fusion.1), channel_id=1, source_target_pairs={{0,32},{8,40},{16,48},{24,56},{32,0},{40,8},{48,16},{56,24},{64,96... | collective-permute-start | bytes 215048 | tf_op jit(solution)/shard_map/ppermute | solution.py:464
  66.6 5.7 %collective-permute-start.11 = (f32[35,512]{1,0:T(8,128)S(1)}, f32[35,512]{1,0:T(8,128)S(1)}, u32[]{:S(2)}, u32[]{:S(2)}) collective-permute-start(f32[35,512]{1,0:T(8,128)S(1)} %pad_maximum_fusion.1), channel_id=1, source_target_pairs={{0,48},{8,56},{16,32},{24,40},{32,16},{40,24},{48,0},{56,8},{64,11... | collective-permute-start | bytes 215048 | tf_op jit(solution)/shard_map/ppermute | solution.py:464
  68.0 5.2 %collective-permute-start.9 = (f32[35,512]{1,0:T(8,128)S(1)}, f32[35,512]{1,0:T(8,128)S(1)}, u32[]{:S(2)}, u32[]{:S(2)}) collective-permute-start(f32[35,512]{1,0:T(8,128)S(1)} %pad_maximum_fusion.1), channel_id=1, source_target_pairs={{0,16},{8,24},{16,0},{24,8},{32,48},{40,56},{48,32},{56,40},{64,80... | collective-permute-start | bytes 215048 | tf_op jit(solution)/shard_map/ppermute | solution.py:464
  73.3 6.8 %collective-permute-start.12 = (f32[35,2048]{1,0:T(8,128)S(1)}, f32[35,2048]{1,0:T(8,128)S(1)}, u32[]{:S(2)}, u32[]{:S(2)}) collective-permute-start(f32[35,2048]{1,0:T(8,128)S(1)} %pad_maximum_fusion.own_ref), channel_id=1, source_target_pairs={{0,8},{8,0},{16,24},{24,16},{32,40},{40,32},{48,56},{56,48},{64,72... | collective-permute-start | bytes 860168 | tf_op jit(solution)/shard_map/ppermute | solution.py:464

commit v4 on v3

--- a/solution.py
+++ b/solution.py
@@ -21,8 +21,12 @@
 
 PTS = 256
 BLK = 256
-CHUNK = 16
-UNROLL = 16
+CHUNK = 32
+GRADS_AT = (0, 1, 3, 4)
+SUMS_AT = (0, 1, 2, 3, 4, 5)
+SUM_ROWS = 128
+SCORE_AT = (6, 7)
+SCORE_ROWS = 128
 (NZ, VZ, NV0, AM1, KEEP, KOFF, C1, C0, YA, YD, YG, ALB) = range(12)
 NCONST = 14
 
@@ -45,7 +49,7 @@
 
 
 def fold(x):
-    return x[0:8] + x[8:16]
+    return (x[0:8] + x[8:16]) + (x[16:24] + x[24:32])
 
 
 def shade_kernel(
@@ -146,13 +150,13 @@
     def spec_copy(step):
         return pltpu.make_async_copy(spec_buf.at[step], spec_ref.at[step], sems.at[step])
 
-    def shade(step, score, mats):
+    def shade(step, score, mats, beside):
         sin_t = theta_ref[0, first + step]
         cos_t = theta_ref[1, first + step]
         light = light_of(step)
 
         def chunk(i, eng):
-            r0 = pl.multiple_of(i * CHUNK, CHUNK)
+            r0 = i * CHUNK
             rows = pl.ds(r0, CHUNK)
             c = [const[k, rows, :] for k in range(NCONST)]
             nz = c[NZ] * cos_t
@@ -190,8 +194,11 @@
                 acc_rad[k, rows, :] += rad[k]
             return tuple(eng)
 
-        zero = jnp.zeros((8, 128), F32)
-        eng = lax.fori_loop(0, PTS // CHUNK, chunk, (zero,) * 6, unroll=UNROLL)
+        eng = (jnp.zeros((8, 128), F32),) * 6
+        for i in range(PTS // CHUNK):
+            finish = beside(i)
+            eng = chunk(i, eng)
+            finish()
         for h in range(BLK // 128):
             for k in range(3):
                 lk = light[k : k + 1, 128 * h : 128 * h + 128]
@@ -199,26 +206,52 @@
 
         spec_copy(step).start()
 
-    def contract(step, mats):
+    def light_rows(step):
         light = light_of(step)
         l_hi = light.astype(BF16).astype(F32)
         ebuf[0:3, :] = l_hi
         ebuf[3:6, :] = light - l_hi
-        acc[...] += dot(ebuf[0:16, :].astype(BF16), mats[...], NT)
+        return ebuf[0:16, :].astype(BF16)
+
+    def beside(lmat, mats, score, nxt):
+        t_hi, t_lo = split(tfeat_ref[:, place(nxt)])
+        feats = jnp.concatenate([t_hi, t_hi, t_lo], axis=0)
+
+        def run(i):
+            if i in SUMS_AT:
+                part = pl.ds(SUMS_AT.index(i) * SUM_ROWS, SUM_ROWS)
+                x = dot(lmat, mats[part, :], NT)
+
+                def finish():
+                    acc[:, part] += x
+
+            elif i in SCORE_AT:
+                rows = pl.ds(SCORE_AT.index(i) * SCORE_ROWS, SCORE_ROWS)
+                x = dot(pfs[rows, :], feats, NN)
+
+                def finish():
+                    score[rows, :] = x
+
+            else:
+
+                def finish():
+                    pass
+
+            return finish
+
+        return run
 
     score_a[...] = score_tile(pfs, tfeat_ref[:, place(0)])
 
     @pl.loop(0, steps // 2)
     def pair(j):
         a = 2 * j
-        score_b[...] = score_tile(pfs, tfeat_ref[:, place(a + 1)])
-        shade(a, score_a, mats_a)
-        contract(jnp.maximum(a - 1, 0), mats_b)
-        score_a[...] = score_tile(pfs, tfeat_ref[:, place(jnp.minimum(a + 2, steps - 1))])
-        shade(a + 1, score_b, mats_b)
-        contract(a, mats_a)
-
-    contract(steps - 1, mats_b)
+        lmat = light_rows(jnp.maximum(a - 1, 0))
+        shade(a, score_a, mats_a, beside(lmat, mats_b, score_b, a + 1))
+        lmat = light_rows(a)
+        shade(a + 1, score_b, mats_b, beside(lmat, mats_a, score_a, jnp.minimum(a + 2, steps - 1)))
+
+    acc[...] += dot(light_rows(steps - 1), mats_b[...], NT)
     both = acc[0:3, :] + acc[3:6, :]
     rows = [both[:, 0:PTS], both[:, PTS : 2 * PTS] + both[:, 2 * PTS : 3 * PTS]]
     for k in range(3):
@@ -233,9 +266,132 @@
         spec_copy(step).wait()
 
 
+def grad_half(
+    base_tile,
+    steps,
+    spec_copy,
+    theta_ref,
+    pfs,
+    nz_ref,
+    azim_n,
+    tfeat_ref,
+    env_ref,
+    energy_ref,
+    out_ref,
+    const,
+    wmat,
+    score_a,
+    score_b,
+    d_a,
+    d_b,
+    acc,
+    spec_buf,
+):
+    first = lax.axis_index("lts") * (2 * steps) + base_tile
+    mine = pl.ds(pl.multiple_of(base_tile * BLK, BLK), steps * BLK)
+    out_ref[35:38, :] = energy_ref[:, mine]
+    out_ref[38:40, :] = jnp.zeros((2, steps * BLK), F32)
+    d_b[...] = jnp.zeros_like(d_b)
+
+    def place(step):
+        return pl.ds(pl.multiple_of(step * BLK, BLK), BLK)
+
+    def tfeat_of(step):
+        return tfeat_ref[:, place(base_tile + step)]
+
+    def combine(step, score, d, beside):
+        sin_t = theta_ref[0, first + step]
+        cos_t = theta_ref[1, first + step]
+        light = env_ref[:, place(base_tile + step)] * (sin_t * (0.25 * math.pi))
+        spec_copy(base_tile + step).wait()
+
+        def chunk(i, gain):
+            r0 = i * CHUNK
+            rows = pl.ds(r0, CHUNK)
+            c = [const[k, rows, :] for k in range(6)]
+            nz = nz_ref[rows, :] * cos_t
+            gain = list(gain)
+            for h in range(BLK // 128):
+                lanes = pl.ds(h * 128, 128)
+                tt = jnp.tanh(score[rows, lanes])
+                lit = jnp.maximum(azim_n[rows, lanes] * sin_t + nz, 0.0)
+                base = (1.0 + tt) * lit
+                spec = spec_buf[base_tile + step, rows, lanes]
+                total = None
+                for k in range(3):
+                    v = c[k] * base + c[3 + k] * spec
+                    gain[3 * h + k] += fold(v)
+                    lv = light[k : k + 1, 128 * h : 128 * h + 128] * v
+                    total = lv if total is None else total + lv
+                hi, lo = split(total * (1.0 - tt))
+                d[0, rows, lanes] = hi
+                d[1, rows, lanes] = lo
+            return tuple(gain)
+
+        gain = (jnp.zeros((8, 128), F32),) * 6
+        for i in range(PTS // CHUNK):
+            finish = beside(i)
+            gain = chunk(i, gain)
+            finish()
+        for h in range(BLK // 128):
+            for k in range(3):
+                lk = light[k : k + 1, 128 * h : 128 * h + 128]
+                out_ref[32 + k : 33 + k, pl.ds(pl.multiple_of(step * BLK + 128 * h, 128), 128)] = lk * jnp.sum(gain[3 * h + k], axis=0, keepdims=True)
+
+    def contract(step, d, i):
+        if i < 2:
+            cols = pl.ds(128 * i, 128)
+            x = dot(wmat[...], d[0, :, cols], NN)
+            y = dot(wmat[0:32, :], d[1, :, cols], NN)
+
+            def finish():
+                here = pl.ds(pl.multiple_of(step * BLK + 128 * i, 128), 128)
+                out_ref[0:32, here] = x[0:32] + x[32:64] + y
+
+        else:
+            t_hi, t_lo = split(tfeat_of(step))
+            rows = pl.ds(128 * (i - 2), 128)
+            x = dot(jnp.concatenate([t_hi, t_lo], axis=0), d[0, rows, :], NT)
+            y = dot(t_hi, d[1, rows, :], NT)
+
+            def finish():
+                acc[0:32, rows] += x[0:32] + x[32:64] + y
+
+        return finish
+
+    def beside(step, d, score, nxt):
+        t_hi, t_lo = split(tfeat_of(nxt))
+        feats = jnp.concatenate([t_hi, t_hi, t_lo], axis=0)
+
+        def run(i):
+            if i in GRADS_AT:
+                return contract(step, d, GRADS_AT.index(i))
+            if i in SCORE_AT:
+                rows = pl.ds(SCORE_AT.index(i) * SCORE_ROWS, SCORE_ROWS)
+                x = dot(pfs[rows, :], feats, NN)
+
+                def finish():
+                    score[rows, :] = x
+
+                return finish
+            return lambda: None
+
+        return run
+
+    score_a[...] = score_tile(pfs, tfeat_of(0))
+
+    @pl.loop(0, steps // 2)
+    def pair(j):
+        a = 2 * j
+        combine(a, score_a, d_a, beside(jnp.maximum(a - 1, 0), d_b, score_b, a + 1))
+        combine(a + 1, score_b, d_b, beside(a, d_a, score_a, jnp.minimum(a + 2, steps - 1)))
+
+    for i in range(4):
+        contract(steps - 1, d_b, i)()
+
+
 def grad_kernel(
     scale,
-    half,
     theta_ref,
     sums_ref,
     albedo_ref,
@@ -248,12 +404,12 @@
     env_ref,
     spec_ref,
     energy_ref,
-    before_ref,
     rad_ref,
     galb_ref,
     grough_ref,
     gpf_ref,
-    out_ref,
+    other_ref,
+    own_ref,
     const,
     rbuf,
     wmat,
@@ -268,8 +424,6 @@
     tiles = tfeat_ref.shape[1] // BLK
     steps = tiles // 2
     core = lax.axis_index("pts") % 2
-    base_tile = (core if half else 1 - core) * steps
-    first = lax.axis_index("lts") * tiles + base_tile
     half_root = 0.5 / math.sqrt(pfeat_ref.shape[0])
 
     def prologue():
@@ -293,87 +447,22 @@
         wmat[32:64, :] = lo
         acc[...] = jnp.zeros_like(acc)
 
-    def spec_copy(step):
-        return pltpu.make_async_copy(
-            spec_ref.at[base_tile + step], spec_buf.at[step], sems.at[step]
+    def spec_copy(tile):
+        return pltpu.make_async_copy(spec_ref.at[tile], spec_buf.at[tile], sems.at[tile])
+
+    @pl.loop(0, tiles)
+    def fetch(step):
+        spec_copy(lax.rem(step + (1 - core) * steps, tiles)).start()
+
+    prologue()
+    for part, out_ref in enumerate((other_ref, own_ref)):
+        grad_half(
+            (core if part else 1 - core) * steps, steps, spec_copy, theta_ref, pfs, nz_ref, azim_n,
+            tfeat_ref, env_ref, energy_ref, out_ref, const, wmat, score_a, score_b, d_a, d_b, acc,
+            spec_buf,
         )
-
-    @pl.loop(0, steps)
-    def fetch(step):
-        spec_copy(step).start()
-
-    prologue()
-    mine = pl.ds(pl.multiple_of(base_tile * BLK, BLK), steps * BLK)
-    out_ref[35:38, :] = energy_ref[:, mine]
-    out_ref[38:40, :] = jnp.zeros((2, steps * BLK), F32)
-    d_b[...] = jnp.zeros_like(d_b)
-
-    def place(step):
-        return pl.ds(pl.multiple_of(step * BLK, BLK), BLK)
-
-    def tfeat_of(step):
-        return tfeat_ref[:, place(base_tile + step)]
-
-    def combine(step, score, d):
-        sin_t = theta_ref[0, first + step]
-        cos_t = theta_ref[1, first + step]
-        light = env_ref[:, place(base_tile + step)] * (sin_t * (0.25 * math.pi))
-        spec_copy(step).wait()
-
-        def chunk(i, gain):
-            r0 = pl.multiple_of(i * CHUNK, CHUNK)
-            rows = pl.ds(r0, CHUNK)
-            c = [const[k, rows, :] for k in range(6)]
-            nz = nz_ref[rows, :] * cos_t
-            gain = list(gain)
-            for h in range(BLK // 128):
-                lanes = pl.ds(h * 128, 128)
-                tt = jnp.tanh(score[rows, lanes])
-                lit = jnp.maximum(azim_n[rows, lanes] * sin_t + nz, 0.0)
-                base = (1.0 + tt) * lit
-                spec = spec_buf[step, rows, lanes]
-                total = None
-                for k in range(3):
-                    v = c[k] * base + c[3 + k] * spec
-                    gain[3 * h + k] += fold(v)
-                    lv = light[k : k + 1, 128 * h : 128 * h + 128] * v
-                    total = lv if total is None else total + lv
-                hi, lo = split(total * (1.0 - tt))
-                d[0, rows, lanes] = hi
-                d[1, rows, lanes] = lo
-            return tuple(gain)
-
-        zero = jnp.zeros((8, 128), F32)
-        gain = lax.fori_loop(0, PTS // CHUNK, chunk, (zero,) * 6, unroll=UNROLL)
-        for h in range(BLK // 128):
-            for k in range(3):
-                lk = light[k : k + 1, 128 * h : 128 * h + 128]
-                out_ref[32 + k : 33 + k, pl.ds(pl.multiple_of(step * BLK + 128 * h, 128), 128)] = lk * jnp.sum(gain[3 * h + k], axis=0, keepdims=True)
-
-    def contract(step, d):
-        dh = d[0]
-        dl = d[1]
-        x = dot(wmat[...], dh, NN)
-        out_ref[0:32, place(step)] = x[0:32] + x[32:64] + dot(wmat[0:32, :], dl, NN)
-        t_hi, t_lo = split(tfeat_of(step))
-        acc[...] += dot(jnp.concatenate([t_hi, t_lo], axis=0), dh, NT)
-        acc[0:32, :] += dot(t_hi, dl, NT)
-
-    score_a[...] = score_tile(pfs, tfeat_of(0))
-
-    @pl.loop(0, steps // 2)
-    def pair(j):
-        a = 2 * j
-        score_b[...] = score_tile(pfs, tfeat_of(a + 1))
-        combine(a, score_a, d_a)
-        contract(jnp.maximum(a - 1, 0), d_b)
-        score_a[...] = score_tile(pfs, tfeat_of(jnp.minimum(a + 2, steps - 1)))
-        combine(a + 1, score_b, d_b)
-        contract(a, d_a)
-
-    contract(steps - 1, d_b)
-    gpf = (scale * half_root) * (acc[0:32, :] + acc[32:64, :])
-    gpf_ref[...] = gpf + before_ref[...] if half else gpf
+    gpf = (scale * half_root) * acc[...]
+    gpf_ref[...] = gpf
 
 
 def join_kernel(own_ref, other_ref, feat_ref, light_ref):
@@ -466,17 +555,14 @@
     spec = hbm(spec)
     sums = lax.all_to_all(sums, "lts", 0, 0)
 
-    def grads(half, *before):
-        def kernel(*refs):
-            refs = refs if half else refs[:12] + (None,) + refs[12:]
-            grad_kernel(scale, half, *refs)
-
+    def grads():
         anywhere = pl.BlockSpec(memory_space=pl.ANY)
         return pl.pallas_call(
-            kernel,
-            in_specs=[smem] + [vmem] * 9 + [anywhere, vmem] + [vmem] * half,
-            out_specs=[vmem] * 5,
-            out_shape=[shape(3, pts), shape(3, pts), shape(1, pts), shape(32, pts), shape(40, tex // 2)],
+            functools.partial(grad_kernel, scale),
+            in_specs=[smem] + [vmem] * 9 + [anywhere, vmem],
+            out_specs=[vmem] * 6,
+            out_shape=[shape(3, pts), shape(3, pts), shape(1, pts), shape(32, pts)]
+            + [shape(40, tex // 2)] * 2,
             scratch_shapes=[
                 pltpu.VMEM((6, PTS, 128), F32),
                 pltpu.VMEM((8, PTS), F32),
@@ -485,12 +571,12 @@
                 pltpu.VMEM((PTS, BLK), F32),
                 pltpu.VMEM((2, PTS, BLK), BF16),
                 pltpu.VMEM((2, PTS, BLK), BF16),
-                pltpu.VMEM((64, PTS), F32),
-                pltpu.VMEM((steps // 2, PTS, BLK), F32),
-                pltpu.SemaphoreType.DMA((steps // 2,)),
+                pltpu.VMEM((32, PTS), F32),
+                pltpu.VMEM((steps, PTS, BLK), F32),
+                pltpu.SemaphoreType.DMA((steps,)),
             ],
             compiler_params=params,
-            name="grads" + str(half),
+            name="grads",
         )(
             theta,
             sums,
@@ -504,14 +590,12 @@
             env,
             spec,
             energy,
-            *before,
         )
 
     place = lax.axis_index("pts")
     barrier = lax.optimization_barrier
-    *_, gpf, other = grads(0)
+    radiance, grad_albedo, grad_rough, gpf, other, own = grads()
     other = swap(other, "pts", 1)
-    radiance, grad_albedo, grad_rough, gpf, own = grads(1, gpf)
 
     quad = tex // 8
     group = (place >> 1) & 3
@@ -520,18 +604,18 @@
     cut = [lax.dynamic_slice(x, (0, quad * (group ^ m)), (40, quad)) for m in range(4)]
     got = [swap(cut[m], "pts", 2 * m) for m in (1, 2, 3)]
     x = (cut[0] + got[0]) + (got[1] + got[2])
-    for m, n in ((8, 1), (24, 2)):
-        x, gpf_other = barrier((x, gpf_other))
-        x_other = swap(x, "pts", m)
-        gpf = gpf + gpf_other
-        gpf_other = swap(gpf, "lts", n)
-        x = x + x_other
+    x, gpf_other = barrier((x, gpf_other))
+    got = [swap(x, "pts", m) for m in (8, 16, 24)]
+    gpf = gpf + gpf_other
+    gpf_other = swap(gpf, "lts", 1)
+    x = (x + got[0]) + (got[1] + got[2])
     light_step = x[32:35] * lax.rsqrt(x[35:38] + 1e-06 * points_all)
     total = jnp.sum(x[35:38], axis=0, keepdims=True)
     feat_step = x[0:32] * lax.rsqrt(total + 3e-06 * points_all)
     x = jnp.concatenate([feat_step, light_step], axis=0)
     x, gpf_other = barrier((x, gpf_other))
     gpf = gpf + gpf_other
+    gpf_other = swap(gpf, "lts", 2)
     got = [x] + [swap(x, "pts", 2 * m) for m in (1, 2, 3)]
     pieces = []
     for j in range(4):
@@ -539,7 +623,9 @@
         low = jnp.where(k == 0, got[0], got[1])
         pieces.append(jnp.where(k < 2, low, jnp.where(k == 2, got[2], got[3])))
     x = jnp.concatenate(pieces, axis=1)
+    x, gpf_other = barrier((x, gpf_other))
     other = swap(x, "pts", 1)
+    gpf = gpf + gpf_other
     feat_step, light_step = join(x, other, tex)
     return (radiance, grad_albedo, grad_rough.reshape(pts), gpf, light_step, feat_step)
 

time: 81.2 us -> 77.9 us (0.959)
  Pallas kernels: 27.6 us -> 24 us
  waiting for transfers between devices: 15.4 us -> 16.7 us
  starting transfers between devices: 25.2 us -> 24.3 us
    pallas_call x2 -> x1, Pallas kernels: 12.7 us -> 10 us  [grads(): pl.pallas_call(functools.partial(grad_kernel, scale), in_specs=[smem] + [...]
    ppermute x13 -> x14, waiting for transfers between devices: 15.4 us -> 16.7 us  [swap(): return lax.ppermute(x, axis, [(i, i ^ bits) for i in range(n)])]
    pallas_call x1, Pallas kernels: 14 us -> 13.1 us  [shards(): pl.pallas_call(shade_kernel, in_specs=[smem] + [vmem] * 9, out_specs=[pl....]
    ppermute x13 -> x14, starting transfers between devices: 25.2 us -> 24.3 us  [swap(): return lax.ppermute(x, axis, [(i, i ^ bits) for i in range(n)])]
  transfers between devices with their start and end apart: 13 -> 14, of which waited for: 10 -> 10; matrix products, arithmetic and copies ran while one was open for 1% -> 1% of each run, Pallas kernels for 8% -> 0%
where the time goes in v4:
time: 77.9 us; the launch traced here: 77.7 us
  starting transfers between devices  24.3 us (31%)
  Pallas kernels  24 us (31%)
  waiting for transfers between devices  16.7 us (21%)
  blocking collectives  11.1 us (14%)
  other arithmetic  0.83 us (1%)
    ppermute x14, starting transfers between devices, swap(): return lax.ppermute(x, axis, [(i, i ^ bits) for i in range(n)])  24.3 us
    ppermute x14, waiting for transfers between devices, swap(): return lax.ppermute(x, axis, [(i, i ^ bits) for i in range(n)])  16.7 us
    pallas_call x1, Pallas kernels, shards(): pl.pallas_call(shade_kernel, in_specs=[smem] + [vmem] * 9, out_specs=[pl....  13.1 us
    all_to_all x1, blocking collectives, shards(): sums = lax.all_to_all(sums, 'lts', 0, 0)  11.1 us
    pallas_call x1, Pallas kernels, grads(): pl.pallas_call(functools.partial(grad_kernel, scale), in_specs=[smem] + [...  10 us
  transfers between devices with their start and end apart: 14, of which 10 were waited for; matrix products, arithmetic and copies ran while one was open for 1% of the time, Pallas kernels for 0%

profile of v4, /device:TPU:1, one launch (start us, length us, event | category | flops | bytes accessed | tf_op | source)
XLA Modules:
  0.0 77.7 jit_solution(2265537812321278982)
XLA Ops:
  0.6 13.1 %shade.1 = (f32[16,256,256]{2,1,0:T(8,128)}, f32[8,9,256]{2,1,0:T(8,128)S(1)}, f32[3,4096]{1,0:T(4,128)S(1)}, f32[256,256]{1,0:T(8,128)S(1)}, bf16[256,96]{1,0:T(8,128)(2,1)S(1)}, /*index=5*/f32[256,128]{1,0:T(8,128)S(1)}) custom-call(f32[2,128]{1,0:T(2,128)} %constant.28.clone.theta_ref, f32[2,256]{1,0:T(2,128)} %constant.29.clone.phi_ref, ...), custom_call_target="tpu_custom_call" | custom-call | tf_op jit(solution)/shard_map/shade/pallas_call | solution.py:511
  13.8 11.1 %all_to_all.5.sums_ref = f32[8,9,256]{2,1,0:T(8,128)S(1)} all-to-all(f32[8,9,256]{2,1,0:T(8,128)S(1)} %get-tuple-element.26), channel_id=1, replica_groups=mesh['pts'=32,'lts'=8] {'lts'}, dimensions={0} | all-to-all | bytes 147456 | tf_op jit(solution)/shard_map/all_to_all | solution.py:556
  24.9 10.0 %grads.1 = (f32[3,256]{1,0:T(4,128)}, f32[3,256]{1,0:T(4,128)}, f32[1,256]{1,0:T(1,128)}, f32[32,256]{1,0:T(8,128)S(1)}, f32[40,2048]{1,0:T(8,128)S(1)}, /*index=5*/f32[40,2048]{1,0:T(8,128)S(1)}) custom-call(f32[2,128]{1,0:T(2,128)} %constant.28.clone.theta_ref, f32[8,9,256]{2,1,0:T(8,128)S(1)} %all_to_all.5.sums_ref, f32[3,256]{1,0:T(4,128)} %albedo_ref.3, ...), custom_call_target="tpu_custom_call" | custom-call | tf_op jit(solution)/shard_map/grads/pallas_call | solution.py:560
  34.9 2.2 %collective-permute-start = (f32[40,2048]{1,0:T(8,128)S(1)}, f32[40,2048]{1,0:T(8,128)S(1)}, u32[]{:S(2)}, u32[]{:S(2)}) collective-permute-start(f32[40,2048]{1,0:T(8,128)S(1)} %get-tuple-element.37), channel_id=1, source_target_pairs={{0,8},{8,0},{16,24},{24,16},{32,40},{40,32},{48,56},{56,48},{64,72... | collective-permute-start | bytes 983048 | tf_op jit(solution)/shard_map/ppermute | solution.py:553
  37.1 1.3 %collective-permute-done = f32[40,2048]{1,0:T(8,128)S(1)} collective-permute-done((f32[40,2048]{1,0:T(8,128)S(1)}, f32[40,2048]{1,0:T(8,128)S(1)}, u32[]{:S(2)}, u32[]{:S(2)}) %collective-permute-start) | collective-permute-done | bytes 327712 | tf_op jit(solution)/shard_map/ppermute | solution.py:553
  38.4 2.7 %collective-permute-start.1 = (f32[40,512]{1,0:T(8,128)S(1)}, f32[40,512]{1,0:T(8,128)S(1)}, u32[]{:S(2)}, u32[]{:S(2)}) collective-permute-start(f32[40,512]{1,0:T(8,128)S(1)} %get-tuple-element.50), channel_id=1, source_target_pairs={{0,16},{8,24},{16,0},{24,8},{32,48},{40,56},{48,32},{56,40},{64,80... | collective-permute-start | bytes 245768 | tf_op jit(solution)/shard_map/ppermute | solution.py:553
  41.1 1.6 %collective-permute-start.2 = (f32[40,512]{1,0:T(8,128)S(1)}, f32[40,512]{1,0:T(8,128)S(1)}, u32[]{:S(2)}, u32[]{:S(2)}) collective-permute-start(f32[40,512]{1,0:T(8,128)S(1)} %get-tuple-element.52), channel_id=1, source_target_pairs={{0,32},{8,40},{16,48},{24,56},{32,0},{40,8},{48,16},{56,24},{64,96... | collective-permute-start | bytes 245768 | tf_op jit(solution)/shard_map/ppermute | solution.py:553
  43.6 0.9 %collective-permute-done.2 = f32[40,512]{1,0:T(8,128)S(1)} collective-permute-done((f32[40,512]{1,0:T(8,128)S(1)}, f32[40,512]{1,0:T(8,128)S(1)}, u32[]{:S(2)}, u32[]{:S(2)}) %collective-permute-start.2) | collective-permute-done | bytes 81952 | tf_op jit(solution)/shard_map/ppermute | solution.py:553
  44.6 3.9 %collective-permute-done.3 = f32[40,512]{1,0:T(8,128)S(1)} collective-permute-done((f32[40,512]{1,0:T(8,128)S(1)}, f32[40,512]{1,0:T(8,128)S(1)}, u32[]{:S(2)}, u32[]{:S(2)}) %collective-permute-start.3) | collective-permute-done | bytes 81952 | tf_op jit(solution)/shard_map/ppermute | solution.py:553
  48.5 3.1 %collective-permute-start.5 = (f32[40,512]{1,0:T(8,128)S(1)}, f32[40,512]{1,0:T(8,128)S(1)}, u32[]{:S(2)}, u32[]{:S(2)}) collective-permute-start(f32[40,512]{1,0:T(8,128)S(1)} %add_add_fusion.1), channel_id=1, source_target_pairs={{0,64},{8,72},{16,80},{24,88},{32,96},{40,104},{48,112},{56,120},{... | collective-permute-start | bytes 245768 | tf_op jit(solution)/shard_map/ppermute | solution.py:553
  51.6 4.3 %collective-permute-start.6 = (f32[40,512]{1,0:T(8,128)S(1)}, f32[40,512]{1,0:T(8,128)S(1)}, u32[]{:S(2)}, u32[]{:S(2)}) collective-permute-start(f32[40,512]{1,0:T(8,128)S(1)} %add_add_fusion.1), channel_id=1, source_target_pairs={{0,128},{8,136},{16,144},{24,152},{32,160},{40,168},{48,176},{56,1... | collective-permute-start | bytes 245768 | tf_op jit(solution)/shard_map/ppermute | solution.py:553
  55.9 0.7 collective-permute-start.8
  56.5 2.3 %collective-permute-done.6 = f32[40,512]{1,0:T(8,128)S(1)} collective-permute-done((f32[40,512]{1,0:T(8,128)S(1)}, f32[40,512]{1,0:T(8,128)S(1)}, u32[]{:S(2)}, u32[]{:S(2)}) %collective-permute-start.6) | collective-permute-done | bytes 81952 | tf_op jit(solution)/shard_map/ppermute | solution.py:553
  58.8 3.8 %collective-permute-done.7 = f32[40,512]{1,0:T(8,128)S(1)} collective-permute-done((f32[40,512]{1,0:T(8,128)S(1)}, f32[40,512]{1,0:T(8,128)S(1)}, u32[]{:S(2)}, u32[]{:S(2)}) %collective-permute-start.7) | collective-permute-done | bytes 81952 | tf_op jit(solution)/shard_map/ppermute | solution.py:553
  62.7 1.5 %collective-permute-start.10 = (f32[35,512]{1,0:T(8,128)S(1)}, f32[35,512]{1,0:T(8,128)S(1)}, u32[]{:S(2)}, u32[]{:S(2)}) collective-permute-start(f32[35,512]{1,0:T(8,128)S(1)} %pad_maximum_fusion.1), channel_id=1, source_target_pairs={{0,32},{8,40},{16,48},{24,56},{32,0},{40,8},{48,16},{56,24},{64,96... | collective-permute-start | bytes 215048 | tf_op jit(solution)/shard_map/ppermute | solution.py:553
  64.3 0.6 collective-permute-start.11
  64.9 2.2 %collective-permute-start.9 = (f32[35,512]{1,0:T(8,128)S(1)}, f32[35,512]{1,0:T(8,128)S(1)}, u32[]{:S(2)}, u32[]{:S(2)}) collective-permute-start(f32[35,512]{1,0:T(8,128)S(1)} %pad_maximum_fusion.1), channel_id=1, source_target_pairs={{0,16},{8,24},{16,0},{24,8},{32,48},{40,56},{48,32},{56,40},{64,80... | collective-permute-start | bytes 215048 | tf_op jit(solution)/shard_map/ppermute | solution.py:553
  67.1 0.8 %collective-permute-start.12 = (f32[32,256]{1,0:T(8,128)S(1)}, f32[32,256]{1,0:T(8,128)S(1)}, u32[]{:S(2)}, u32[]{:S(2)}) collective-permute-start(f32[32,256]{1,0:T(8,128)S(1)} %add.75), channel_id=1, source_target_pairs={{0,2},{1,3},{2,0},{3,1},{4,6},{5,7},{6,4},{7,5},{8,10},{9,11},{10,... | collective-permute-start | bytes 98312 | tf_op jit(solution)/shard_map/ppermute | solution.py:553
  67.9 2.4 %collective-permute-done.11 = f32[35,512]{1,0:T(8,128)S(1)} collective-permute-done((f32[35,512]{1,0:T(8,128)S(1)}, f32[35,512]{1,0:T(8,128)S(1)}, u32[]{:S(2)}, u32[]{:S(2)}) %collective-permute-start.11) | collective-permute-done | bytes 71712 | tf_op jit(solution)/shard_map/ppermute | solution.py:553
  70.7 0.7 collective-permute-done.12
  71.4 4.3 %collective-permute-start.13 = (f32[35,2048]{1,0:T(8,128)S(1)}, f32[35,2048]{1,0:T(8,128)S(1)}, u32[]{:S(2)}, u32[]{:S(2)}) collective-permute-start(f32[35,2048]{1,0:T(8,128)S(1)} %pad_maximum_fusion.own_ref), channel_id=1, source_target_pairs={{0,8},{8,0},{16,24},{24,16},{32,40},{40,32},{48,56},{56,48},{64,72... | collective-permute-start | bytes 860168 | tf_op jit(solution)/shard_map/ppermute | solution.py:553
  75.6 0.6 add.76
  76.2 0.6 collective-permute-done.13.other_ref
  76.9 0.9 %join.1 = (f32[32,4096]{1,0:T(8,128)}, f32[3,4096]{1,0:T(4,128)}) custom-call(f32[35,2048]{1,0:T(8,128)S(1)} %pad_maximum_fusion.own_ref, f32[35,2048]{1,0:T(8,128)S(1)} %collective-permute-done.13.other_ref), custom_call_target="tpu_custom_call" | custom-call | tf_op jit(solution)/shard_map/join/pallas_call | solution.py:478
  (21 shorter events, 1.4 us)
Async XLA Ops:
  34.9 3.4 %collective-permute-start = (f32[40,2048]{1,0:T(8,128)S(1)}, f32[40,2048]{1,0:T(8,128)S(1)}, u32[]{:S(2)}, u32[]{:S(2)}) collective-permute-start(f32[40,2048]{1,0:T(8,128)S(1)} %get-tuple-element.37), channel_id=1, source_target_pairs={{0,8},{8,0},{16,24},{24,16},{32,40},{40,32},{48,56},{56,48},{64,72... | collective-permute-start | bytes 983048 | tf_op jit(solution)/shard_map/ppermute | solution.py:553
  38.4 5.2 %collective-permute-start.1 = (f32[40,512]{1,0:T(8,128)S(1)}, f32[40,512]{1,0:T(8,128)S(1)}, u32[]{:S(2)}, u32[]{:S(2)}) collective-permute-start(f32[40,512]{1,0:T(8,128)S(1)} %get-tuple-element.50), channel_id=1, source_target_pairs={{0,16},{8,24},{16,0},{24,8},{32,48},{40,56},{48,32},{56,40},{64,80... | collective-permute-start | bytes 245768 | tf_op jit(solution)/shard_map/ppermute | solution.py:553
  41.1 3.5 %collective-permute-start.2 = (f32[40,512]{1,0:T(8,128)S(1)}, f32[40,512]{1,0:T(8,128)S(1)}, u32[]{:S(2)}, u32[]{:S(2)}) collective-permute-start(f32[40,512]{1,0:T(8,128)S(1)} %get-tuple-element.52), channel_id=1, source_target_pairs={{0,32},{8,40},{16,48},{24,56},{32,0},{40,8},{48,16},{56,24},{64,96... | collective-permute-start | bytes 245768 | tf_op jit(solution)/shard_map/ppermute | solution.py:553
  42.7 5.7 %collective-permute-start.3 = (f32[40,512]{1,0:T(8,128)S(1)}, f32[40,512]{1,0:T(8,128)S(1)}, u32[]{:S(2)}, u32[]{:S(2)}) collective-permute-start(f32[40,512]{1,0:T(8,128)S(1)} %get-tuple-element.51), channel_id=1, source_target_pairs={{0,48},{8,56},{16,32},{24,40},{32,16},{40,24},{48,0},{56,8},{64,11... | collective-permute-start | bytes 245768 | tf_op jit(solution)/shard_map/ppermute | solution.py:553
  42.8 5.7 %collective-permute-start.4 = (f32[32,256]{1,0:T(8,128)S(1)}, f32[32,256]{1,0:T(8,128)S(1)}, u32[]{:S(2)}, u32[]{:S(2)}) collective-permute-start(f32[32,256]{1,0:T(8,128)S(1)} %get-tuple-element.35), channel_id=1, source_target_pairs={{0,4},{1,5},{2,6},{3,7},{4,0},{5,1},{6,2},{7,3},{8,12},{9,13},{10,... | collective-permute-start | bytes 98312 | tf_op jit(solution)/shard_map/ppermute | solution.py:553
  48.5 8.0 %collective-permute-start.5 = (f32[40,512]{1,0:T(8,128)S(1)}, f32[40,512]{1,0:T(8,128)S(1)}, u32[]{:S(2)}, u32[]{:S(2)}) collective-permute-start(f32[40,512]{1,0:T(8,128)S(1)} %add_add_fusion.1), channel_id=1, source_target_pairs={{0,64},{8,72},{16,80},{24,88},{32,96},{40,104},{48,112},{56,120},{... | collective-permute-start | bytes 245768 | tf_op jit(solution)/shard_map/ppermute | solution.py:553
  51.6 7.2 %collective-permute-start.6 = (f32[40,512]{1,0:T(8,128)S(1)}, f32[40,512]{1,0:T(8,128)S(1)}, u32[]{:S(2)}, u32[]{:S(2)}) collective-permute-start(f32[40,512]{1,0:T(8,128)S(1)} %add_add_fusion.1), channel_id=1, source_target_pairs={{0,128},{8,136},{16,144},{24,152},{32,160},{40,168},{48,176},{56,1... | collective-permute-start | bytes 245768 | tf_op jit(solution)/shard_map/ppermute | solution.py:553
  55.9 6.8 %collective-permute-start.7 = (f32[40,512]{1,0:T(8,128)S(1)}, f32[40,512]{1,0:T(8,128)S(1)}, u32[]{:S(2)}, u32[]{:S(2)}) collective-permute-start(f32[40,512]{1,0:T(8,128)S(1)} %add_add_fusion.1), channel_id=1, source_target_pairs={{0,192},{8,200},{16,208},{24,216},{32,224},{40,232},{48,240},{56,2... | collective-permute-start | bytes 245768 | tf_op jit(solution)/shard_map/ppermute | solution.py:553
  55.9 6.9 %collective-permute-start.8 = (f32[32,256]{1,0:T(8,128)S(1)}, f32[32,256]{1,0:T(8,128)S(1)}, u32[]{:S(2)}, u32[]{:S(2)}) collective-permute-start(f32[32,256]{1,0:T(8,128)S(1)} %add.67), channel_id=1, source_target_pairs={{0,1},{1,0},{2,3},{3,2},{4,5},{5,4},{6,7},{7,6},{8,9},{9,8},{10,11... | collective-permute-start | bytes 98312 | tf_op jit(solution)/shard_map/ppermute | solution.py:553
  62.7 5.2 %collective-permute-start.10 = (f32[35,512]{1,0:T(8,128)S(1)}, f32[35,512]{1,0:T(8,128)S(1)}, u32[]{:S(2)}, u32[]{:S(2)}) collective-permute-start(f32[35,512]{1,0:T(8,128)S(1)} %pad_maximum_fusion.1), channel_id=1, source_target_pairs={{0,32},{8,40},{16,48},{24,56},{32,0},{40,8},{48,16},{56,24},{64,96... | collective-permute-start | bytes 215048 | tf_op jit(solution)/shard_map/ppermute | solution.py:553
  64.3 6.0 %collective-permute-start.11 = (f32[35,512]{1,0:T(8,128)S(1)}, f32[35,512]{1,0:T(8,128)S(1)}, u32[]{:S(2)}, u32[]{:S(2)}) collective-permute-start(f32[35,512]{1,0:T(8,128)S(1)} %pad_maximum_fusion.1), channel_id=1, source_target_pairs={{0,48},{8,56},{16,32},{24,40},{32,16},{40,24},{48,0},{56,8},{64,11... | collective-permute-start | bytes 215048 | tf_op jit(solution)/shard_map/ppermute | solution.py:553
  64.9 5.7 %collective-permute-start.9 = (f32[35,512]{1,0:T(8,128)S(1)}, f32[35,512]{1,0:T(8,128)S(1)}, u32[]{:S(2)}, u32[]{:S(2)}) collective-permute-start(f32[35,512]{1,0:T(8,128)S(1)} %pad_maximum_fusion.1), channel_id=1, source_target_pairs={{0,16},{8,24},{16,0},{24,8},{32,48},{40,56},{48,32},{56,40},{64,80... | collective-permute-start | bytes 215048 | tf_op jit(solution)/shard_map/ppermute | solution.py:553
  67.1 4.3 %collective-permute-start.12 = (f32[32,256]{1,0:T(8,128)S(1)}, f32[32,256]{1,0:T(8,128)S(1)}, u32[]{:S(2)}, u32[]{:S(2)}) collective-permute-start(f32[32,256]{1,0:T(8,128)S(1)} %add.75), channel_id=1, source_target_pairs={{0,2},{1,3},{2,0},{3,1},{4,6},{5,7},{6,4},{7,5},{8,10},{9,11},{10,... | collective-permute-start | bytes 98312 | tf_op jit(solution)/shard_map/ppermute | solution.py:553
  71.4 5.5 %collective-permute-start.13 = (f32[35,2048]{1,0:T(8,128)S(1)}, f32[35,2048]{1,0:T(8,128)S(1)}, u32[]{:S(2)}, u32[]{:S(2)}) collective-permute-start(f32[35,2048]{1,0:T(8,128)S(1)} %pad_maximum_fusion.own_ref), channel_id=1, source_target_pairs={{0,8},{8,0},{16,24},{24,16},{32,40},{40,32},{48,56},{56,48},{64,72... | collective-permute-start | bytes 860168 | tf_op jit(solution)/shard_map/ppermute | solution.py:553

commit v5 on v4

--- a/solution.py
+++ b/solution.py
@@ -25,10 +25,10 @@
 GRADS_AT = (0, 1, 3, 4)
 SUMS_AT = (0, 1, 2, 3, 4, 5)
 SUM_ROWS = 128
-SCORE_AT = (6, 7)
-SCORE_ROWS = 128
-(NZ, VZ, NV0, AM1, KEEP, KOFF, C1, C0, YA, YD, YG, ALB) = range(12)
-NCONST = 14
+SCORE_AT = (6,)
+SCORE_ROWS = 256
+(NZ, VZ, NV0, KEEP, KOFF, C1, C0, YA, ALB) = range(9)
+NCONST = 11
 
 NT = (((1,), (1,)), ((), ()))
 NN = (((1,), (0,)), ((), ()))
@@ -61,7 +61,7 @@
     albedo_ref,
     rough_ref,
     pfeat_ref,
-    tfeat_ref,
+    tfeat_in,
     env_ref,
     spec_ref,
     sums_ref,
@@ -69,8 +69,12 @@
     azim_n,
     pfs,
     nz_ref,
+    tfeat_ref,
+    last_ref,
     const,
+    azim_s,
     azim_v,
+    undo,
     score_a,
     score_b,
     mats_a,
@@ -80,9 +84,16 @@
     acc_rad,
     spec_buf,
     sems,
+    tfeat_sem,
 ):
     steps = tfeat_ref.shape[1] // BLK
     first = lax.axis_index("lts") * steps
+    core = lax.axis_index("pts") % 2
+    offset = (1 - core) * (steps // 2) + 2
+
+    def tile_of(k):
+        return lax.rem(k + offset, steps)
+
 
     def prologue():
         normals = normals_ref[...]
@@ -102,34 +113,36 @@
         y_d = -4.0 * alpha / (1.0 - alpha_sq)
         y_g = -0.5 / (1.0 - half)
         y_a = 2.0 / alpha - y_d - y_g - (1.0 - nv) / (2.0 * geo_v)
-        two_r = 2.0 * rough
+        root = 0.5 * jnp.sqrt(1.0 - alpha_sq)
+        ratio = y_d / y_g
         rows = [None] * NCONST
-        rows[NZ] = normals[2:3]
+        rows[NZ] = root * normals[2:3]
         rows[VZ] = 0.5 * views[2:3]
-        rows[NV0] = nv0
-        rows[AM1] = 0.25 * (alpha_sq - 1.0)
-        rows[KEEP] = 1.0 - half
-        rows[KOFF] = half
-        rows[C1] = 0.96 * lead
-        rows[C0] = 0.04 * lead
-        rows[YA] = two_r * y_a
-        rows[YD] = two_r * y_d
-        rows[YG] = two_r * y_g
+        rows[NV0] = root * nv0
+        rows[KEEP] = ratio * (1.0 - half) / root
+        rows[KOFF] = ratio * half
+        rows[C1] = 0.96 * lead * ratio / root
+        rows[C0] = 0.04 * lead * ratio / root
+        rows[YA] = y_a / y_d
         for k in range(3):
-            rows[ALB + k] = albedo_ref[k : k + 1, :] * (1.0 / math.pi)
-        rows += [normals[0:1], normals[1:2], 0.5 * views[0:1], 0.5 * views[1:2]]
+            rows[ALB + k] = albedo_ref[k : k + 1, :] * (1.0 / math.pi) / root
+        rows += [normals[0:1], normals[1:2], normals[2:3], root * normals[0:1], root * normals[1:2]]
+        rows += [0.5 * views[0:1], 0.5 * views[1:2]]
+        undo[0:1, :] = 1.0 / root
+        undo[1:2, :] = 2.0 * rough * y_d
         ebuf[...] = jnp.zeros_like(ebuf)
         for k, r in enumerate(rows):
             ebuf[k : k + 1, :] = r
         cols = ebuf[...].T
         for k in range(NCONST):
             const[k] = jnp.broadcast_to(cols[:, k : k + 1], (PTS, 128))
-        nz_ref[...] = const[NZ]
+        nz_ref[...] = jnp.broadcast_to(cols[:, NCONST + 2 : NCONST + 3], (PTS, 128))
         cos_p = phi_ref[0:1, :]
         sin_p = phi_ref[1:2, :]
         k = NCONST
         azim_n[...] = cols[:, k : k + 1] * cos_p + cols[:, k + 1 : k + 2] * sin_p
-        azim_v[...] = cols[:, k + 2 : k + 3] * cos_p + cols[:, k + 3 : k + 4] * sin_p
+        azim_s[...] = cols[:, k + 3 : k + 4] * cos_p + cols[:, k + 4 : k + 5] * sin_p
+        azim_v[...] = cols[:, k + 5 : k + 6] * cos_p + cols[:, k + 6 : k + 7] * sin_p
         hi, lo = split((pfeat_ref[...] * (0.5 / math.sqrt(pfeat_ref.shape[0]))).T)
         pfs[:, 0:32] = hi
         pfs[:, 32:64] = lo
@@ -138,7 +151,10 @@
         acc[...] = jnp.zeros_like(acc)
         acc_rad[...] = jnp.zeros_like(acc_rad)
 
+    tfeat_copy = pltpu.make_async_copy(tfeat_in, tfeat_ref, tfeat_sem)
+    tfeat_copy.start()
     prologue()
+    tfeat_copy.wait()
     mats_b[...] = jnp.zeros_like(mats_b)
 
     def place(step):
@@ -147,10 +163,11 @@
     def light_of(step):
         return env_ref[:, place(step)] * (theta_ref[0, first + step] * (0.25 * math.pi))
 
-    def spec_copy(step):
-        return pltpu.make_async_copy(spec_buf.at[step], spec_ref.at[step], sems.at[step])
-
-    def shade(step, score, mats, beside):
+    def spec_copy(k):
+        return pltpu.make_async_copy(spec_buf.at[k], spec_ref.at[tile_of(k)], sems.at[k])
+
+    def shade(k_step, score, mats, beside):
+        step = tile_of(k_step)
         sin_t = theta_ref[0, first + step]
         cos_t = theta_ref[1, first + step]
         light = light_of(step)
@@ -165,13 +182,13 @@
             rad = [None] * 3
             for h in range(BLK // 128):
                 lanes = pl.ds(h * 128, 128)
-                nl = azim_n[rows, lanes] * sin_t + nz
+                nl = azim_s[rows, lanes] * sin_t + nz
                 vv = azim_v[rows, lanes] * sin_t + vz
                 tt = jnp.tanh(score[rows, lanes])
                 lit = jnp.maximum(nl, 0.0)
                 inv_len = lax.rsqrt(jnp.maximum(vv, 0.125))
                 nh = (nl + c[NV0]) * inv_len
-                dd = nh * nh * c[AM1] + 1.0
+                dd = 1.0 - nh * nh
                 gg = lit * c[KEEP] + c[KOFF]
                 inv = pl.reciprocal(dd * dd * gg, approx=True)
                 x1 = 1.0 - vv * inv_len
@@ -179,8 +196,8 @@
                 fres = x2 * x2 * x1 * c[C1] + c[C0]
                 base = (1.0 + tt) * lit
                 spec = fres * inv * base
-                fact = inv * dd * (c[YD] * gg + c[YG] * dd) + c[YA]
-                spec_buf[step, rows, lanes] = spec
+                fact = inv * dd * (gg + dd) + c[YA]
+                spec_buf[k_step, rows, lanes] = spec
                 hi, lo = split(spec * fact)
                 mats[pl.ds(r0, CHUNK), lanes] = base.astype(BF16)
                 mats[pl.ds(PTS + r0, CHUNK), lanes] = hi
@@ -204,17 +221,16 @@
                 lk = light[k : k + 1, 128 * h : 128 * h + 128]
                 energy_ref[k : k + 1, pl.ds(pl.multiple_of(step * BLK + 128 * h, 128), 128)] = lk * lk * jnp.sum(eng[3 * h + k], axis=0, keepdims=True)
 
-        spec_copy(step).start()
-
-    def light_rows(step):
-        light = light_of(step)
+
+    def light_rows(k_step):
+        light = light_of(tile_of(k_step))
         l_hi = light.astype(BF16).astype(F32)
         ebuf[0:3, :] = l_hi
         ebuf[3:6, :] = light - l_hi
         return ebuf[0:16, :].astype(BF16)
 
     def beside(lmat, mats, score, nxt):
-        t_hi, t_lo = split(tfeat_ref[:, place(nxt)])
+        t_hi, t_lo = split(tfeat_ref[:, place(tile_of(nxt))])
         feats = jnp.concatenate([t_hi, t_hi, t_lo], axis=0)
 
         def run(i):
@@ -241,9 +257,8 @@
 
         return run
 
-    score_a[...] = score_tile(pfs, tfeat_ref[:, place(0)])
-
-    @pl.loop(0, steps // 2)
+    score_a[...] = score_tile(pfs, tfeat_ref[:, place(tile_of(0))])
+
     def pair(j):
         a = 2 * j
         lmat = light_rows(jnp.maximum(a - 1, 0))
@@ -251,9 +266,18 @@
         lmat = light_rows(a)
         shade(a + 1, score_b, mats_b, beside(lmat, mats_a, score_a, jnp.minimum(a + 2, steps - 1)))
 
+        @pl.when(j < steps // 2 - 1)
+        def send():
+            spec_copy(a).start()
+            spec_copy(a + 1).start()
+
+    pl.loop(0, steps // 2)(pair)
     acc[...] += dot(light_rows(steps - 1), mats_b[...], NT)
     both = acc[0:3, :] + acc[3:6, :]
-    rows = [both[:, 0:PTS], both[:, PTS : 2 * PTS] + both[:, 2 * PTS : 3 * PTS]]
+    rows = [
+        both[:, 0:PTS] * undo[0:1, :],
+        (both[:, PTS : 2 * PTS] + both[:, 2 * PTS : 3 * PTS]) * undo[1:2, :],
+    ]
     for k in range(3):
         const[0, :, k : k + 1] = jnp.sum(acc_rad[k], axis=1, keepdims=True)
     rows.append(const[0].T[0:3, :])
@@ -261,7 +285,9 @@
         for k in range(3):
             sums_ref[j, 3 * k : 3 * k + 3, :] = rows[k]
 
-    @pl.loop(0, steps)
+    last_ref[...] = spec_buf[steps - 2 : steps]
+
+    @pl.loop(0, steps - 2)
     def drain(step):
         spec_copy(step).wait()
 
@@ -404,6 +430,7 @@
     env_ref,
     spec_ref,
     energy_ref,
+    last_ref,
     rad_ref,
     galb_ref,
     grough_ref,
@@ -450,7 +477,11 @@
     def spec_copy(tile):
         return pltpu.make_async_copy(spec_ref.at[tile], spec_buf.at[tile], sems.at[tile])
 
-    @pl.loop(0, tiles)
+    for step in range(2):
+        tile = (1 - core) * steps + step
+        pltpu.make_async_copy(last_ref.at[step], spec_buf.at[tile], sems.at[tile]).start()
+
+    @pl.loop(2, tiles)
     def fetch(step):
         spec_copy(lax.rem(step + (1 - core) * steps, tiles)).start()
 
@@ -495,6 +526,7 @@
 
     vmem = pl.BlockSpec(memory_space=pltpu.VMEM)
     smem = pl.BlockSpec(memory_space=pltpu.SMEM)
+    anywhere = pl.BlockSpec(memory_space=pl.ANY)
     params = pltpu.CompilerParams(vmem_limit_bytes=20 * 1024 * 1024)
 
     def hbm(x):
@@ -508,10 +540,10 @@
     def shape(*dims, dtype=F32):
         return jax.ShapeDtypeStruct(dims, dtype)
 
-    spec, sums, energy, azim_n, pfs, nz = pl.pallas_call(
+    spec, sums, energy, azim_n, pfs, nz, tfeat, last = pl.pallas_call(
         shade_kernel,
-        in_specs=[smem] + [vmem] * 9,
-        out_specs=[pl.BlockSpec(memory_space=pl.ANY)] + [vmem] * 5,
+        in_specs=[smem] + [vmem] * 7 + [anywhere, vmem],
+        out_specs=[anywhere] + [vmem] * 7,
         out_shape=[
             pltpu.HBM((steps, pts, BLK), F32),
             shape(lax.axis_size("lts"), 9, pts),
@@ -519,10 +551,14 @@
             shape(pts, COLS),
             shape(pts, 96, dtype=BF16),
             shape(pts, 128),
+            shape(32, tex),
+            shape(2, pts, BLK),
         ],
         scratch_shapes=[
             pltpu.VMEM((NCONST, PTS, 128), F32),
             pltpu.VMEM((PTS, COLS), F32),
+            pltpu.VMEM((PTS, COLS), F32),
+            pltpu.VMEM((8, PTS), F32),
             pltpu.VMEM((PTS, BLK), F32),
             pltpu.VMEM((PTS, BLK), F32),
             pltpu.VMEM((3 * PTS, BLK), BF16),
@@ -532,6 +568,7 @@
             pltpu.VMEM((3, PTS, 128), F32),
             pltpu.VMEM((steps, PTS, BLK), F32),
             pltpu.SemaphoreType.DMA((steps,)),
+            pltpu.SemaphoreType.DMA,
         ],
         compiler_params=params,
         name="shade",
@@ -556,10 +593,9 @@
     sums = lax.all_to_all(sums, "lts", 0, 0)
 
     def grads():
-        anywhere = pl.BlockSpec(memory_space=pl.ANY)
         return pl.pallas_call(
             functools.partial(grad_kernel, scale),
-            in_specs=[smem] + [vmem] * 9 + [anywhere, vmem],
+            in_specs=[smem] + [vmem] * 9 + [anywhere, vmem, vmem],
             out_specs=[vmem] * 6,
             out_shape=[shape(3, pts), shape(3, pts), shape(1, pts), shape(32, pts)]
             + [shape(40, tex // 2)] * 2,
@@ -586,10 +622,11 @@
             azim_n,
             pfs,
             nz,
-            texel_feat,
+            tfeat,
             env,
             spec,
             energy,
+            last,
         )
 
     place = lax.axis_index("pts")

time: 77.9 us -> 75.8 us (0.973)
  Pallas kernels: 24 us -> 21.8 us
    pallas_call x1, Pallas kernels: 13.1 us -> 11.7 us  [shards(): pl.pallas_call(shade_kernel, in_specs=[smem] + [vmem] * 7 + [anywhere, vm...]
where the time goes in v5:
time: 75.8 us; the launch traced here: 75.6 us
  starting transfers between devices  24.3 us (32%)
  Pallas kernels  21.8 us (29%)
  waiting for transfers between devices  16.8 us (22%)
  blocking collectives  11.1 us (15%)
  other arithmetic  0.83 us (1%)
    ppermute x14, starting transfers between devices, swap(): return lax.ppermute(x, axis, [(i, i ^ bits) for i in range(n)])  24.3 us
    ppermute x14, waiting for transfers between devices, swap(): return lax.ppermute(x, axis, [(i, i ^ bits) for i in range(n)])  16.8 us
    pallas_call x1, Pallas kernels, shards(): pl.pallas_call(shade_kernel, in_specs=[smem] + [vmem] * 7 + [anywhere, vm...  11.7 us
    all_to_all x1, blocking collectives, shards(): sums = lax.all_to_all(sums, 'lts', 0, 0)  11.1 us
    pallas_call x1, Pallas kernels, grads(): pl.pallas_call(functools.partial(grad_kernel, scale), in_specs=[smem] + [...  9.25 us
  transfers between devices with their start and end apart: 14, of which 10 were waited for; matrix products, arithmetic and copies ran while one was open for 1% of the time, Pallas kernels for 0%

profile of v5, /device:TPU:1, one launch (start us, length us, event | category | flops | bytes accessed | tf_op | source)
XLA Modules:
  0.0 75.6 jit_solution(2078134971800183627)
XLA Ops:
  0.6 11.7 %shade.1 = (f32[16,256,256]{2,1,0:T(8,128)}, f32[8,9,256]{2,1,0:T(8,128)S(1)}, f32[3,4096]{1,0:T(4,128)S(1)}, f32[256,256]{1,0:T(8,128)S(1)}, bf16[256,96]{1,0:T...) custom-call(f32[2,128]{1,0:T(2,128)} %constant.28.clone.theta_ref, ...), custom_call_target="tpu_custom_call" | custom-call | tf_op jit(solution)/shard_map/shade/pallas_call | solution.py:543
  12.3 11.1 %all_to_all.5.sums_ref = f32[8,9,256]{2,1,0:T(8,128)S(1)} all-to-all(f32[8,9,256]{2,1,0:T(8,128)S(1)} %get-tuple-element.28), channel_id=1, replica_groups=mesh['pts'=32,'lts'=8] {'lts'}, dimensions={0} | all-to-all | bytes 147456 | tf_op jit(solution)/shard_map/all_to_all | solution.py:593
  23.5 9.3 %grads.1 = (f32[3,256]{1,0:T(4,128)}, f32[3,256]{1,0:T(4,128)}, f32[1,256]{1,0:T(1,128)}, f32[32,256]{1,0:T(8,128)S(1)}, f32[40,2048]{1,0:T(8,128)S(1)}, /*index=5*/f32[40,2048]{1,0:T(8,128)S(1)}) custom-call(f32[2,128]{1,0:T(2,128)} %constant.28.clone.theta_ref, f32[8,9,256]{2,1,0:T(8,128)S(1)} %all_to_all.5.sums_ref, f32[3,256]{1,0:T(4,128)} %albedo_ref.3, ...), custom_call_target="tpu_custom_call" | custom-call | tf_op jit(solution)/shard_map/grads/pallas_call | solution.py:596
  32.7 2.2 %collective-permute-start = (f32[40,2048]{1,0:T(8,128)S(1)}, f32[40,2048]{1,0:T(8,128)S(1)}, u32[]{:S(2)}, u32[]{:S(2)}) collective-permute-start(f32[40,2048]{1,0:T(8,128)S(1)} %get-tuple-element.41), channel_id=1, source_target_pairs={{0,8},{8,0},{16,24},{24,16},{32,40},{40,32},{48,56},{56,48},{64,72... | collective-permute-start | bytes 983048 | tf_op jit(solution)/shard_map/ppermute | solution.py:590
  34.9 1.3 %collective-permute-done = f32[40,2048]{1,0:T(8,128)S(1)} collective-permute-done((f32[40,2048]{1,0:T(8,128)S(1)}, f32[40,2048]{1,0:T(8,128)S(1)}, u32[]{:S(2)}, u32[]{:S(2)}) %collective-permute-start) | collective-permute-done | bytes 327712 | tf_op jit(solution)/shard_map/ppermute | solution.py:590
  36.2 2.7 %collective-permute-start.1 = (f32[40,512]{1,0:T(8,128)S(1)}, f32[40,512]{1,0:T(8,128)S(1)}, u32[]{:S(2)}, u32[]{:S(2)}) collective-permute-start(f32[40,512]{1,0:T(8,128)S(1)} %get-tuple-element.54), channel_id=1, source_target_pairs={{0,16},{8,24},{16,0},{24,8},{32,48},{40,56},{48,32},{56,40},{64,80... | collective-permute-start | bytes 245768 | tf_op jit(solution)/shard_map/ppermute | solution.py:590
  38.9 1.6 %collective-permute-start.2 = (f32[40,512]{1,0:T(8,128)S(1)}, f32[40,512]{1,0:T(8,128)S(1)}, u32[]{:S(2)}, u32[]{:S(2)}) collective-permute-start(f32[40,512]{1,0:T(8,128)S(1)} %get-tuple-element.56), channel_id=1, source_target_pairs={{0,32},{8,40},{16,48},{24,56},{32,0},{40,8},{48,16},{56,24},{64,96... | collective-permute-start | bytes 245768 | tf_op jit(solution)/shard_map/ppermute | solution.py:590
  41.5 0.9 %collective-permute-done.2 = f32[40,512]{1,0:T(8,128)S(1)} collective-permute-done((f32[40,512]{1,0:T(8,128)S(1)}, f32[40,512]{1,0:T(8,128)S(1)}, u32[]{:S(2)}, u32[]{:S(2)}) %collective-permute-start.2) | collective-permute-done | bytes 81952 | tf_op jit(solution)/shard_map/ppermute | solution.py:590
  42.4 3.9 %collective-permute-done.3 = f32[40,512]{1,0:T(8,128)S(1)} collective-permute-done((f32[40,512]{1,0:T(8,128)S(1)}, f32[40,512]{1,0:T(8,128)S(1)}, u32[]{:S(2)}, u32[]{:S(2)}) %collective-permute-start.3) | collective-permute-done | bytes 81952 | tf_op jit(solution)/shard_map/ppermute | solution.py:590
  46.3 3.1 %collective-permute-start.5 = (f32[40,512]{1,0:T(8,128)S(1)}, f32[40,512]{1,0:T(8,128)S(1)}, u32[]{:S(2)}, u32[]{:S(2)}) collective-permute-start(f32[40,512]{1,0:T(8,128)S(1)} %add_add_fusion.1), channel_id=1, source_target_pairs={{0,64},{8,72},{16,80},{24,88},{32,96},{40,104},{48,112},{56,120},{... | collective-permute-start | bytes 245768 | tf_op jit(solution)/shard_map/ppermute | solution.py:590
  49.4 4.3 %collective-permute-start.6 = (f32[40,512]{1,0:T(8,128)S(1)}, f32[40,512]{1,0:T(8,128)S(1)}, u32[]{:S(2)}, u32[]{:S(2)}) collective-permute-start(f32[40,512]{1,0:T(8,128)S(1)} %add_add_fusion.1), channel_id=1, source_target_pairs={{0,128},{8,136},{16,144},{24,152},{32,160},{40,168},{48,176},{56,1... | collective-permute-start | bytes 245768 | tf_op jit(solution)/shard_map/ppermute | solution.py:590
  53.7 0.7 collective-permute-start.8
  54.4 2.3 %collective-permute-done.6 = f32[40,512]{1,0:T(8,128)S(1)} collective-permute-done((f32[40,512]{1,0:T(8,128)S(1)}, f32[40,512]{1,0:T(8,128)S(1)}, u32[]{:S(2)}, u32[]{:S(2)}) %collective-permute-start.6) | collective-permute-done | bytes 81952 | tf_op jit(solution)/shard_map/ppermute | solution.py:590
  56.6 3.9 %collective-permute-done.7 = f32[40,512]{1,0:T(8,128)S(1)} collective-permute-done((f32[40,512]{1,0:T(8,128)S(1)}, f32[40,512]{1,0:T(8,128)S(1)}, u32[]{:S(2)}, u32[]{:S(2)}) %collective-permute-start.7) | collective-permute-done | bytes 81952 | tf_op jit(solution)/shard_map/ppermute | solution.py:590
  60.6 1.5 %collective-permute-start.10 = (f32[35,512]{1,0:T(8,128)S(1)}, f32[35,512]{1,0:T(8,128)S(1)}, u32[]{:S(2)}, u32[]{:S(2)}) collective-permute-start(f32[35,512]{1,0:T(8,128)S(1)} %pad_maximum_fusion.1), channel_id=1, source_target_pairs={{0,32},{8,40},{16,48},{24,56},{32,0},{40,8},{48,16},{56,24},{64,96... | collective-permute-start | bytes 215048 | tf_op jit(solution)/shard_map/ppermute | solution.py:590
  62.1 0.6 collective-permute-start.11
  62.7 2.2 %collective-permute-start.9 = (f32[35,512]{1,0:T(8,128)S(1)}, f32[35,512]{1,0:T(8,128)S(1)}, u32[]{:S(2)}, u32[]{:S(2)}) collective-permute-start(f32[35,512]{1,0:T(8,128)S(1)} %pad_maximum_fusion.1), channel_id=1, source_target_pairs={{0,16},{8,24},{16,0},{24,8},{32,48},{40,56},{48,32},{56,40},{64,80... | collective-permute-start | bytes 215048 | tf_op jit(solution)/shard_map/ppermute | solution.py:590
  64.9 0.8 %collective-permute-start.12 = (f32[32,256]{1,0:T(8,128)S(1)}, f32[32,256]{1,0:T(8,128)S(1)}, u32[]{:S(2)}, u32[]{:S(2)}) collective-permute-start(f32[32,256]{1,0:T(8,128)S(1)} %add.75), channel_id=1, source_target_pairs={{0,2},{1,3},{2,0},{3,1},{4,6},{5,7},{6,4},{7,5},{8,10},{9,11},{10,... | collective-permute-start | bytes 98312 | tf_op jit(solution)/shard_map/ppermute | solution.py:590
  65.7 2.4 %collective-permute-done.11 = f32[35,512]{1,0:T(8,128)S(1)} collective-permute-done((f32[35,512]{1,0:T(8,128)S(1)}, f32[35,512]{1,0:T(8,128)S(1)}, u32[]{:S(2)}, u32[]{:S(2)}) %collective-permute-start.11) | collective-permute-done | bytes 71712 | tf_op jit(solution)/shard_map/ppermute | solution.py:590
  68.5 0.7 collective-permute-done.12
  69.2 4.3 %collective-permute-start.13 = (f32[35,2048]{1,0:T(8,128)S(1)}, f32[35,2048]{1,0:T(8,128)S(1)}, u32[]{:S(2)}, u32[]{:S(2)}) collective-permute-start(f32[35,2048]{1,0:T(8,128)S(1)} %pad_maximum_fusion.own_ref), channel_id=1, source_target_pairs={{0,8},{8,0},{16,24},{24,16},{32,40},{40,32},{48,56},{56,48},{64,72... | collective-permute-start | bytes 860168 | tf_op jit(solution)/shard_map/ppermute | solution.py:590
  73.5 0.6 add.76
  74.1 0.6 collective-permute-done.13.other_ref
  74.7 0.9 %join.1 = (f32[32,4096]{1,0:T(8,128)}, f32[3,4096]{1,0:T(4,128)}) custom-call(f32[35,2048]{1,0:T(8,128)S(1)} %pad_maximum_fusion.own_ref, f32[35,2048]{1,0:T(8,128)S(1)} %collective-permute-done.13.other_ref), custom_call_target="tpu_custom_call" | custom-call | tf_op jit(solution)/shard_map/join/pallas_call | solution.py:509
  (21 shorter events, 1.4 us)
Async XLA Ops:
  32.7 3.4 %collective-permute-start = (f32[40,2048]{1,0:T(8,128)S(1)}, f32[40,2048]{1,0:T(8,128)S(1)}, u32[]{:S(2)}, u32[]{:S(2)}) collective-permute-start(f32[40,2048]{1,0:T(8,128)S(1)} %get-tuple-element.41), channel_id=1, source_target_pairs={{0,8},{8,0},{16,24},{24,16},{32,40},{40,32},{48,56},{56,48},{64,72... | collective-permute-start | bytes 983048 | tf_op jit(solution)/shard_map/ppermute | solution.py:590
  36.2 5.2 %collective-permute-start.1 = (f32[40,512]{1,0:T(8,128)S(1)}, f32[40,512]{1,0:T(8,128)S(1)}, u32[]{:S(2)}, u32[]{:S(2)}) collective-permute-start(f32[40,512]{1,0:T(8,128)S(1)} %get-tuple-element.54), channel_id=1, source_target_pairs={{0,16},{8,24},{16,0},{24,8},{32,48},{40,56},{48,32},{56,40},{64,80... | collective-permute-start | bytes 245768 | tf_op jit(solution)/shard_map/ppermute | solution.py:590
  38.9 3.5 %collective-permute-start.2 = (f32[40,512]{1,0:T(8,128)S(1)}, f32[40,512]{1,0:T(8,128)S(1)}, u32[]{:S(2)}, u32[]{:S(2)}) collective-permute-start(f32[40,512]{1,0:T(8,128)S(1)} %get-tuple-element.56), channel_id=1, source_target_pairs={{0,32},{8,40},{16,48},{24,56},{32,0},{40,8},{48,16},{56,24},{64,96... | collective-permute-start | bytes 245768 | tf_op jit(solution)/shard_map/ppermute | solution.py:590
  40.6 5.7 %collective-permute-start.3 = (f32[40,512]{1,0:T(8,128)S(1)}, f32[40,512]{1,0:T(8,128)S(1)}, u32[]{:S(2)}, u32[]{:S(2)}) collective-permute-start(f32[40,512]{1,0:T(8,128)S(1)} %get-tuple-element.55), channel_id=1, source_target_pairs={{0,48},{8,56},{16,32},{24,40},{32,16},{40,24},{48,0},{56,8},{64,11... | collective-permute-start | bytes 245768 | tf_op jit(solution)/shard_map/ppermute | solution.py:590
  40.6 5.7 %collective-permute-start.4 = (f32[32,256]{1,0:T(8,128)S(1)}, f32[32,256]{1,0:T(8,128)S(1)}, u32[]{:S(2)}, u32[]{:S(2)}) collective-permute-start(f32[32,256]{1,0:T(8,128)S(1)} %get-tuple-element.39), channel_id=1, source_target_pairs={{0,4},{1,5},{2,6},{3,7},{4,0},{5,1},{6,2},{7,3},{8,12},{9,13},{10,... | collective-permute-start | bytes 98312 | tf_op jit(solution)/shard_map/ppermute | solution.py:590
  46.3 8.0 %collective-permute-start.5 = (f32[40,512]{1,0:T(8,128)S(1)}, f32[40,512]{1,0:T(8,128)S(1)}, u32[]{:S(2)}, u32[]{:S(2)}) collective-permute-start(f32[40,512]{1,0:T(8,128)S(1)} %add_add_fusion.1), channel_id=1, source_target_pairs={{0,64},{8,72},{16,80},{24,88},{32,96},{40,104},{48,112},{56,120},{... | collective-permute-start | bytes 245768 | tf_op jit(solution)/shard_map/ppermute | solution.py:590
  49.4 7.2 %collective-permute-start.6 = (f32[40,512]{1,0:T(8,128)S(1)}, f32[40,512]{1,0:T(8,128)S(1)}, u32[]{:S(2)}, u32[]{:S(2)}) collective-permute-start(f32[40,512]{1,0:T(8,128)S(1)} %add_add_fusion.1), channel_id=1, source_target_pairs={{0,128},{8,136},{16,144},{24,152},{32,160},{40,168},{48,176},{56,1... | collective-permute-start | bytes 245768 | tf_op jit(solution)/shard_map/ppermute | solution.py:590
  53.7 6.8 %collective-permute-start.7 = (f32[40,512]{1,0:T(8,128)S(1)}, f32[40,512]{1,0:T(8,128)S(1)}, u32[]{:S(2)}, u32[]{:S(2)}) collective-permute-start(f32[40,512]{1,0:T(8,128)S(1)} %add_add_fusion.1), channel_id=1, source_target_pairs={{0,192},{8,200},{16,208},{24,216},{32,224},{40,232},{48,240},{56,2... | collective-permute-start | bytes 245768 | tf_op jit(solution)/shard_map/ppermute | solution.py:590
  53.7 6.9 %collective-permute-start.8 = (f32[32,256]{1,0:T(8,128)S(1)}, f32[32,256]{1,0:T(8,128)S(1)}, u32[]{:S(2)}, u32[]{:S(2)}) collective-permute-start(f32[32,256]{1,0:T(8,128)S(1)} %add.67), channel_id=1, source_target_pairs={{0,1},{1,0},{2,3},{3,2},{4,5},{5,4},{6,7},{7,6},{8,9},{9,8},{10,11... | collective-permute-start | bytes 98312 | tf_op jit(solution)/shard_map/ppermute | solution.py:590
  60.6 5.2 %collective-permute-start.10 = (f32[35,512]{1,0:T(8,128)S(1)}, f32[35,512]{1,0:T(8,128)S(1)}, u32[]{:S(2)}, u32[]{:S(2)}) collective-permute-start(f32[35,512]{1,0:T(8,128)S(1)} %pad_maximum_fusion.1), channel_id=1, source_target_pairs={{0,32},{8,40},{16,48},{24,56},{32,0},{40,8},{48,16},{56,24},{64,96... | collective-permute-start | bytes 215048 | tf_op jit(solution)/shard_map/ppermute | solution.py:590
  62.1 6.0 %collective-permute-start.11 = (f32[35,512]{1,0:T(8,128)S(1)}, f32[35,512]{1,0:T(8,128)S(1)}, u32[]{:S(2)}, u32[]{:S(2)}) collective-permute-start(f32[35,512]{1,0:T(8,128)S(1)} %pad_maximum_fusion.1), channel_id=1, source_target_pairs={{0,48},{8,56},{16,32},{24,40},{32,16},{40,24},{48,0},{56,8},{64,11... | collective-permute-start | bytes 215048 | tf_op jit(solution)/shard_map/ppermute | solution.py:590
  62.7 5.7 %collective-permute-start.9 = (f32[35,512]{1,0:T(8,128)S(1)}, f32[35,512]{1,0:T(8,128)S(1)}, u32[]{:S(2)}, u32[]{:S(2)}) collective-permute-start(f32[35,512]{1,0:T(8,128)S(1)} %pad_maximum_fusion.1), channel_id=1, source_target_pairs={{0,16},{8,24},{16,0},{24,8},{32,48},{40,56},{48,32},{56,40},{64,80... | collective-permute-start | bytes 215048 | tf_op jit(solution)/shard_map/ppermute | solution.py:590
  64.9 4.3 %collective-permute-start.12 = (f32[32,256]{1,0:T(8,128)S(1)}, f32[32,256]{1,0:T(8,128)S(1)}, u32[]{:S(2)}, u32[]{:S(2)}) collective-permute-start(f32[32,256]{1,0:T(8,128)S(1)} %add.75), channel_id=1, source_target_pairs={{0,2},{1,3},{2,0},{3,1},{4,6},{5,7},{6,4},{7,5},{8,10},{9,11},{10,... | collective-permute-start | bytes 98312 | tf_op jit(solution)/shard_map/ppermute | solution.py:590
  69.2 5.5 %collective-permute-start.13 = (f32[35,2048]{1,0:T(8,128)S(1)}, f32[35,2048]{1,0:T(8,128)S(1)}, u32[]{:S(2)}, u32[]{:S(2)}) collective-permute-start(f32[35,2048]{1,0:T(8,128)S(1)} %pad_maximum_fusion.own_ref), channel_id=1, source_target_pairs={{0,8},{8,0},{16,24},{24,16},{32,40},{40,32},{48,56},{56,48},{64,72... | collective-permute-start | bytes 860168 | tf_op jit(solution)/shard_map/ppermute | solution.py:590

commit v6 on v5

--- a/solution.py
+++ b/solution.py
@@ -639,10 +639,10 @@
     gpf_other = swap(gpf, "lts", 4)
     x = own + other
     cut = [lax.dynamic_slice(x, (0, quad * (group ^ m)), (40, quad)) for m in range(4)]
-    got = [swap(cut[m], "pts", 2 * m) for m in (1, 2, 3)]
+    got = [swap(cut[m], "pts", 2 * m) for m in (3, 2, 1)]
     x = (cut[0] + got[0]) + (got[1] + got[2])
     x, gpf_other = barrier((x, gpf_other))
-    got = [swap(x, "pts", m) for m in (8, 16, 24)]
+    got = [swap(x, "pts", m) for m in (16, 24, 8)]
     gpf = gpf + gpf_other
     gpf_other = swap(gpf, "lts", 1)
     x = (x + got[0]) + (got[1] + got[2])

time: 75.8 us -> 74.5 us (0.983)
  waiting for transfers between devices: 16.8 us -> 15.5 us
    ppermute x14, waiting for transfers between devices: 16.8 us -> 15.5 us  [swap(): return lax.ppermute(x, axis, [(i, i ^ bits) for i in range(n)])]
where the time goes in v6:
time: 74.5 us; the launch traced here: 74.3 us
  starting transfers between devices  24.3 us (33%)
  Pallas kernels  21.8 us (29%)
  waiting for transfers between devices  15.5 us (21%)
  blocking collectives  11.1 us (15%)
  other arithmetic  0.83 us (1%)
  between operations  0.75 us (1%)
    ppermute x14, starting transfers between devices, swap(): return lax.ppermute(x, axis, [(i, i ^ bits) for i in range(n)])  24.3 us
    ppermute x14, waiting for transfers between devices, swap(): return lax.ppermute(x, axis, [(i, i ^ bits) for i in range(n)])  15.5 us
    pallas_call x1, Pallas kernels, shards(): pl.pallas_call(shade_kernel, in_specs=[smem] + [vmem] * 7 + [anywhere, vm...  11.7 us
    all_to_all x1, blocking collectives, shards(): sums = lax.all_to_all(sums, 'lts', 0, 0)  11.1 us
    pallas_call x1, Pallas kernels, grads(): pl.pallas_call(functools.partial(grad_kernel, scale), in_specs=[smem] + [...  9.25 us
  transfers between devices with their start and end apart: 14, of which 10 were waited for; matrix products, arithmetic and copies ran while one was open for 1% of the time, Pallas kernels for 0%

profile of v6, /device:TPU:1, one launch (start us, length us, event | category | flops | bytes accessed | tf_op | source)
XLA Modules:
  0.0 74.3 jit_solution(13097353026504897205)
XLA Ops:
  0.6 11.7 %shade.1 = (f32[16,256,256]{2,1,0:T(8,128)}, f32[8,9,256]{2,1,0:T(8,128)S(1)}, f32[3,4096]{1,0:T(4,128)S(1)}, f32[256,256]{1,0:T(8,128)S(1)}, bf16[256,96]{1,0:T...) custom-call(f32[2,128]{1,0:T(2,128)} %constant.28.clone.theta_ref, ...), custom_call_target="tpu_custom_call" | custom-call | tf_op jit(solution)/shard_map/shade/pallas_call | solution.py:543
  12.3 11.1 %all_to_all.5.sums_ref = f32[8,9,256]{2,1,0:T(8,128)S(1)} all-to-all(f32[8,9,256]{2,1,0:T(8,128)S(1)} %get-tuple-element.28), channel_id=1, replica_groups=mesh['pts'=32,'lts'=8] {'lts'}, dimensions={0} | all-to-all | bytes 147456 | tf_op jit(solution)/shard_map/all_to_all | solution.py:593
  23.5 9.3 %grads.1 = (f32[3,256]{1,0:T(4,128)}, f32[3,256]{1,0:T(4,128)}, f32[1,256]{1,0:T(1,128)}, f32[32,256]{1,0:T(8,128)S(1)}, f32[40,2048]{1,0:T(8,128)S(1)}, /*index=5*/f32[40,2048]{1,0:T(8,128)S(1)}) custom-call(f32[2,128]{1,0:T(2,128)} %constant.28.clone.theta_ref, f32[8,9,256]{2,1,0:T(8,128)S(1)} %all_to_all.5.sums_ref, f32[3,256]{1,0:T(4,128)} %albedo_ref.3, ...), custom_call_target="tpu_custom_call" | custom-call | tf_op jit(solution)/shard_map/grads/pallas_call | solution.py:596
  32.7 2.2 %collective-permute-start = (f32[40,2048]{1,0:T(8,128)S(1)}, f32[40,2048]{1,0:T(8,128)S(1)}, u32[]{:S(2)}, u32[]{:S(2)}) collective-permute-start(f32[40,2048]{1,0:T(8,128)S(1)} %get-tuple-element.41), channel_id=1, source_target_pairs={{0,8},{8,0},{16,24},{24,16},{32,40},{40,32},{48,56},{56,48},{64,72... | collective-permute-start | bytes 983048 | tf_op jit(solution)/shard_map/ppermute | solution.py:590
  34.9 1.3 %collective-permute-done = f32[40,2048]{1,0:T(8,128)S(1)} collective-permute-done((f32[40,2048]{1,0:T(8,128)S(1)}, f32[40,2048]{1,0:T(8,128)S(1)}, u32[]{:S(2)}, u32[]{:S(2)}) %collective-permute-start) | collective-permute-done | bytes 327712 | tf_op jit(solution)/shard_map/ppermute | solution.py:590
  36.2 4.1 %collective-permute-start.1 = (f32[40,512]{1,0:T(8,128)S(1)}, f32[40,512]{1,0:T(8,128)S(1)}, u32[]{:S(2)}, u32[]{:S(2)}) collective-permute-start(f32[40,512]{1,0:T(8,128)S(1)} %get-tuple-element.54), channel_id=1, source_target_pairs={{0,48},{8,56},{16,32},{24,40},{32,16},{40,24},{48,0},{56,8},{64,11... | collective-permute-start | bytes 245768 | tf_op jit(solution)/shard_map/ppermute | solution.py:590
  40.3 0.4 collective-permute-start.3
  40.9 1.7 %collective-permute-done.1 = f32[40,512]{1,0:T(8,128)S(1)} collective-permute-done((f32[40,512]{1,0:T(8,128)S(1)}, f32[40,512]{1,0:T(8,128)S(1)}, u32[]{:S(2)}, u32[]{:S(2)}) %collective-permute-start.1) | collective-permute-done | bytes 81952 | tf_op jit(solution)/shard_map/ppermute | solution.py:590
  42.6 1.1 %collective-permute-done.2 = f32[40,512]{1,0:T(8,128)S(1)} collective-permute-done((f32[40,512]{1,0:T(8,128)S(1)}, f32[40,512]{1,0:T(8,128)S(1)}, u32[]{:S(2)}, u32[]{:S(2)}) %collective-permute-start.2) | collective-permute-done | bytes 81952 | tf_op jit(solution)/shard_map/ppermute | solution.py:590
  43.7 1.4 %collective-permute-done.3 = f32[40,512]{1,0:T(8,128)S(1)} collective-permute-done((f32[40,512]{1,0:T(8,128)S(1)}, f32[40,512]{1,0:T(8,128)S(1)}, u32[]{:S(2)}, u32[]{:S(2)}) %collective-permute-start.3) | collective-permute-done | bytes 81952 | tf_op jit(solution)/shard_map/ppermute | solution.py:590
  45.1 6.8 %collective-permute-start.5 = (f32[40,512]{1,0:T(8,128)S(1)}, f32[40,512]{1,0:T(8,128)S(1)}, u32[]{:S(2)}, u32[]{:S(2)}) collective-permute-start(f32[40,512]{1,0:T(8,128)S(1)} %add_add_fusion.1), channel_id=1, source_target_pairs={{0,128},{8,136},{16,144},{24,152},{32,160},{40,168},{48,176},{56,1... | collective-permute-start | bytes 245768 | tf_op jit(solution)/shard_map/ppermute | solution.py:590
  51.9 1.2 %collective-permute-start.7 = (f32[40,512]{1,0:T(8,128)S(1)}, f32[40,512]{1,0:T(8,128)S(1)}, u32[]{:S(2)}, u32[]{:S(2)}) collective-permute-start(f32[40,512]{1,0:T(8,128)S(1)} %add_add_fusion.1), channel_id=1, source_target_pairs={{0,64},{8,72},{16,80},{24,88},{32,96},{40,104},{48,112},{56,120},{... | collective-permute-start | bytes 245768 | tf_op jit(solution)/shard_map/ppermute | solution.py:590
  53.1 0.6 collective-permute-start.8
  53.9 3.7 %collective-permute-done.6 = f32[40,512]{1,0:T(8,128)S(1)} collective-permute-done((f32[40,512]{1,0:T(8,128)S(1)}, f32[40,512]{1,0:T(8,128)S(1)}, u32[]{:S(2)}, u32[]{:S(2)}) %collective-permute-start.6) | collective-permute-done | bytes 81952 | tf_op jit(solution)/shard_map/ppermute | solution.py:590
  57.5 0.4 collective-permute-done.7
  58.0 2.0 %collective-permute-start.10 = (f32[35,512]{1,0:T(8,128)S(1)}, f32[35,512]{1,0:T(8,128)S(1)}, u32[]{:S(2)}, u32[]{:S(2)}) collective-permute-start(f32[35,512]{1,0:T(8,128)S(1)} %pad_maximum_fusion.1), channel_id=1, source_target_pairs={{0,32},{8,40},{16,48},{24,56},{32,0},{40,8},{48,16},{56,24},{64,96... | collective-permute-start | bytes 215048 | tf_op jit(solution)/shard_map/ppermute | solution.py:590
  60.0 4.3 %collective-permute-start.11 = (f32[35,512]{1,0:T(8,128)S(1)}, f32[35,512]{1,0:T(8,128)S(1)}, u32[]{:S(2)}, u32[]{:S(2)}) collective-permute-start(f32[35,512]{1,0:T(8,128)S(1)} %pad_maximum_fusion.1), channel_id=1, source_target_pairs={{0,48},{8,56},{16,32},{24,40},{32,16},{40,24},{48,0},{56,8},{64,11... | collective-permute-start | bytes 215048 | tf_op jit(solution)/shard_map/ppermute | solution.py:590
  64.3 0.9 %collective-permute-start.12 = (f32[32,256]{1,0:T(8,128)S(1)}, f32[32,256]{1,0:T(8,128)S(1)}, u32[]{:S(2)}, u32[]{:S(2)}) collective-permute-start(f32[32,256]{1,0:T(8,128)S(1)} %add.75), channel_id=1, source_target_pairs={{0,2},{1,3},{2,0},{3,1},{4,6},{5,7},{6,4},{7,5},{8,10},{9,11},{10,... | collective-permute-start | bytes 98312 | tf_op jit(solution)/shard_map/ppermute | solution.py:590
  65.2 2.6 %collective-permute-done.11 = f32[35,512]{1,0:T(8,128)S(1)} collective-permute-done((f32[35,512]{1,0:T(8,128)S(1)}, f32[35,512]{1,0:T(8,128)S(1)}, u32[]{:S(2)}, u32[]{:S(2)}) %collective-permute-start.11) | collective-permute-done | bytes 71712 | tf_op jit(solution)/shard_map/ppermute | solution.py:590
  67.8 2.6 %collective-permute-done.9 = f32[35,512]{1,0:T(8,128)S(1)} collective-permute-done((f32[35,512]{1,0:T(8,128)S(1)}, f32[35,512]{1,0:T(8,128)S(1)}, u32[]{:S(2)}, u32[]{:S(2)}) %collective-permute-start.9) | collective-permute-done | bytes 71712 | tf_op jit(solution)/shard_map/ppermute | solution.py:590
  70.5 1.7 %collective-permute-start.13 = (f32[35,2048]{1,0:T(8,128)S(1)}, f32[35,2048]{1,0:T(8,128)S(1)}, u32[]{:S(2)}, u32[]{:S(2)}) collective-permute-start(f32[35,2048]{1,0:T(8,128)S(1)} %pad_maximum_fusion.own_ref), channel_id=1, source_target_pairs={{0,8},{8,0},{16,24},{24,16},{32,40},{40,32},{48,56},{56,48},{64,72... | collective-permute-start | bytes 860168 | tf_op jit(solution)/shard_map/ppermute | solution.py:590
  72.2 0.6 add.76
  72.8 0.6 collective-permute-done.13.other_ref
  73.4 0.9 %join.1 = (f32[32,4096]{1,0:T(8,128)}, f32[3,4096]{1,0:T(4,128)}) custom-call(f32[35,2048]{1,0:T(8,128)S(1)} %pad_maximum_fusion.own_ref, f32[35,2048]{1,0:T(8,128)S(1)} %collective-permute-done.13.other_ref), custom_call_target="tpu_custom_call" | custom-call | tf_op jit(solution)/shard_map/join/pallas_call | solution.py:509
  (21 shorter events, 0.6 us)
Async XLA Ops:
  32.7 3.4 %collective-permute-start = (f32[40,2048]{1,0:T(8,128)S(1)}, f32[40,2048]{1,0:T(8,128)S(1)}, u32[]{:S(2)}, u32[]{:S(2)}) collective-permute-start(f32[40,2048]{1,0:T(8,128)S(1)} %get-tuple-element.41), channel_id=1, source_target_pairs={{0,8},{8,0},{16,24},{24,16},{32,40},{40,32},{48,56},{56,48},{64,72... | collective-permute-start | bytes 983048 | tf_op jit(solution)/shard_map/ppermute | solution.py:590
  36.2 6.4 %collective-permute-start.1 = (f32[40,512]{1,0:T(8,128)S(1)}, f32[40,512]{1,0:T(8,128)S(1)}, u32[]{:S(2)}, u32[]{:S(2)}) collective-permute-start(f32[40,512]{1,0:T(8,128)S(1)} %get-tuple-element.54), channel_id=1, source_target_pairs={{0,48},{8,56},{16,32},{24,40},{32,16},{40,24},{48,0},{56,8},{64,11... | collective-permute-start | bytes 245768 | tf_op jit(solution)/shard_map/ppermute | solution.py:590
  40.3 3.4 %collective-permute-start.2 = (f32[40,512]{1,0:T(8,128)S(1)}, f32[40,512]{1,0:T(8,128)S(1)}, u32[]{:S(2)}, u32[]{:S(2)}) collective-permute-start(f32[40,512]{1,0:T(8,128)S(1)} %get-tuple-element.56), channel_id=1, source_target_pairs={{0,32},{8,40},{16,48},{24,56},{32,0},{40,8},{48,16},{56,24},{64,96... | collective-permute-start | bytes 245768 | tf_op jit(solution)/shard_map/ppermute | solution.py:590
  40.3 4.8 %collective-permute-start.3 = (f32[40,512]{1,0:T(8,128)S(1)}, f32[40,512]{1,0:T(8,128)S(1)}, u32[]{:S(2)}, u32[]{:S(2)}) collective-permute-start(f32[40,512]{1,0:T(8,128)S(1)} %get-tuple-element.55), channel_id=1, source_target_pairs={{0,16},{8,24},{16,0},{24,8},{32,48},{40,56},{48,32},{56,40},{64,80... | collective-permute-start | bytes 245768 | tf_op jit(solution)/shard_map/ppermute | solution.py:590
  40.7 4.4 %collective-permute-start.4 = (f32[32,256]{1,0:T(8,128)S(1)}, f32[32,256]{1,0:T(8,128)S(1)}, u32[]{:S(2)}, u32[]{:S(2)}) collective-permute-start(f32[32,256]{1,0:T(8,128)S(1)} %get-tuple-element.39), channel_id=1, source_target_pairs={{0,4},{1,5},{2,6},{3,7},{4,0},{5,1},{6,2},{7,3},{8,12},{9,13},{10,... | collective-permute-start | bytes 98312 | tf_op jit(solution)/shard_map/ppermute | solution.py:590
  45.1 8.8 %collective-permute-start.5 = (f32[40,512]{1,0:T(8,128)S(1)}, f32[40,512]{1,0:T(8,128)S(1)}, u32[]{:S(2)}, u32[]{:S(2)}) collective-permute-start(f32[40,512]{1,0:T(8,128)S(1)} %add_add_fusion.1), channel_id=1, source_target_pairs={{0,128},{8,136},{16,144},{24,152},{32,160},{40,168},{48,176},{56,1... | collective-permute-start | bytes 245768 | tf_op jit(solution)/shard_map/ppermute | solution.py:590
  51.9 5.6 %collective-permute-start.6 = (f32[40,512]{1,0:T(8,128)S(1)}, f32[40,512]{1,0:T(8,128)S(1)}, u32[]{:S(2)}, u32[]{:S(2)}) collective-permute-start(f32[40,512]{1,0:T(8,128)S(1)} %add_add_fusion.1), channel_id=1, source_target_pairs={{0,192},{8,200},{16,208},{24,216},{32,224},{40,232},{48,240},{56,2... | collective-permute-start | bytes 245768 | tf_op jit(solution)/shard_map/ppermute | solution.py:590
  51.9 6.0 %collective-permute-start.7 = (f32[40,512]{1,0:T(8,128)S(1)}, f32[40,512]{1,0:T(8,128)S(1)}, u32[]{:S(2)}, u32[]{:S(2)}) collective-permute-start(f32[40,512]{1,0:T(8,128)S(1)} %add_add_fusion.1), channel_id=1, source_target_pairs={{0,64},{8,72},{16,80},{24,88},{32,96},{40,104},{48,112},{56,120},{... | collective-permute-start | bytes 245768 | tf_op jit(solution)/shard_map/ppermute | solution.py:590
  53.1 4.9 %collective-permute-start.8 = (f32[32,256]{1,0:T(8,128)S(1)}, f32[32,256]{1,0:T(8,128)S(1)}, u32[]{:S(2)}, u32[]{:S(2)}) collective-permute-start(f32[32,256]{1,0:T(8,128)S(1)} %add.67), channel_id=1, source_target_pairs={{0,1},{1,0},{2,3},{3,2},{4,5},{5,4},{6,7},{7,6},{8,9},{9,8},{10,11... | collective-permute-start | bytes 98312 | tf_op jit(solution)/shard_map/ppermute | solution.py:590
  58.0 7.2 %collective-permute-start.10 = (f32[35,512]{1,0:T(8,128)S(1)}, f32[35,512]{1,0:T(8,128)S(1)}, u32[]{:S(2)}, u32[]{:S(2)}) collective-permute-start(f32[35,512]{1,0:T(8,128)S(1)} %pad_maximum_fusion.1), channel_id=1, source_target_pairs={{0,32},{8,40},{16,48},{24,56},{32,0},{40,8},{48,16},{56,24},{64,96... | collective-permute-start | bytes 215048 | tf_op jit(solution)/shard_map/ppermute | solution.py:590
  60.0 7.8 %collective-permute-start.11 = (f32[35,512]{1,0:T(8,128)S(1)}, f32[35,512]{1,0:T(8,128)S(1)}, u32[]{:S(2)}, u32[]{:S(2)}) collective-permute-start(f32[35,512]{1,0:T(8,128)S(1)} %pad_maximum_fusion.1), channel_id=1, source_target_pairs={{0,48},{8,56},{16,32},{24,40},{32,16},{40,24},{48,0},{56,8},{64,11... | collective-permute-start | bytes 215048 | tf_op jit(solution)/shard_map/ppermute | solution.py:590
  64.3 6.1 %collective-permute-start.9 = (f32[35,512]{1,0:T(8,128)S(1)}, f32[35,512]{1,0:T(8,128)S(1)}, u32[]{:S(2)}, u32[]{:S(2)}) collective-permute-start(f32[35,512]{1,0:T(8,128)S(1)} %pad_maximum_fusion.1), channel_id=1, source_target_pairs={{0,16},{8,24},{16,0},{24,8},{32,48},{40,56},{48,32},{56,40},{64,80... | collective-permute-start | bytes 215048 | tf_op jit(solution)/shard_map/ppermute | solution.py:590
  64.3 6.2 %collective-permute-start.12 = (f32[32,256]{1,0:T(8,128)S(1)}, f32[32,256]{1,0:T(8,128)S(1)}, u32[]{:S(2)}, u32[]{:S(2)}) collective-permute-start(f32[32,256]{1,0:T(8,128)S(1)} %add.75), channel_id=1, source_target_pairs={{0,2},{1,3},{2,0},{3,1},{4,6},{5,7},{6,4},{7,5},{8,10},{9,11},{10,... | collective-permute-start | bytes 98312 | tf_op jit(solution)/shard_map/ppermute | solution.py:590
  70.5 2.9 %collective-permute-start.13 = (f32[35,2048]{1,0:T(8,128)S(1)}, f32[35,2048]{1,0:T(8,128)S(1)}, u32[]{:S(2)}, u32[]{:S(2)}) collective-permute-start(f32[35,2048]{1,0:T(8,128)S(1)} %pad_maximum_fusion.own_ref), channel_id=1, source_target_pairs={{0,8},{8,0},{16,24},{24,16},{32,40},{40,32},{48,56},{56,48},{64,72... | collective-permute-start | bytes 860168 | tf_op jit(solution)/shard_map/ppermute | solution.py:590
